TPU v7x, 128 devices: a whole 4x4x4 slice. The times are simulated.
128 devices in a mesh: rep: 4 (over y), ty: 4 (over z), tx: 8 (over x, core).
Axes of the slice: x: 4, y: 4, z: 4, core: 2. Of those that a mesh axis runs over, the one named last changes fastest.
Arguments:
- inputs: bfloat16 [4, 256, 384, 256], P('rep', None, 'ty', 'tx'), may hold values from -6 to 6
- targets: bfloat16 [4, 256, 384, 256], P('rep', None, 'ty', 'tx'), may hold values from -6 to 6
- kern_one: float32 [3, 3, 256], replicated, may hold values from -2 to 2
- point_one: float32 [256, 512], replicated, may hold values from -0.375 to 0.375
- coarsening_taps: float32 [2, 2, 512, 512], replicated, may hold values from -0.125 to 0.125
- kern_two: float32 [3, 3, 512], replicated, may hold values from -2 to 2
- point_two: float32 [512, 256], replicated, may hold values from -0.25 to 0.25
Outputs:
- expected_precip_map: bfloat16 [4, 256, 384, 256], P('rep', None, 'ty', 'tx')
- new_kern_one: float32 [3, 3, 256], replicated
- new_point_one: float32 [256, 512], replicated
- new_stride: float32 [2, 2, 512, 512], replicated
- new_kern_two: float32 [3, 3, 512], replicated
- new_point_two: float32 [512, 256], replicated
- step_kern_one: float32 [3, 3, 256], replicated
- step_point_one: float32 [256, 512], replicated
- step_stride: float32 [2, 2, 512, 512], replicated
- step_kern_two: float32 [3, 3, 512], replicated
- step_point_two: float32 [512, 256], replicated
All inputs are finite; a program needn't handle non-finite values.
Results may differ from a plain program's by a relative error of at most 0.008.
Values may be sent and summed in bfloat16 or wider, within the bound.
No kernel may reach another device: no remote copies, remote signals or barrier semaphores. Data moves between devices by JAX's collectives and lax.ppermute only.
A program may use at most 128 MiB of HBM per device.

v0:
```python
import jax
import jax.numpy as jnp
from jax import lax
from jax.experimental import pallas as pl
from jax.experimental.pallas import tpu as pltpu
from jax.sharding import PartitionSpec as P

EPS = 1e-05
RATE = 0.05
F32 = jnp.float32
BF16 = jnp.bfloat16
LANES = 128
HALO = 4
ROWS = 6
AXES = ("rep", "ty", "tx")


def mm(a, b):
    return jnp.dot(a, b, preferred_element_type=F32)


def mm_t(a, b):
    return lax.dot_general(a, b, (((1,), (1,)), ((), ())), preferred_element_type=F32)


def t_mm(a, b):
    return lax.dot_general(a, b, (((0,), (0,)), ((), ())), preferred_element_type=F32)


def sigmoid(v):
    return 0.5 + 0.5 * jnp.tanh(0.5 * v)


def tile_kernel(
    limits,
    x_ref,
    t_ref,
    top_ref,
    bot_ref,
    right_ref,
    left_ref,
    k1_ref,
    p1_ref,
    taps_ref,
    k2_ref,
    p2_ref,
    pred_ref,
    gk1_ref,
    gp1_ref,
    gst_ref,
    gk2_ref,
    gp2_ref,
    xf,
    tf,
    d2,
    out_e,
    out_own,
    pre_own,
    co,
    sl,
    cout,
    up,
    ot_own,
    ce_own,
    bc,
    bp,
):
    rows, cols, chan = x_ref.shape
    hid = k2_ref.shape[1]
    hr, hc = rows // 2, cols // 2
    slots = hc + 2 * HALO
    cb1, cb2 = chan // LANES, hid // LANES
    er = hr + 4
    fr = hr + 2

    def lanes(c):
        return slice(c * LANES, (c + 1) * LANES)

    def put(row, count, block, c):
        xf[c, pl.ds(row, count), 8 : 8 + cols, :] = block.astype(F32)

    for c in range(cb1):
        put(0, ROWS, top_ref[0:ROWS, :, lanes(c)], c)
        put(rows + ROWS, ROWS, bot_ref[0:ROWS, :, lanes(c)], c)

    step = 12

    @pl.loop(0, rows // step)
    def _(n):
        for c in range(cb1):
            put(ROWS + n * step, step, x_ref[pl.ds(n * step, step), :, lanes(c)], c)

    @pl.loop(0, (rows + 2 * ROWS) // step)
    def _(n):
        at = pl.ds(n * step, step)
        for c in range(cb1):
            right = right_ref[at, :, lanes(c)].astype(F32)
            left = left_ref[at, :, lanes(c)].astype(F32)
            xf[c, at, 8 + cols : 16 + cols, :] = right
            xf[c, at, 16 + cols : 24 + cols, :] = left
            xf[c, at, 7:8, :] = left[:, 7:8, :]
            xf[c, at, 24 + cols : 25 + cols, :] = xf[c, at, 8:9, :]

    def diff(first, count, block, c):
        e = 2 * first + ROWS
        at = pl.ds(e, 2 * count)
        tf[c, 0 : 2 * count, cols - 5 : cols + 3, :] = right_ref[at, :, lanes(c)].astype(F32)
        tf[c, 0 : 2 * count, cols + 13 : cols + 21, :] = left_ref[at, :, lanes(c)].astype(F32)
        tf[c, 0 : 2 * count, 0:cols, :] = block.astype(F32)
        both = xf[c, at, 8 : 24 + cols, :] - tf[c, 0 : 2 * count, 0 : 16 + cols, :]
        both = both.reshape(count, 2, 16 + cols, LANES)
        tf[c, 0:count, 0 : 16 + cols, :] = both[:, 0] + both[:, 1]
        even = tf[c, 0:count, pl.ds(0, slots, stride=2), :]
        odd = tf[c, 0:count, pl.ds(1, slots, stride=2), :]
        d2[c, pl.ds(first + 1, count), :, :] = (even + odd) * 0.25

    for c in range(cb1):
        diff(-1, 1, top_ref[ROWS : ROWS + 2, :, lanes(c)], c)
        diff(hr, 1, bot_ref[ROWS : ROWS + 2, :, lanes(c)], c)

    @pl.loop(0, hr // 4)
    def _(n):
        for c in range(cb1):
            diff(n * 4, 4, t_ref[pl.ds(n * 8, 8), :, lanes(c)], c)

    take = 4

    @pl.loop(0, er // take)
    def _(n):
        pres = []
        for c in range(cb1):
            k = k1_ref[:, lanes(c)]
            per = [[None] * take for _ in range(4)]
            for i in range(take):
                e = 2 * (n * take + i) + ROWS - 4
                for r in range(2):
                    total = [None, None]
                    for a in range(3):
                        at = e + r + a - 1
                        col = [xf[c, at, pl.ds(7 + o, slots, stride=2), :] for o in range(4)]
                        for q in range(2):
                            for b in range(3):
                                term = k[3 * a + b : 3 * a + b + 1, :] * col[q + b]
                                total[q] = term if total[q] is None else total[q] + term
                    for q in range(2):
                        per[2 * r + q][i] = total[q]
            pres.append([jnp.stack(p) for p in per])
        for ph in range(4):
            for c in range(cb1):
                own = pres[c][ph][:, 0:hc, :].reshape(take * hc, LANES).astype(BF16)
                pre_own[ph, pl.ds(n * (take * hc), take * hc), lanes(c)] = own
        low = [
            jnp.concatenate(
                [pres[c][ph].reshape(take * slots, LANES).astype(BF16) for c in range(cb1)], axis=1
            )
            for ph in range(4)
        ]
        for ph in range(4):
            act = mm(low[ph], p1_ref[...])
            out = act * sigmoid(act)
            out_e[ph, pl.ds(n * (take * slots), take * slots), :] = out.astype(BF16)
            own = out.reshape(take, slots, hid)[:, 0:hc, :].reshape(take * hc, hid)
            out_own[ph, pl.ds(n * (take * hc), take * hc), :] = own.astype(BF16)

    row_lo, row_hi, col_lo, col_hi = limits[0], limits[1], limits[2], limits[3]

    def inside(first, count):
        row = lax.broadcasted_iota(jnp.int32, (count, slots, LANES), 0) + first
        slot = lax.broadcasted_iota(jnp.int32, (count, slots, LANES), 1)
        col = jnp.where(slot < hc + HALO, slot, slot - slots)
        ok = (row >= row_lo) & (row < row_hi) & (col >= col_lo) & (col < col_hi)
        return jnp.where(ok, 1.0, 0.0).astype(F32)

    def wrapped(ref, c, at, value):
        ref[c, at, 8 : 8 + slots, :] = value
        ref[c, at, 7:8, :] = value[:, slots - 1 : slots, :]
        ref[c, at, 8 + slots : 9 + slots, :] = value[:, 0:1, :]

    half = er // 2

    @pl.loop(0, 2)
    def _(n):
        ok = inside(n * half - 2, half)
        for m in range(hid // 256):
            acc = None
            for ph in range(4):
                term = mm(
                    out_e[ph, pl.ds(n * (half * slots), half * slots), :],
                    taps_ref[ph, :, m * 256 : (m + 1) * 256],
                )
                acc = term if acc is None else acc + term
            acc = acc.astype(BF16).astype(F32).reshape(half, slots, 256)
            for j in range(2):
                wrapped(co, 2 * m + j, pl.ds(n * half, half), acc[:, :, lanes(j)] * ok)

    part = 10

    @pl.loop(0, fr // part)
    def _(n):
        pre = []
        for c in range(cb2):
            k = k2_ref[:, lanes(c)]
            total = None
            for a in range(3):
                for b in range(3):
                    at = pl.ds(n * part + a, part)
                    term = k[3 * a + b : 3 * a + b + 1, :] * co[c, at, 7 + b : 7 + b + slots, :]
                    total = term if total is None else total + term
            pre.append(total.reshape(part * slots, LANES))
        gate = [sigmoid(p) for p in pre]
        out = [p * g for p, g in zip(pre, gate)]
        low = jnp.concatenate([o.astype(BF16) for o in out], axis=1)
        for c in range(cb2):
            own = out[c].reshape(part, slots, LANES)[:, 0:hc, :].reshape(part * hc, LANES)
            ot_own[pl.ds(n * (part * hc), part * hc), lanes(c)] = own.astype(BF16)
        back = mm(low, p2_ref[...]).reshape(part, slots, chan)
        errs = []
        for c in range(cb1):
            own = back[:, :, lanes(c)]
            cout[c, pl.ds(n * part, part), :, :] = own[:, 0:hc, :]
            err = own + d2[c, pl.ds(n * part, part), :, :]
            errs.append(err.reshape(part * slots, LANES).astype(BF16))
            ce_own[pl.ds(n * (part * hc), part * hc), lanes(c)] = (
                err[:, 0:hc, :].reshape(part * hc, LANES).astype(BF16)
            )
        err = jnp.concatenate(errs, axis=1)
        ok = inside(n * part - 1, part)
        back_two = mm_t(err, p2_ref[...])
        for c in range(cb2):
            slope = back_two[:, lanes(c)] * (gate[c] * (1.0 + pre[c] * (1.0 - gate[c])))
            slope = slope.astype(BF16).astype(F32).reshape(part, slots, LANES) * ok
            wrapped(sl, c, pl.ds(n * part, part), slope)

    gp2_ref[...] = t_mm(ot_own[hc : hc + hr * hc, :], ce_own[hc : hc + hr * hc, :])

    @pl.loop(0, hr // 4)
    def _(n):
        for c in range(cb1):
            block = cout[c, pl.ds(n * 4 + 1, 4), :, :]
            up[c, :, pl.ds(0, hc, stride=2), :] = block
            up[c, :, pl.ds(1, hc, stride=2), :] = block
            wide = up[c, :, :, :]
            wide = jnp.stack([wide, wide], axis=1).reshape(8, cols, LANES)
            fine = xf[c, pl.ds(n * 8 + ROWS, 8), 8 : 8 + cols, :]
            pred_ref[pl.ds(n * 8, 8), :, lanes(c)] = (wide + fine).astype(BF16)

    for c in range(cb2):
        k = k2_ref[:, lanes(c)]

        def body(n, acc, c=c, k=k):
            acc = list(acc)
            for i in range(2):
                row = n * 2 + i
                slope = sl[c, row + 1, 8 : 8 + hc, :]
                total = None
                for a in range(3):
                    for b in range(3):
                        p = slope * co[c, row + 1 + a, 7 + b : 7 + b + hc, :]
                        acc[3 * a + b] = acc[3 * a + b] + (p[0:8] + p[8:16])
                        term = k[3 * a + b : 3 * a + b + 1, :] * sl[c, row + 2 - a, 9 - b : 9 - b + hc, :]
                        total = term if total is None else total + term
                bc[pl.ds(row * hc, hc), lanes(c)] = total.astype(BF16)
            return tuple(acc)

        acc = lax.fori_loop(0, hr // 2, body, tuple(jnp.zeros((8, LANES), F32) for _ in range(9)))
        for j in range(9):
            gk2_ref[j : j + 1, lanes(c)] = jnp.sum(acc[j], axis=0, keepdims=True)

    skip = 2 * hc
    own_rows = slice(skip, skip + hr * hc)
    for ph in range(4):
        gst_ref[ph] = t_mm(out_own[ph, own_rows, :], bc[...]).astype(gst_ref.dtype)
        back = mm_t(bc[...], taps_ref[ph])
        act = mm(pre_own[ph, own_rows, :], p1_ref[...])
        gate = sigmoid(act)
        slope = (back * (gate * (1.0 + act * (1.0 - gate)))).astype(BF16)
        gp1 = t_mm(pre_own[ph, own_rows, :], slope)
        if ph == 0:
            gp1_ref[...] = gp1
        else:
            gp1_ref[...] += gp1
        back_pre = mm_t(slope, p1_ref[...])
        for c in range(cb1):
            bp[ph, c] = back_pre[:, lanes(c)].reshape(hr, hc, LANES)

    for c in range(cb1):

        def body(n, acc, c=c):
            acc = list(acc)
            grads = [bp[ph, c, n] for ph in range(4)]
            for s in range(4):
                e = 2 * n + ROWS + s - 1
                col = [xf[c, e, pl.ds(7 + o, hc, stride=2), :] for o in range(4)]
                for r in range(2):
                    a = s - r
                    if 0 <= a < 3:
                        for q in range(2):
                            for b in range(3):
                                p = grads[2 * r + q] * col[q + b]
                                acc[3 * a + b] = acc[3 * a + b] + (p[0:8] + p[8:16])
            return tuple(acc)

        acc = lax.fori_loop(0, hr, body, tuple(jnp.zeros((8, LANES), F32) for _ in range(9)))
        for j in range(9):
            gk1_ref[j : j + 1, lanes(c)] = jnp.sum(acc[j], axis=0, keepdims=True)


def tile_step(limits, x, t, top, bot, right, left, k1, p1, taps, k2, p2):
    rows, cols, chan = x.shape
    hid = k2.shape[1]
    hr, hc = rows // 2, cols // 2
    slots = hc + 2 * HALO
    cb1, cb2 = chan // LANES, hid // LANES
    vm = pl.BlockSpec(memory_space=pltpu.VMEM)
    return pl.pallas_call(
        tile_kernel,
        out_shape=(
            jax.ShapeDtypeStruct(x.shape, BF16),
            jax.ShapeDtypeStruct(k1.shape, F32),
            jax.ShapeDtypeStruct(p1.shape, F32),
            jax.ShapeDtypeStruct(taps.shape, F32),
            jax.ShapeDtypeStruct(k2.shape, F32),
            jax.ShapeDtypeStruct(p2.shape, F32),
        ),
        in_specs=[pl.BlockSpec(memory_space=pltpu.SMEM)] + [vm] * 11,
        out_specs=[vm] * 6,
        scratch_shapes=[
            pltpu.VMEM((cb1, rows + 2 * ROWS, cols + 32, LANES), F32),
            pltpu.VMEM((cb1, 8, cols + 32, LANES), F32),
            pltpu.VMEM((cb1, hr + 2, slots, LANES), F32),
            pltpu.VMEM((4, (hr + 4) * slots, hid), BF16),
            pltpu.VMEM((4, (hr + 4) * hc, hid), BF16),
            pltpu.VMEM((4, (hr + 4) * hc, chan), BF16),
            pltpu.VMEM((cb2, hr + 4, slots + 16, LANES), F32),
            pltpu.VMEM((cb2, hr + 2, slots + 16, LANES), F32),
            pltpu.VMEM((cb1, hr + 2, hc, LANES), F32),
            pltpu.VMEM((cb1, 4, cols, LANES), F32),
            pltpu.VMEM(((hr + 2) * hc, hid), BF16),
            pltpu.VMEM(((hr + 2) * hc, chan), BF16),
            pltpu.VMEM((hr * hc, hid), BF16),
            pltpu.VMEM((4, cb1, hr, hc, LANES), F32),
        ],
        compiler_params=pltpu.CompilerParams(vmem_limit_bytes=63 * 1024 * 1024),
    )(limits, x, t, top, bot, right, left, k1, p1, taps, k2, p2)


def shift(block, axis, step):
    count = lax.axis_size(axis)
    return lax.ppermute(
        block, axis, [(i, i + step) for i in range(count) if 0 <= i + step < count]
    )


def adjusted(weight, grad):
    normed = grad / jnp.sqrt(jnp.mean(grad * grad) + EPS)
    return weight - RATE * jnp.sqrt(jnp.mean(weight * weight) + EPS) * normed, normed


def per_device(inputs, targets, kern_one, point_one, coarsening_taps, kern_two, point_two):
    x = jnp.transpose(inputs[0], (1, 2, 0))
    t = jnp.transpose(targets[0], (1, 2, 0))
    rows, cols, chan = x.shape
    hid = point_one.shape[1]
    hr, hc = rows // 2, cols // 2
    top = shift(jnp.concatenate([x[rows - ROWS :], t[rows - 2 :]], axis=0), "ty", 1)
    bot = shift(jnp.concatenate([x[:ROWS], t[:2]], axis=0), "ty", -1)

    def edge(cut):
        e = jnp.concatenate([top[:ROWS, cut], x[:, cut], bot[:ROWS, cut]], axis=0)
        z = jnp.zeros((ROWS - 2,) + e.shape[1:], BF16)
        f = jnp.concatenate([z, top[ROWS:, cut], t[:, cut], bot[ROWS:, cut], z], axis=0)
        return e, f

    e, f = edge(slice(0, 8))
    right = shift(jnp.concatenate([e[:, :5], f[:, :2], e[:, 7:]], axis=1), "tx", -1)
    e, f = edge(slice(cols - 8, cols))
    left = shift(jnp.concatenate([e[:, :1], f[:, 6:], e[:, 3:]], axis=1), "tx", 1)
    ty, tx = lax.axis_index("ty"), lax.axis_index("tx")
    big = 1 << 20
    limits = jnp.stack(
        [
            jnp.where(ty == 0, 0, -big),
            jnp.where(ty == lax.axis_size("ty") - 1, hr, big),
            jnp.where(tx == 0, 0, -big),
            jnp.where(tx == lax.axis_size("tx") - 1, hc, big),
        ]
    ).astype(jnp.int32)
    pred, gk1, gp1, gst, gk2, gp2 = tile_step(
        limits,
        x,
        t,
        top,
        bot,
        right,
        left,
        kern_one.reshape(9, chan),
        point_one.astype(BF16),
        coarsening_taps.astype(BF16).reshape(4, hid, hid),
        kern_two.reshape(9, hid),
        point_two.astype(BF16),
    )
    weights = (kern_one, point_one, coarsening_taps, kern_two, point_two)
    grads = lax.psum((gk1, gp1, gst, gk2, gp2), AXES)
    pairs = [adjusted(w, g.reshape(w.shape)) for w, g in zip(weights, grads)]
    return (
        jnp.transpose(pred, (2, 0, 1))[None],
        *[p[0] for p in pairs],
        *[p[1] for p in pairs],
    )


def solution(mesh):
    tile = P("rep", None, "ty", "tx")
    return jax.shard_map(
        per_device,
        mesh=mesh,
        in_specs=(tile, tile, P(), P(), P(), P(), P()),
        out_specs=(tile,) + (P(),) * 10,
        check_vma=False,
    )
```

profile of v0, /device:TPU:1, one launch (start us, length us, event | category | flops | bytes accessed | tf_op | source)
XLA Modules:
  0.0 255.3 jit_solution(14271837442584811608)
XLA Ops:
  7.3 0.9 fusion.20
  8.1 1.0 fusion.19
  9.1 4.4 %collective-permute-start = (bf16[8,32,256]{2,1,0:T(8,128)(2,1)S(1)}, bf16[8,32,256]{2,1,0:T(8,128)(2,1)S(1)}, u32[]{:S(2)}, u32[]{:S(2)}) collective-permute-start(bf16[8,32,256]{2,1,0:T(8,128)(2,1)S(1)} %pad_maximum_fusion.2), channel_id=1, source_target_pairs={{0,8},{8,16},{16,24},{1,9},{9,17},{17,25},{2,10},{10,18},{18,26},{... | collective-permute-start | bytes 393224 | tf_op jit(solution)/shard_map/ppermute | solution.py:349
  13.5 1.3 collective-permute-start.1
  14.8 1.2 fusion.18
  16.0 2.6 %multiply_reduce_fusion.5 = (f32[]{:T(128)}, bf16[256,512]{1,0:T(8,128)(2,1)}) fusion(f32[256,512]{1,0:T(8,128)} %param.10), kind=kLoop, calls=%fused_computation.23 | loop fusion | flops 393215 | bytes 786436 | tf_op jit(solution)/shard_map/reduce_sum | solution.py:356
  18.6 2.8 %multiply_reduce_fusion.3 = (f32[]{:T(128)}, bf16[512,256]{1,0:T(8,128)(2,1)}) fusion(f32[512,256]{1,0:T(8,128)} %param.13), kind=kLoop, calls=%fused_computation.20 | loop fusion | flops 393215 | bytes 786436 | tf_op jit(solution)/shard_map/reduce_sum | solution.py:356
  21.3 0.6 reshape.40.k1_ref
  21.9 0.6 reshape.42.k2_ref
  23.6 3.0 %collective-permute-start.2 = (bf16[108,8,256]{2,1,0:T(8,128)(2,1)S(1)}, bf16[108,8,256]{2,1,0:T(8,128)(2,1)S(1)}, u32[]{:S(2)}, u32[]{:S(2)}) collective-permute-start(bf16[108,8,256]{2,1,0:T(8,128)(2,1)S(1)} %fusion.11), channel_id=1, source_target_pairs={{1,0},{2,1},{3,2},{4,3},{5,4},{6,5},{7,6},{9,8},{10,9},{11,10},{12... | collective-permute-start | bytes 1327112 | tf_op jit(solution)/shard_map/ppermute | solution.py:349
  26.9 3.0 %collective-permute-start.3 = (bf16[108,8,256]{2,1,0:T(8,128)(2,1)S(1)}, bf16[108,8,256]{2,1,0:T(8,128)(2,1)S(1)}, u32[]{:S(2)}, u32[]{:S(2)}) collective-permute-start(bf16[108,8,256]{2,1,0:T(8,128)(2,1)S(1)} %fusion.15), channel_id=1, source_target_pairs={{0,1},{1,2},{2,3},{3,4},{4,5},{5,6},{6,7},{8,9},{9,10},{10,11},{11... | collective-permute-start | bytes 1327112 | tf_op jit(solution)/shard_map/ppermute | solution.py:349
  30.0 0.7 pad_add_fusion.limits
  30.6 2.9 %multiply_reduce_fusion.1 = (f32[]{:T(128)}, bf16[2,2,512,512]{3,2,1,0:T(8,128)(2,1)}) fusion(f32[2,2,512,512]{3,2,1,0:T(8,128)S(1)} %copy-done), kind=kLoop, calls=%fused_computation.2 | loop fusion | flops 3145727 | bytes 6291460 | tf_op jit(solution)/shard_map/reduce_sum | solution.py:356
  33.7 1.5 collective-permute-done.3.left_ref
  35.2 0.8 copy-done.9
  35.9 32.4 %shard_map.158 = (bf16[96,32,256]{2,1,0:T(8,128)(2,1)}, f32[9,256]{1,0:T(8,128)}, f32[256,512]{1,0:T(8,128)}, f32[4,512,512]{2,1,0:T(8,128)}, f32[9,512]{1,0:T(8,128)}, /*index=5*/f32[512,256]{1,0:T(8,128)}) custom-call(s32[4]{0:T(128)} %pad_add_fusion.limits, bf16[96,32,256]{2,1,0:T(8,128)(2,1)} %bitcast.21, bf16[96,32,256]{2,1,0:T(8,128)(2,1)} %bitcast.23, ...), custom_call_target="tpu_custom_call" | custom-call | tf_op jit(solution)/shard_map/pallas_call | solution.py:315
  68.4 0.6 multiply_reduce_fusion.7
  69.7 0.6 multiply_reduce_fusion.9
  73.0 69.2 %all-reduce = (f32[9,256]{1,0:T(8,128)S(1)}, f32[9,512]{1,0:T(8,128)S(1)}) all-reduce(f32[9,256]{1,0:T(8,128)S(1)} %copy-done.17, f32[9,512]{1,0:T(8,128)S(1)} %copy-done.16), channel_id=1, replica_groups=mesh['rep'=4,'ty'=4,'tx'=8] {'rep','ty','tx'}, use_global_device_ids=true, to_apply=%region_1.2 | all-reduce | flops 6912 | bytes 55296 | tf_op jit(solution)/shard_map/psum | solution.py:403
  142.2 0.6 multiply_reduce_fusion.6
  143.6 0.6 multiply_reduce_fusion.8
  144.9 0.6 multiply_subtract_fusion.4
  145.5 0.6 multiply_subtract_fusion.3
  146.2 83.4 %all-reduce.4.cloned.1.call-done = (f32[256,512]{1,0:T(8,128)}, f32[4,512,512]{2,1,0:T(8,128)}, f32[512,256]{1,0:T(8,128)}) async-done(((f32[256,512]{1,0:T(8,128)}, f32[4,512,512]{2,1,0:T(8,128)}, f32[512,256]{1,0:T(8,128)}), (f32[256,512]{1,0:T(8,128)}, f32[4,512,512]{2,1,0:T(8,128)}, f32[512,256]{1,0:T(8,128)})) %all-reduce.4.cloned.1.call-update) | async-done | bytes 5242896 | tf_op jit(solution)/shard_map/psum | solution.py:403
  229.5 1.8 multiply_reduce_fusion.2
  232.1 3.9 %multiply_reduce_fusion = f32[]{:T(128)} fusion(f32[4,512,512]{2,1,0:T(8,128)} %get-tuple-element.26), kind=kLoop, calls=%fused_computation.1 | loop fusion | flops 2097151 | bytes 4194308 | tf_op jit(solution)/shard_map/reduce_sum | solution.py:355
  236.7 0.7 multiply_reduce_fusion.4
  238.1 2.8 %broadcast_divide_fusion = f32[4,512,512]{2,1,0:T(8,128)S(1)} fusion(f32[4,512,512]{2,1,0:T(8,128)} %get-tuple-element.26, f32[]{:T(128)S(6)} %sqrt.35), kind=kLoop, calls=%fused_computation.3 | loop fusion | flops 1048576 | bytes 8388612 | tf_op jit(solution)/shard_map/div | solution.py:355
  241.0 1.1 multiply_subtract_fusion.2
  242.1 1.0 multiply_subtract_fusion.1
  243.1 2.3 copy-done.1
  245.4 3.0 %multiply_subtract_fusion = f32[2,2,512,512]{3,2,1,0:T(8,128)} fusion(f32[2,2,512,512]{3,2,1,0:T(8,128)S(1)} %copy-done.1, f32[2,2,512,512]{3,2,1,0:T(8,128)S(1)} %bitcast.16, f32[]{:T(128)S(6)} %mul.89), kind=kLoop, calls=%fused_computation | loop fusion | flops 2097152 | bytes 12582916 | tf_op jit(solution)/shard_map/sub | solution.py:356
  (58 shorter events, 1.6 us)
Async XLA Ops:
  7.2 15.4 %copy-start.3 = (bf16[1,256,96,32]{1,3,2,0:T(8,128)(2,1)S(1)}, bf16[1,256,96,32]{1,3,2,0:T(8,128)(2,1)}, u32[]{:S(2)}) copy-start(bf16[1,256,96,32]{1,3,2,0:T(8,128)(2,1)} %param.8) | copy-start | bytes 4718596
  7.2 14.1 %copy-start.13 = (f32[3,3,256]{2,1,0:T(4,128)S(1)}, f32[3,3,256]{2,1,0:T(4,128)}, u32[]{:S(2)}) copy-start(f32[3,3,256]{2,1,0:T(4,128)} %param.9) | copy-start | bytes 27652
  7.2 14.7 %copy-start.12 = (f32[3,3,512]{2,1,0:T(4,128)S(1)}, f32[3,3,512]{2,1,0:T(4,128)}, u32[]{:S(2)}) copy-start(f32[3,3,512]{2,1,0:T(4,128)} %param.12) | copy-start | bytes 55300
  7.2 222.3 %all-reduce.4.cloned.1.call-start = ((), (), s32[]{:S(2)}) async-start(), calls=%async_computation | async-start | bytes 10485760 | tf_op jit(solution)/shard_map/psum | solution.py:403
  9.1 13.5 %collective-permute-start = (bf16[8,32,256]{2,1,0:T(8,128)(2,1)S(1)}, bf16[8,32,256]{2,1,0:T(8,128)(2,1)S(1)}, u32[]{:S(2)}, u32[]{:S(2)}) collective-permute-start(bf16[8,32,256]{2,1,0:T(8,128)(2,1)S(1)} %pad_maximum_fusion.2), channel_id=1, source_target_pairs={{0,8},{8,16},{16,24},{1,9},{9,17},{17,25},{2,10},{10,18},{18,26},{... | collective-permute-start | bytes 393224 | tf_op jit(solution)/shard_map/ppermute | solution.py:349
  13.5 9.1 %collective-permute-start.1 = (bf16[8,32,256]{2,1,0:T(8,128)(2,1)S(1)}, bf16[8,32,256]{2,1,0:T(8,128)(2,1)S(1)}, u32[]{:S(2)}, u32[]{:S(2)}) collective-permute-start(bf16[8,32,256]{2,1,0:T(8,128)(2,1)S(1)} %pad_maximum_fusion.3), channel_id=1, source_target_pairs={{8,0},{16,8},{24,16},{9,1},{17,9},{25,17},{10,2},{18,10},{26,18},{... | collective-permute-start | bytes 393224 | tf_op jit(solution)/shard_map/ppermute | solution.py:349
  22.6 8.1 %copy-start = (f32[2,2,512,512]{3,2,1,0:T(8,128)S(1)}, f32[2,2,512,512]{3,2,1,0:T(8,128)}, u32[]{:S(2)}) copy-start(f32[2,2,512,512]{3,2,1,0:T(8,128)} %param.11) | copy-start | bytes 12582916
  22.6 11.0 %copy-start.10 = (bf16[8,32,256]{2,1,0:T(8,128)(2,1)}, bf16[8,32,256]{2,1,0:T(8,128)(2,1)S(1)}, u32[]{:S(2)}) copy-start(bf16[8,32,256]{2,1,0:T(8,128)(2,1)S(1)} %collective-permute-done.top_ref) | copy-start | bytes 393220
  22.7 0.7 copy-start.11
  23.6 10.1 %collective-permute-start.2 = (bf16[108,8,256]{2,1,0:T(8,128)(2,1)S(1)}, bf16[108,8,256]{2,1,0:T(8,128)(2,1)S(1)}, u32[]{:S(2)}, u32[]{:S(2)}) collective-permute-start(bf16[108,8,256]{2,1,0:T(8,128)(2,1)S(1)} %fusion.11), channel_id=1, source_target_pairs={{1,0},{2,1},{3,2},{4,3},{5,4},{6,5},{7,6},{9,8},{10,9},{11,10},{12... | collective-permute-start | bytes 1327112 | tf_op jit(solution)/shard_map/ppermute | solution.py:349
  26.9 8.3 %collective-permute-start.3 = (bf16[108,8,256]{2,1,0:T(8,128)(2,1)S(1)}, bf16[108,8,256]{2,1,0:T(8,128)(2,1)S(1)}, u32[]{:S(2)}, u32[]{:S(2)}) collective-permute-start(bf16[108,8,256]{2,1,0:T(8,128)(2,1)S(1)} %fusion.15), channel_id=1, source_target_pairs={{0,1},{1,2},{2,3},{3,4},{4,5},{5,6},{6,7},{8,9},{9,10},{10,11},{11... | collective-permute-start | bytes 1327112 | tf_op jit(solution)/shard_map/ppermute | solution.py:349
  33.7 1.5 copy-start.8
  35.2 0.8 copy-start.9
  68.3 4.7 %copy-start.16 = (f32[9,512]{1,0:T(8,128)S(1)}, f32[9,512]{1,0:T(8,128)}, u32[]{:S(2)}) copy-start(f32[9,512]{1,0:T(8,128)} %get-tuple-element.21) | copy-start | bytes 55300
  68.4 4.7 %copy-start.17 = (f32[9,256]{1,0:T(8,128)S(1)}, f32[9,256]{1,0:T(8,128)}, u32[]{:S(2)}) copy-start(f32[9,256]{1,0:T(8,128)} %get-tuple-element.18) | copy-start | bytes 27652
  144.9 96.0 %copy-start.15 = (f32[3,3,256]{2,1,0:T(4,128)}, f32[3,3,256]{2,1,0:T(4,128)S(1)}, u32[]{:S(2)}) copy-start(f32[3,3,256]{2,1,0:T(4,128)S(1)} %div.73) | copy-start | bytes 27652
  144.9 96.0 %copy-start.14 = (f32[3,3,512]{2,1,0:T(4,128)}, f32[3,3,512]{2,1,0:T(4,128)S(1)}, u32[]{:S(2)}) copy-start(f32[3,3,512]{2,1,0:T(4,128)S(1)} %div.87) | copy-start | bytes 55300
  229.5 7.1 %copy-start.7 = (f32[256,512]{1,0:T(8,128)S(1)}, f32[256,512]{1,0:T(8,128)}, u32[]{:S(2)}) copy-start(f32[256,512]{1,0:T(8,128)} %get-tuple-element.25) | copy-start | bytes 1572868
  238.1 2.9 %copy-start.4 = (f32[256,512]{1,0:T(8,128)S(1)}, f32[256,512]{1,0:T(8,128)}, u32[]{:S(2)}) copy-start(f32[256,512]{1,0:T(8,128)} %param.10) | copy-start | bytes 1572868
  238.1 4.0 %copy-start.5 = (f32[512,256]{1,0:T(8,128)S(1)}, f32[512,256]{1,0:T(8,128)}, u32[]{:S(2)}) copy-start(f32[512,256]{1,0:T(8,128)} %param.13) | copy-start | bytes 1572868
  238.1 4.0 %copy-start.6 = (f32[512,256]{1,0:T(8,128)S(1)}, f32[512,256]{1,0:T(8,128)}, u32[]{:S(2)}) copy-start(f32[512,256]{1,0:T(8,128)} %get-tuple-element.27) | copy-start | bytes 1572868
  241.0 7.5 %copy-start.2 = (f32[4,512,512]{2,1,0:T(8,128)}, f32[4,512,512]{2,1,0:T(8,128)S(1)}, u32[]{:S(2)}) copy-start(f32[4,512,512]{2,1,0:T(8,128)S(1)} %broadcast_divide_fusion) | copy-start | bytes 12582916
  241.0 4.4 %copy-start.1 = (f32[2,2,512,512]{3,2,1,0:T(8,128)S(1)}, f32[2,2,512,512]{3,2,1,0:T(8,128)}, u32[]{:S(2)}) copy-start(f32[2,2,512,512]{3,2,1,0:T(8,128)} %param.11) | copy-start | bytes 12582916
Sparse Core Ops, SparseCore 0:
  68.5 160.9 all-reduce.3
where the time goes:
time: 256 us; the launch traced here: 255 us
  waiting for transfers between devices  85 us (33%)
  blocking collectives  69.2 us (27%)
  Pallas kernels  32.4 us (13%)
  other arithmetic  27.6 us (11%)
  between operations  21.3 us (8%)
  starting transfers between devices  11.7 us (5%)
  local copies, waits for them, and re-layouts  7.97 us (3%)
    psum x1, waiting for transfers between devices, per_device(): grads = lax.psum((gk1, gp1, gst, gk2, gp2), AXES)  83.4 us
    psum x1, blocking collectives, per_device(): grads = lax.psum((gk1, gp1, gst, gk2, gp2), AXES)  69.2 us
    pallas_call x1, Pallas kernels, tile_step(): pl.pallas_call(tile_kernel, out_shape=(jax.ShapeDtypeStruct(x.shape, BF16...  32.4 us
    ppermute x4, starting transfers between devices, shift(): lax.ppermute(block, axis, [(i, i + step) for i in range(count) if 0 <= i...  11.7 us
    reduce_sum x5, other arithmetic, adjusted(): jnp.mean(weight * weight) + EPS  9.47 us
    reduce_sum x5, other arithmetic, adjusted(): normed = grad / jnp.sqrt(jnp.mean(grad * grad) + EPS)  7.65 us
    sub x5, other arithmetic, adjusted(): weight - RATE * jnp.sqrt(jnp.mean(weight * weight) + EPS) * normed  6.37 us
  transfers between devices with their start and end apart: 5, of which 3 were waited for; matrix products, arithmetic and copies ran while one was open for 6% of the time, Pallas kernels for 0%

commit v1 on v0

--- a/solution.py
+++ b/solution.py
@@ -12,7 +12,7 @@
 LANES = 128
 HALO = 4
 ROWS = 6
-AXES = ("rep", "ty", "tx")
+SMALL = 64
 
 
 def mm(a, b):
@@ -45,11 +45,8 @@
     k2_ref,
     p2_ref,
     pred_ref,
-    gk1_ref,
-    gp1_ref,
-    gst_ref,
-    gk2_ref,
-    gp2_ref,
+    keep_ref,
+    send_ref,
     xf,
     tf,
     d2,
@@ -64,9 +61,10 @@
     ce_own,
     bc,
     bp,
+    small,
 ):
     rows, cols, chan = x_ref.shape
-    hid = k2_ref.shape[1]
+    hid = k2_ref.shape[2]
     hr, hc = rows // 2, cols // 2
     slots = hc + 2 * HALO
     cb1, cb2 = chan // LANES, hid // LANES
@@ -75,6 +73,25 @@
 
     def lanes(c):
         return slice(c * LANES, (c + 1) * LANES)
+
+    core = limits[4]
+    st_rows, p1_rows, p2_rows = hid * (hid // LANES), chan * (hid // LANES), hid * (chan // LANES)
+    p1_at = 2 * st_rows
+    p2_at = p1_at + p1_rows // 2
+    small_at = p2_at + p2_rows // 2
+
+    def emit(half, at, value):
+        value = value.astype(BF16)
+
+        @pl.when(core == half)
+        def _():
+            keep_ref[at : at + value.shape[0], :] = value
+
+        @pl.when(core != half)
+        def _():
+            send_ref[at : at + value.shape[0], :] = value
+
+    small[...] = jnp.zeros_like(small)
 
     def put(row, count, block, c):
         xf[c, pl.ds(row, count), 8 : 8 + cols, :] = block.astype(F32)
@@ -129,7 +146,6 @@
     def _(n):
         pres = []
         for c in range(cb1):
-            k = k1_ref[:, lanes(c)]
             per = [[None] * take for _ in range(4)]
             for i in range(take):
                 e = 2 * (n * take + i) + ROWS - 4
@@ -140,7 +156,7 @@
                         col = [xf[c, at, pl.ds(7 + o, slots, stride=2), :] for o in range(4)]
                         for q in range(2):
                             for b in range(3):
-                                term = k[3 * a + b : 3 * a + b + 1, :] * col[q + b]
+                                term = k1_ref[a, b : b + 1, lanes(c)] * col[q + b]
                                 total[q] = term if total[q] is None else total[q] + term
                     for q in range(2):
                         per[2 * r + q][i] = total[q]
@@ -199,12 +215,11 @@
     def _(n):
         pre = []
         for c in range(cb2):
-            k = k2_ref[:, lanes(c)]
             total = None
             for a in range(3):
                 for b in range(3):
                     at = pl.ds(n * part + a, part)
-                    term = k[3 * a + b : 3 * a + b + 1, :] * co[c, at, 7 + b : 7 + b + slots, :]
+                    term = k2_ref[a, b : b + 1, lanes(c)] * co[c, at, 7 + b : 7 + b + slots, :]
                     total = term if total is None else total + term
             pre.append(total.reshape(part * slots, LANES))
         gate = [sigmoid(p) for p in pre]
@@ -231,7 +246,9 @@
             slope = slope.astype(BF16).astype(F32).reshape(part, slots, LANES) * ok
             wrapped(sl, c, pl.ds(n * part, part), slope)
 
-    gp2_ref[...] = t_mm(ot_own[hc : hc + hr * hc, :], ce_own[hc : hc + hr * hc, :])
+    gp2 = t_mm(ot_own[hc : hc + hr * hc, :], ce_own[hc : hc + hr * hc, :])
+    for c in range(cb1):
+        emit(2 * c // cb1, p2_at + (c % (cb1 // 2)) * hid, gp2[:, lanes(c)])
 
     @pl.loop(0, hr // 4)
     def _(n):
@@ -245,9 +262,7 @@
             pred_ref[pl.ds(n * 8, 8), :, lanes(c)] = (wide + fine).astype(BF16)
 
     for c in range(cb2):
-        k = k2_ref[:, lanes(c)]
-
-        def body(n, acc, c=c, k=k):
+        def body(n, acc, c=c):
             acc = list(acc)
             for i in range(2):
                 row = n * 2 + i
@@ -257,31 +272,34 @@
                     for b in range(3):
                         p = slope * co[c, row + 1 + a, 7 + b : 7 + b + hc, :]
                         acc[3 * a + b] = acc[3 * a + b] + (p[0:8] + p[8:16])
-                        term = k[3 * a + b : 3 * a + b + 1, :] * sl[c, row + 2 - a, 9 - b : 9 - b + hc, :]
+                        term = k2_ref[a, b : b + 1, lanes(c)] * sl[c, row + 2 - a, 9 - b : 9 - b + hc, :]
                         total = term if total is None else total + term
                 bc[pl.ds(row * hc, hc), lanes(c)] = total.astype(BF16)
             return tuple(acc)
 
         acc = lax.fori_loop(0, hr // 2, body, tuple(jnp.zeros((8, LANES), F32) for _ in range(9)))
         for j in range(9):
-            gk2_ref[j : j + 1, lanes(c)] = jnp.sum(acc[j], axis=0, keepdims=True)
+            at = 9 * (cb1 + c) + j
+            small[at : at + 1, :] = jnp.sum(acc[j], axis=0, keepdims=True)
 
     skip = 2 * hc
     own_rows = slice(skip, skip + hr * hc)
     for ph in range(4):
-        gst_ref[ph] = t_mm(out_own[ph, own_rows, :], bc[...]).astype(gst_ref.dtype)
+        gst = t_mm(out_own[ph, own_rows, :], bc[...])
+        for c in range(cb2):
+            emit(ph // 2, (ph % 2) * st_rows + c * hid, gst[:, lanes(c)])
         back = mm_t(bc[...], taps_ref[ph])
         act = mm(pre_own[ph, own_rows, :], p1_ref[...])
         gate = sigmoid(act)
         slope = (back * (gate * (1.0 + act * (1.0 - gate)))).astype(BF16)
-        gp1 = t_mm(pre_own[ph, own_rows, :], slope)
-        if ph == 0:
-            gp1_ref[...] = gp1
-        else:
-            gp1_ref[...] += gp1
+        term = t_mm(pre_own[ph, own_rows, :], slope)
+        gp1 = term if ph == 0 else gp1 + term
         back_pre = mm_t(slope, p1_ref[...])
         for c in range(cb1):
             bp[ph, c] = back_pre[:, lanes(c)].reshape(hr, hc, LANES)
+
+    for c in range(cb2):
+        emit(2 * c // cb2, p1_at + (c % (cb2 // 2)) * chan, gp1[:, lanes(c)])
 
     for c in range(cb1):
 
@@ -302,28 +320,38 @@
 
         acc = lax.fori_loop(0, hr, body, tuple(jnp.zeros((8, LANES), F32) for _ in range(9)))
         for j in range(9):
-            gk1_ref[j : j + 1, lanes(c)] = jnp.sum(acc[j], axis=0, keepdims=True)
+            at = 9 * c + j
+            small[at : at + 1, :] = jnp.sum(acc[j], axis=0, keepdims=True)
+
+
+    for ref in (keep_ref, send_ref):
+        ref[small_at : small_at + SMALL, :] = small[...].astype(BF16)
+
+
+def vmem():
+    return pl.BlockSpec(memory_space=pltpu.VMEM)
+
+
+def smem():
+    return pl.BlockSpec(memory_space=pltpu.SMEM)
 
 
 def tile_step(limits, x, t, top, bot, right, left, k1, p1, taps, k2, p2):
     rows, cols, chan = x.shape
-    hid = k2.shape[1]
+    hid = k2.shape[2]
     hr, hc = rows // 2, cols // 2
     slots = hc + 2 * HALO
     cb1, cb2 = chan // LANES, hid // LANES
-    vm = pl.BlockSpec(memory_space=pltpu.VMEM)
+    grads = (p1.size + taps.size + p2.size) // (2 * LANES) + SMALL
     return pl.pallas_call(
         tile_kernel,
         out_shape=(
             jax.ShapeDtypeStruct(x.shape, BF16),
-            jax.ShapeDtypeStruct(k1.shape, F32),
-            jax.ShapeDtypeStruct(p1.shape, F32),
-            jax.ShapeDtypeStruct(taps.shape, F32),
-            jax.ShapeDtypeStruct(k2.shape, F32),
-            jax.ShapeDtypeStruct(p2.shape, F32),
+            jax.ShapeDtypeStruct((grads, LANES), BF16),
+            jax.ShapeDtypeStruct((grads, LANES), BF16),
         ),
-        in_specs=[pl.BlockSpec(memory_space=pltpu.SMEM)] + [vm] * 11,
-        out_specs=[vm] * 6,
+        in_specs=[smem()] + [vmem()] * 11,
+        out_specs=[vmem()] * 3,
         scratch_shapes=[
             pltpu.VMEM((cb1, rows + 2 * ROWS, cols + 32, LANES), F32),
             pltpu.VMEM((cb1, 8, cols + 32, LANES), F32),
@@ -339,9 +367,167 @@
             pltpu.VMEM(((hr + 2) * hc, chan), BF16),
             pltpu.VMEM((hr * hc, hid), BF16),
             pltpu.VMEM((4, cb1, hr, hc, LANES), F32),
+            pltpu.VMEM((SMALL, LANES), F32),
         ],
         compiler_params=pltpu.CompilerParams(vmem_limit_bytes=63 * 1024 * 1024),
+        cost_estimate=pl.CostEstimate(flops=9_000_000_000, bytes_accessed=20_000_000, transcendentals=0),
     )(limits, x, t, top, bot, right, left, k1, p1, taps, k2, p2)
+
+
+def norm_kernel(p1_ref, st_ref, p2_ref, k1_ref, k2_ref, out_ref):
+    @pl.when(pl.program_id(0) == 0)
+    def _():
+        for j, ref in ((0, k1_ref), (1, p1_ref), (3, k2_ref), (4, p2_ref)):
+            out_ref[j] = jnp.sum(ref[...] * ref[...])
+        out_ref[2] = 0.0
+
+    out_ref[2] += jnp.sum(st_ref[...] * st_ref[...])
+
+
+def norms(k1, p1, taps, k2, p2):
+    parts = taps.shape[0]
+    return pl.pallas_call(
+        norm_kernel,
+        grid=(parts,),
+        out_shape=jax.ShapeDtypeStruct((5,), F32),
+        in_specs=[
+            pl.BlockSpec(p1.shape, lambda n: (0, 0)),
+            pl.BlockSpec((1,) + taps.shape[1:], lambda n: (n, 0, 0)),
+            pl.BlockSpec(p2.shape, lambda n: (0, 0)),
+            pl.BlockSpec(k1.shape, lambda n: (0, 0, 0)),
+            pl.BlockSpec(k2.shape, lambda n: (0, 0, 0)),
+        ],
+        out_specs=smem(),
+        cost_estimate=pl.CostEstimate(flops=3_000_000, bytes_accessed=5_300_000, transcendentals=0),
+    )(p1, taps, p2, k1, k2)
+
+
+def update_kernel(
+    where,
+    sums,
+    own_ref,
+    other_ref,
+    k1_ref,
+    p1_ref,
+    st_ref,
+    k2_ref,
+    p2_ref,
+    nk1_ref,
+    np1_ref,
+    nst_ref,
+    nk2_ref,
+    np2_ref,
+    sk1_ref,
+    sp1_ref,
+    sst_ref,
+    sk2_ref,
+    sp2_ref,
+    g,
+    small,
+    scale,
+):
+    chan, hid = p1_ref.shape
+    cb1, cb2 = chan // LANES, hid // LANES
+    parts, block = 4, st_ref.shape[1]
+    step = pl.program_id(0)
+    core = where[0]
+    st_rows, p1_rows, p2_rows = hid * cb2, chan * cb2, hid * cb1
+    p1_at = 2 * st_rows
+    p2_at = p1_at + p1_rows // 2
+    small_at = p2_at + p2_rows // 2
+    sizes = (9 * chan, chan * hid, parts * hid * hid, 9 * hid, chan * hid)
+
+    def root(v):
+        v = jnp.full((8, LANES), v, F32)
+        r = lax.rsqrt(v)
+        r = r * (1.5 - 0.5 * v * r * r)
+        return (v * r)[0, 0]
+
+    def squares(at, count):
+        acc = jnp.zeros((8, LANES), F32)
+        for half in range(2):
+
+            def body(n, acc, half=half):
+                v = g[half, pl.ds(at + n * 128, 128), :].astype(F32)
+                return acc + jnp.sum((v * v).reshape(16, 8, LANES), axis=0)
+
+            acc = lax.fori_loop(0, count // 128, body, acc)
+        return jnp.sum(acc)
+
+    def set_scale(j, total):
+        scale[j] = 1.0 / root(total / sizes[j] + EPS)
+        scale[5 + j] = RATE * root(sums[j] / sizes[j] + EPS)
+
+    @pl.when(step == 0)
+    def _():
+        g[core] = own_ref[0:small_at, :]
+        g[1 - core] = other_ref[...]
+        small[...] = own_ref[small_at : small_at + SMALL, :].astype(F32)
+        v = small[0 : 9 * cb1, :]
+        set_scale(0, jnp.sum(v * v))
+        v = small[9 * cb1 : 9 * (cb1 + cb2), :]
+        set_scale(3, jnp.sum(v * v))
+        set_scale(1, squares(p1_at, p1_rows // 2))
+        set_scale(2, squares(0, 2 * st_rows))
+        set_scale(4, squares(p2_at, p2_rows // 2))
+        for j, first, blocks, w, new, out in (
+            (0, 0, cb1, k1_ref, nk1_ref, sk1_ref),
+            (3, 9 * cb1, cb2, k2_ref, nk2_ref, sk2_ref),
+        ):
+            for c in range(blocks):
+                cut = slice(c * LANES, (c + 1) * LANES)
+                for r in range(3):
+                    at = first + 9 * c + 3 * r
+                    normed = small[at : at + 3, :] * scale[j]
+                    out[r, :, cut] = normed
+                    new[r, :, cut] = w[r, :, cut] - scale[5 + j] * normed
+        for c in range(cb2):
+            cut = slice(c * LANES, (c + 1) * LANES)
+            at = p1_at + (c % (cb2 // 2)) * chan
+            normed = g[2 * c // cb2, at : at + chan, :].astype(F32) * scale[1]
+            sp1_ref[:, cut] = normed
+            np1_ref[:, cut] = p1_ref[:, cut] - scale[6] * normed
+        for c in range(cb1):
+            cut = slice(c * LANES, (c + 1) * LANES)
+            at = p2_at + (c % (cb1 // 2)) * hid
+            normed = g[2 * c // cb1, at : at + hid, :].astype(F32) * scale[4]
+            sp2_ref[:, cut] = normed
+            np2_ref[:, cut] = p2_ref[:, cut] - scale[9] * normed
+
+    per = hid // block
+    ph = step // per
+    for c in range(cb2):
+        cut = slice(c * LANES, (c + 1) * LANES)
+        at = (ph % 2) * st_rows + c * hid + (step % per) * block
+        normed = g[ph // 2, pl.ds(at, block), :].astype(F32) * scale[2]
+        sst_ref[0, :, cut] = normed
+        nst_ref[0, :, cut] = st_ref[0, :, cut] - scale[7] * normed
+
+
+def update(where, sums, own, other, k1, p1, taps, k2, p2):
+    hid = taps.shape[1]
+    block = hid // 4
+    per = hid // block
+
+    def whole(w):
+        return pl.BlockSpec(w.shape, lambda n: (0,) * w.ndim)
+
+    st = pl.BlockSpec((1, block, hid), lambda n: (n // per, n % per, 0))
+    specs = [whole(k1), whole(p1), st, whole(k2), whole(p2)]
+    shapes = [jax.ShapeDtypeStruct(w.shape, F32) for w in (k1, p1, taps, k2, p2)]
+    return pl.pallas_call(
+        update_kernel,
+        grid=(4 * per,),
+        out_shape=shapes + shapes,
+        in_specs=[smem(), smem(), whole(own), whole(other)] + specs,
+        out_specs=specs + specs,
+        scratch_shapes=[
+            pltpu.VMEM((2,) + other.shape, BF16),
+            pltpu.VMEM((SMALL, LANES), F32),
+            pltpu.SMEM((10,), F32),
+        ],
+        compiler_params=pltpu.CompilerParams(vmem_limit_bytes=40 * 1024 * 1024),
+    )(where, sums, own, other, k1, p1, taps, k2, p2)
 
 
 def shift(block, axis, step):
@@ -351,9 +537,66 @@
     )
 
 
-def adjusted(weight, grad):
-    normed = grad / jnp.sqrt(jnp.mean(grad * grad) + EPS)
-    return weight - RATE * jnp.sqrt(jnp.mean(weight * weight) + EPS) * normed, normed
+class Ring:
+    def __init__(self, name):
+        axis = {"x": "tx", "y": "rep", "z": "ty"}[name]
+        inner = 2 if name == "x" else 1
+        self.axis, self.inner = axis, inner
+        self.count = lax.axis_size(axis) // inner
+        self.me = lax.axis_index(axis) // inner
+
+    def send(self, block, step):
+        n, inner = self.count, self.inner
+        pairs = [
+            (i * inner + k, (i + step) % n * inner + k) for i in range(n) for k in range(inner)
+        ]
+        return lax.ppermute(block, self.axis, pairs)
+
+    def scatter(self, block, extra):
+        n = self.count
+        shares = block.reshape((n, -1, LANES))
+        share = lax.dynamic_index_in_dim(shares, self.me, 0, False)
+        cut = share.shape[0]
+        got = []
+        for d in range(1, n):
+            out = lax.dynamic_index_in_dim(shares, (self.me + d) % n, 0, False)
+            if extra is not None:
+                out = jnp.concatenate([out, extra], axis=0)
+            got.append(self.send(out, d))
+        total = sum([g[:cut].astype(F32) for g in got], share.astype(F32)).astype(BF16)
+        if extra is not None:
+            extra = sum([g[cut:].astype(F32) for g in got], extra.astype(F32)).astype(BF16)
+        return total, extra
+
+    def gather(self, share):
+        n = self.count
+        out = jnp.zeros((n,) + share.shape, share.dtype)
+        out = lax.dynamic_update_index_in_dim(out, share, self.me, 0)
+        for d in range(1, n):
+            got = self.send(share, d)
+            out = lax.dynamic_update_index_in_dim(out, got, (self.me + n - d) % n, 0)
+        return out.reshape(-1, LANES)
+
+
+def reduced(keep, send):
+    x, y, z = Ring("x"), Ring("y"), Ring("z")
+    cores = [(i, i ^ 1) for i in range(lax.axis_size("tx"))]
+    got = lax.ppermute(send, "tx", cores)
+    both = (keep.astype(F32) + got.astype(F32)).astype(BF16)
+    size = both.shape[0] - SMALL
+    first, second, small = both[: size // 2], both[size // 2 : size], both[size:]
+    first, small = x.scatter(first, small)
+    second, _ = y.scatter(second, None)
+    first, small = y.scatter(first, small)
+    second, _ = x.scatter(second, None)
+    share, small = z.scatter(jnp.concatenate([first, second], axis=0), small)
+    both = z.gather(share)
+    size = both.shape[0]
+    first, second = y.gather(both[: size // 2]), x.gather(both[size // 2 :])
+    first, second = x.gather(first), y.gather(second)
+    half = jnp.concatenate([first, second], axis=0)
+    other = lax.ppermute(half, "tx", cores)
+    return jnp.concatenate([half, small], axis=0), other
 
 
 def per_device(inputs, targets, kern_one, point_one, coarsening_taps, kern_two, point_two):
@@ -383,9 +626,11 @@
             jnp.where(ty == lax.axis_size("ty") - 1, hr, big),
             jnp.where(tx == 0, 0, -big),
             jnp.where(tx == lax.axis_size("tx") - 1, hc, big),
+            tx % 2,
         ]
     ).astype(jnp.int32)
-    pred, gk1, gp1, gst, gk2, gp2 = tile_step(
+    taps = coarsening_taps.reshape(4, hid, hid)
+    pred, keep, send = tile_step(
         limits,
         x,
         t,
@@ -393,20 +638,18 @@
         bot,
         right,
         left,
-        kern_one.reshape(9, chan),
+        kern_one,
         point_one.astype(BF16),
-        coarsening_taps.astype(BF16).reshape(4, hid, hid),
-        kern_two.reshape(9, hid),
+        taps.astype(BF16),
+        kern_two,
         point_two.astype(BF16),
     )
-    weights = (kern_one, point_one, coarsening_taps, kern_two, point_two)
-    grads = lax.psum((gk1, gp1, gst, gk2, gp2), AXES)
-    pairs = [adjusted(w, g.reshape(w.shape)) for w, g in zip(weights, grads)]
-    return (
-        jnp.transpose(pred, (2, 0, 1))[None],
-        *[p[0] for p in pairs],
-        *[p[1] for p in pairs],
-    )
+    weights, send = lax.optimization_barrier(((kern_one, point_one, taps, kern_two, point_two), send))
+    sums = norms(*weights)
+    own, other = reduced(keep, send)
+    outs = update((tx % 2)[None].astype(jnp.int32), sums, own, other, *weights)
+    outs = [o.reshape(coarsening_taps.shape) if o.shape == taps.shape else o for o in outs]
+    return (jnp.transpose(pred, (2, 0, 1))[None], *outs)
 
 
 def solution(mesh):

time: 256 us -> 166 us (0.65)
  blocking collectives: 69.2 us -> 0 us
  starting transfers between devices: 11.7 us -> 62.9 us
  waiting for transfers between devices: 85 us -> 34.2 us
  between operations: 21.3 us -> 1.27 us
  other arithmetic: 27.6 us -> 9.21 us
  Pallas kernels: 32.4 us -> 48.8 us
    psum x1 -> x0, waiting for transfers between devices: 83.4 us -> none  [per_device(): grads = lax.psum((gk1, gp1, gst, gk2, gp2), AXES)]
    psum x1 -> x0, blocking collectives: 69.2 us -> none  [per_device(): grads = lax.psum((gk1, gp1, gst, gk2, gp2), AXES)]
    ppermute x0 -> x32, starting transfers between devices: none -> 50.6 us  [the longest x30 34.9 us: send(): return lax.ppermute(block, self.axis, pairs)]
    ppermute x0 -> x32, waiting for transfers between devices: none -> 30.5 us  [the longest x30 27.2 us: send(): return lax.ppermute(block, self.axis, pairs)]
    reduce_sum x10 -> x0, other arithmetic: 17.1 us -> none  [the longest x5 9.47 us: adjusted(): jnp.mean(weight * weight) + EPS]
    pallas_call x0 -> x2, Pallas kernels: none -> 15.8 us  [the longest x1 11 us: update(): pl.pallas_call(update_kernel, grid=(4 * per,), out_shape=shapes + shapes,...]
    convert_element_type x0 -> x11, other arithmetic: none -> 7.18 us  [the longest x1 3.77 us: per_device(): taps.astype(BF16)]
    sub x5 -> x0, other arithmetic: 6.37 us -> none  [adjusted(): weight - RATE * jnp.sqrt(jnp.mean(weight * weight) + EPS) * normed]
  transfers between devices with their start and end apart: 5 -> 36, of which waited for: 3 -> 15; matrix products, arithmetic and copies ran while one was open for 6% -> 5% of each run, Pallas kernels for 0% -> 3%
where the time goes in v1:
time: 166 us
  starting transfers between devices  62.9 us (38%)
  Pallas kernels  48.8 us (29%)
  waiting for transfers between devices  34.2 us (21%)
  local copies, waits for them, and re-layouts  9.48 us (6%)
  other arithmetic  9.21 us (6%)
    ppermute x30, starting transfers between devices, send(): return lax.ppermute(block, self.axis, pairs)  34.9 us
    pallas_call x1, Pallas kernels, tile_step(): pl.pallas_call(tile_kernel, out_shape=(jax.ShapeDtypeStruct(x.shape, BF16...  33 us
    ppermute x30, waiting for transfers between devices, send(): return lax.ppermute(block, self.axis, pairs)  27.2 us
    ppermute x1, starting transfers between devices, reduced(): other = lax.ppermute(half, 'tx', cores)  15.7 us
    ppermute x4, starting transfers between devices, shift(): lax.ppermute(block, axis, [(i, i + step) for i in range(count) if 0 <= i...  12.3 us
    pallas_call x1, Pallas kernels, update(): pl.pallas_call(update_kernel, grid=(4 * per,), out_shape=shapes + shapes,...  11 us
    pallas_call x1, Pallas kernels, norms(): pl.pallas_call(norm_kernel, grid=(parts,), out_shape=jax.ShapeDtypeStruct...  4.85 us
    unnamed x30, local copies, waits for them, and re-layouts  4.83 us
  transfers between devices with their start and end apart: 36, of which 15 were waited for; matrix products, arithmetic and copies ran while one was open for 5% of the time, Pallas kernels for 3%

profile of v1, /device:TPU:1, one launch (start us, length us, event | category | flops | bytes accessed | tf_op | source)
XLA Modules:
  0.0 165.9 jit_solution(9354945396937334709)
XLA Ops:
  2.5 4.4 %collective-permute-start = (bf16[8,32,256]{2,1,0:T(8,128)(2,1)S(1)}, bf16[8,32,256]{2,1,0:T(8,128)(2,1)S(1)}, u32[]{:S(2)}, u32[]{:S(2)}) collective-permute-start(bf16[8,32,256]{2,1,0:T(8,128)(2,1)S(1)} %pad_maximum_fusion.7), channel_id=1, source_target_pairs={{0,8},{8,16},{16,24},{1,9},{9,17},{17,25},{2,10},{10,18},{18,26},{... | collective-permute-start | bytes 393224 | tf_op jit(solution)/shard_map/ppermute | solution.py:535
  6.9 1.3 collective-permute-start.1
  9.5 3.7 %collective-permute-done.1.bot_ref = bf16[8,32,256]{2,1,0:T(8,128)(2,1)S(1)} collective-permute-done((bf16[8,32,256]{2,1,0:T(8,128)(2,1)S(1)}, bf16[8,32,256]{2,1,0:T(8,128)(2,1)S(1)}, u32[]{:S(2)}, u32[]{:S(2)}) %collective-permute-start.1) | collective-permute-done | bytes 131104 | tf_op jit(solution)/shard_map/ppermute | solution.py:535
  13.9 3.6 %collective-permute-start.2 = (bf16[108,8,256]{2,1,0:T(8,128)(2,1)S(1)}, bf16[108,8,256]{2,1,0:T(8,128)(2,1)S(1)}, u32[]{:S(2)}, u32[]{:S(2)}) collective-permute-start(bf16[108,8,256]{2,1,0:T(8,128)(2,1)S(1)} %fusion.11), channel_id=1, source_target_pairs={{1,0},{2,1},{3,2},{4,3},{5,4},{6,5},{7,6},{9,8},{10,9},{11,10},{12... | collective-permute-start | bytes 1327112 | tf_op jit(solution)/shard_map/ppermute | solution.py:535
  17.8 3.0 %collective-permute-start.3 = (bf16[108,8,256]{2,1,0:T(8,128)(2,1)S(1)}, bf16[108,8,256]{2,1,0:T(8,128)(2,1)S(1)}, u32[]{:S(2)}, u32[]{:S(2)}) collective-permute-start(bf16[108,8,256]{2,1,0:T(8,128)(2,1)S(1)} %fusion.15), channel_id=1, source_target_pairs={{0,1},{1,2},{2,3},{3,4},{4,5},{5,6},{6,7},{8,9},{9,10},{10,11},{11... | collective-permute-start | bytes 1327112 | tf_op jit(solution)/shard_map/ppermute | solution.py:535
  22.9 3.8 %bitcast_convert_fusion.taps_ref = bf16[4,512,512]{2,1,0:T(8,128)(2,1)} fusion(f32[2,2,512,512]{3,2,1,0:T(8,128)} %param.11), kind=kLoop, calls=%fused_computation.106 | loop fusion | flops 1048576 | bytes 6291456 | tf_op jit(solution)/shard_map/convert_element_type | solution.py:643
  28.2 33.0 %shard_map.158 = (bf16[96,32,256]{2,1,0:T(8,128)(2,1)}, bf16[5184,128]{1,0:T(8,128)(2,1)}, bf16[5184,128]{1,0:T(8,128)(2,1)}) custom-call(s32[5]{0:T(128)} %stack.23.limits, bf16[96,32,256]{2,1,0:T(8,128)(2,1)} %bitcast.145, bf16[96,32,256]{2,1,0:T(8,128)(2,1)} %bitcast.147, bf16[8,32,256]{2,1,0:T(8,128)(2,1)} %copy-done.9, bf16[8,32,256]{2,1,0:T(8,128)(2,1)} %copy-done.10, ...), custom_call_target="tpu_custom_call" | custom-call | flops 8999999488 | bytes 20000000 | tf_op jit(solution)/shard_map/pallas_call | solution.py:346
  61.2 3.3 %collective-permute-done.4 = bf16[5184,128]{1,0:T(8,128)(2,1)S(1)} collective-permute-done((bf16[5184,128]{1,0:T(8,128)(2,1)}, bf16[5184,128]{1,0:T(8,128)(2,1)S(1)}, u32[]{:S(2)}, u32[]{:S(2)}) %collective-permute-start.4) | collective-permute-done | bytes 1327136 | tf_op jit(solution)/shard_map/ppermute | solution.py:584
  64.5 1.7 %add_convert_fusion = bf16[5184,128]{1,0:T(8,128)(2,1)S(1)} fusion(bf16[5184,128]{1,0:T(8,128)(2,1)S(1)} %collective-permute-done.4, bf16[5184,128]{1,0:T(8,128)(2,1)} %get-tuple-element.37), kind=kLoop, calls=%fused_computation | loop fusion | flops 2654208 | bytes 3981312 | tf_op jit(solution)/shard_map/convert_element_type | solution.py:585
  66.3 1.4 collective-permute-start.11
  67.7 1.5 collective-permute-start.13
  69.2 1.6 collective-permute-start.12
  72.1 1.5 collective-permute-start.7
  73.6 2.1 %collective-permute-start.6 = (bf16[704,128]{1,0:T(8,128)(2,1)S(1)}, bf16[704,128]{1,0:T(8,128)(2,1)S(1)}, u32[]{:S(2)}, u32[]{:S(2)}) collective-permute-start(bf16[704,128]{1,0:T(8,128)(2,1)S(1)} %get-tuple-element.94), channel_id=1, source_target_pairs={{0,4},{1,5},{2,6},{3,7},{4,0},{5,1},{6,2},{7,3},{8,12},{9,13},{10,... | collective-permute-start | bytes 540680 | tf_op jit(solution)/shard_map/ppermute | solution.py:553
  75.7 2.3 %collective-permute-done.12 = bf16[640,128]{1,0:T(8,128)(2,1)S(1)} collective-permute-done((bf16[640,128]{1,0:T(8,128)(2,1)S(1)}, bf16[640,128]{1,0:T(8,128)(2,1)S(1)}, u32[]{:S(2)}, u32[]{:S(2)}) %collective-permute-start.12) | collective-permute-done | bytes 163872 | tf_op jit(solution)/shard_map/ppermute | solution.py:553
  79.4 1.5 collective-permute-start.16
  82.8 1.6 collective-permute-start.9
  87.8 1.5 collective-permute-start.17
  89.3 1.8 %collective-permute-start.18 = (bf16[144,128]{1,0:T(8,128)(2,1)S(1)}, bf16[144,128]{1,0:T(8,128)(2,1)S(1)}, u32[]{:S(2)}, u32[]{:S(2)}) collective-permute-start(bf16[144,128]{1,0:T(8,128)(2,1)S(1)} %get-tuple-element.87), channel_id=1, source_target_pairs={{0,16},{8,24},{16,0},{24,8},{1,17},{9,25},{17,1},{25,9},{2,18},{10... | collective-permute-start | bytes 110600 | tf_op jit(solution)/shard_map/ppermute | solution.py:553
  91.0 2.0 %collective-permute-start.19 = (bf16[144,128]{1,0:T(8,128)(2,1)S(1)}, bf16[144,128]{1,0:T(8,128)(2,1)S(1)}, u32[]{:S(2)}, u32[]{:S(2)}) collective-permute-start(bf16[144,128]{1,0:T(8,128)(2,1)S(1)} %get-tuple-element.88), channel_id=1, source_target_pairs={{0,24},{8,0},{16,8},{24,16},{1,25},{9,1},{17,9},{25,17},{2,26},{10... | collective-permute-start | bytes 110600 | tf_op jit(solution)/shard_map/ppermute | solution.py:553
  95.1 3.3 %collective-permute-start.21 = (bf16[80,128]{1,0:T(8,128)(2,1)S(1)}, bf16[80,128]{1,0:T(8,128)(2,1)S(1)}, u32[]{:S(2)}, u32[]{:S(2)}) collective-permute-start(bf16[80,128]{1,0:T(8,128)(2,1)S(1)} %get-tuple-element.50), channel_id=1, source_target_pairs={{0,16},{8,24},{16,0},{24,8},{1,17},{9,25},{17,1},{25,9},{2,18},{10... | collective-permute-start | bytes 61448 | tf_op jit(solution)/shard_map/ppermute | solution.py:553
  101.0 1.4 collective-permute-start.31
  103.8 2.4 %collective-permute-start.25 = (bf16[160,128]{1,0:T(8,128)(2,1)S(1)}, bf16[160,128]{1,0:T(8,128)(2,1)S(1)}, u32[]{:S(2)}, u32[]{:S(2)}) collective-permute-start(bf16[160,128]{1,0:T(8,128)(2,1)S(1)} %bitcast.155), channel_id=1, source_target_pairs={{0,96},{32,0},{64,32},{96,64},{1,97},{33,1},{65,33},{97,65},{2,98}... | collective-permute-start | bytes 122888 | tf_op jit(solution)/shard_map/ppermute | solution.py:553
  106.3 4.0 %collective-permute-done.23 = bf16[160,128]{1,0:T(8,128)(2,1)S(1)} collective-permute-done((bf16[160,128]{1,0:T(8,128)(2,1)S(1)}, bf16[160,128]{1,0:T(8,128)(2,1)S(1)}, u32[]{:S(2)}, u32[]{:S(2)}) %collective-permute-start.23) | collective-permute-done | bytes 40992 | tf_op jit(solution)/shard_map/ppermute | solution.py:553
  110.3 4.3 %collective-permute-done.24 = bf16[160,128]{1,0:T(8,128)(2,1)S(1)} collective-permute-done((bf16[160,128]{1,0:T(8,128)(2,1)S(1)}, bf16[160,128]{1,0:T(8,128)(2,1)S(1)}, u32[]{:S(2)}, u32[]{:S(2)}) %collective-permute-start.24) | collective-permute-done | bytes 40992 | tf_op jit(solution)/shard_map/ppermute | solution.py:553
  114.6 2.2 %collective-permute-start.28 = (bf16[640,128]{1,0:T(8,128)(2,1)S(1)}, bf16[640,128]{1,0:T(8,128)(2,1)S(1)}, u32[]{:S(2)}, u32[]{:S(2)}) collective-permute-start(bf16[640,128]{1,0:T(8,128)(2,1)S(1)} %bitcast.131), channel_id=1, source_target_pairs={{0,6},{1,7},{2,0},{3,1},{4,2},{5,3},{6,4},{7,5},{8,14},{9,15},{10,... | collective-permute-start | bytes 491528 | tf_op jit(solution)/shard_map/ppermute | solution.py:553
  119.0 5.3 %collective-permute-done.26 = bf16[640,128]{1,0:T(8,128)(2,1)S(1)} collective-permute-done((bf16[640,128]{1,0:T(8,128)(2,1)S(1)}, bf16[640,128]{1,0:T(8,128)(2,1)S(1)}, u32[]{:S(2)}, u32[]{:S(2)}) %collective-permute-start.26) | collective-permute-done | bytes 163872 | tf_op jit(solution)/shard_map/ppermute | solution.py:553
  124.4 5.3 %collective-permute-done.32 = bf16[640,128]{1,0:T(8,128)(2,1)S(1)} collective-permute-done((bf16[640,128]{1,0:T(8,128)(2,1)S(1)}, bf16[640,128]{1,0:T(8,128)(2,1)S(1)}, u32[]{:S(2)}, u32[]{:S(2)}) %collective-permute-start.32) | collective-permute-done | bytes 163872 | tf_op jit(solution)/shard_map/ppermute | solution.py:553
  130.9 15.7 %collective-permute-start.35 = (bf16[5120,128]{1,0:T(8,128)(2,1)}, bf16[5120,128]{1,0:T(8,128)(2,1)S(1)}, u32[]{:S(2)}, u32[]{:S(2)}) collective-permute-start(bf16[5120,128]{1,0:T(8,128)(2,1)} %pad_maximum_fusion.1), channel_id=1, source_target_pairs={{0,1},{1,0},{2,3},{3,2},{4,5},{5,4},{6,7},{7,6},{8,9},{9,8},{10,11... | collective-permute-start | bytes 3932168 | tf_op jit(solution)/shard_map/ppermute | solution.py:598
  146.6 4.8 %shard_map.159.sums = f32[5]{0:T(128)} custom-call(f32[256,512]{1,0:T(8,128)} %p1_ref.1, f32[4,512,512]{2,1,0:T(8,128)} %bitcast.120, f32[512,256]{1,0:T(8,128)} %p2_ref.1, f32[3,3,256]{2,1,0:T(4,128)} %k1_ref.3, f32[3,3,512]{2,1,0:T(4,128)} %k2_ref.3), custom_call_target="tpu_custom_call" | custom-call | flops 3000000 | bytes 5300000 | tf_op jit(solution)/shard_map/pallas_call | solution.py:389
  152.7 2.2 %copy-done = f32[2,2,512,512]{3,2,1,0:T(8,128)S(1)} copy-done((f32[2,2,512,512]{3,2,1,0:T(8,128)S(1)}, f32[2,2,512,512]{3,2,1,0:T(8,128)}, u32[]{:S(2)}) %copy-start) | copy-done | bytes 4194328
  154.9 11.0 %shard_map.160 = (f32[3,3,256]{2,1,0:T(4,128)}, f32[256,512]{1,0:T(8,128)}, f32[4,512,512]{2,1,0:T(8,128)}, f32[3,3,512]{2,1,0:T(4,128)}, f32[512,256]{1,0:T(8,1...) custom-call(s32[1]{0:T(128)} %bitcast.4.where, ...), custom_call_target="tpu_custom_call" | custom-call | tf_op jit(solution)/shard_map/pallas_call | solution.py:518
  (138 shorter events, 26.5 us)
Async XLA Ops:
  2.5 6.9 %collective-permute-start = (bf16[8,32,256]{2,1,0:T(8,128)(2,1)S(1)}, bf16[8,32,256]{2,1,0:T(8,128)(2,1)S(1)}, u32[]{:S(2)}, u32[]{:S(2)}) collective-permute-start(bf16[8,32,256]{2,1,0:T(8,128)(2,1)S(1)} %pad_maximum_fusion.7), channel_id=1, source_target_pairs={{0,8},{8,16},{16,24},{1,9},{9,17},{17,25},{2,10},{10,18},{18,26},{... | collective-permute-start | bytes 393224 | tf_op jit(solution)/shard_map/ppermute | solution.py:535
  6.9 6.3 %collective-permute-start.1 = (bf16[8,32,256]{2,1,0:T(8,128)(2,1)S(1)}, bf16[8,32,256]{2,1,0:T(8,128)(2,1)S(1)}, u32[]{:S(2)}, u32[]{:S(2)}) collective-permute-start(bf16[8,32,256]{2,1,0:T(8,128)(2,1)S(1)} %pad_maximum_fusion.8), channel_id=1, source_target_pairs={{8,0},{16,8},{24,16},{9,1},{17,9},{25,17},{10,2},{18,10},{26,18},{... | collective-permute-start | bytes 393224 | tf_op jit(solution)/shard_map/ppermute | solution.py:535
  13.9 12.8 %collective-permute-start.2 = (bf16[108,8,256]{2,1,0:T(8,128)(2,1)S(1)}, bf16[108,8,256]{2,1,0:T(8,128)(2,1)S(1)}, u32[]{:S(2)}, u32[]{:S(2)}) collective-permute-start(bf16[108,8,256]{2,1,0:T(8,128)(2,1)S(1)} %fusion.11), channel_id=1, source_target_pairs={{1,0},{2,1},{3,2},{4,3},{5,4},{6,5},{7,6},{9,8},{10,9},{11,10},{12... | collective-permute-start | bytes 1327112 | tf_op jit(solution)/shard_map/ppermute | solution.py:535
  17.8 8.9 %collective-permute-start.3 = (bf16[108,8,256]{2,1,0:T(8,128)(2,1)S(1)}, bf16[108,8,256]{2,1,0:T(8,128)(2,1)S(1)}, u32[]{:S(2)}, u32[]{:S(2)}) collective-permute-start(bf16[108,8,256]{2,1,0:T(8,128)(2,1)S(1)} %fusion.15), channel_id=1, source_target_pairs={{0,1},{1,2},{2,3},{3,4},{4,5},{5,6},{6,7},{8,9},{9,10},{10,11},{11... | collective-permute-start | bytes 1327112 | tf_op jit(solution)/shard_map/ppermute | solution.py:535
  66.3 7.3 %collective-permute-start.11 = (bf16[640,128]{1,0:T(8,128)(2,1)S(1)}, bf16[640,128]{1,0:T(8,128)(2,1)S(1)}, u32[]{:S(2)}, u32[]{:S(2)}) collective-permute-start(bf16[640,128]{1,0:T(8,128)(2,1)S(1)} %get-tuple-element.61), channel_id=1, source_target_pairs={{0,32},{32,64},{64,96},{96,0},{1,33},{33,65},{65,97},{97,1},{2,34}... | collective-permute-start | bytes 491528 | tf_op jit(solution)/shard_map/ppermute | solution.py:553
  67.7 8.0 %collective-permute-start.13 = (bf16[640,128]{1,0:T(8,128)(2,1)S(1)}, bf16[640,128]{1,0:T(8,128)(2,1)S(1)}, u32[]{:S(2)}, u32[]{:S(2)}) collective-permute-start(bf16[640,128]{1,0:T(8,128)(2,1)S(1)} %get-tuple-element.62), channel_id=1, source_target_pairs={{0,96},{32,0},{64,32},{96,64},{1,97},{33,1},{65,33},{97,65},{2,98}... | collective-permute-start | bytes 491528 | tf_op jit(solution)/shard_map/ppermute | solution.py:553
  69.2 8.8 %collective-permute-start.12 = (bf16[640,128]{1,0:T(8,128)(2,1)S(1)}, bf16[640,128]{1,0:T(8,128)(2,1)S(1)}, u32[]{:S(2)}, u32[]{:S(2)}) collective-permute-start(bf16[640,128]{1,0:T(8,128)(2,1)S(1)} %get-tuple-element.63), channel_id=1, source_target_pairs={{0,64},{32,96},{64,0},{96,32},{1,65},{33,97},{65,1},{97,33},{2,66}... | collective-permute-start | bytes 491528 | tf_op jit(solution)/shard_map/ppermute | solution.py:553
  70.8 10.0 %collective-permute-start.5 = (bf16[704,128]{1,0:T(8,128)(2,1)S(1)}, bf16[704,128]{1,0:T(8,128)(2,1)S(1)}, u32[]{:S(2)}, u32[]{:S(2)}) collective-permute-start(bf16[704,128]{1,0:T(8,128)(2,1)S(1)} %get-tuple-element.92), channel_id=1, source_target_pairs={{0,2},{1,3},{2,4},{3,5},{4,6},{5,7},{6,0},{7,1},{8,10},{9,11},{10,... | collective-permute-start | bytes 540680 | tf_op jit(solution)/shard_map/ppermute | solution.py:553
  72.1 9.9 %collective-permute-start.7 = (bf16[704,128]{1,0:T(8,128)(2,1)S(1)}, bf16[704,128]{1,0:T(8,128)(2,1)S(1)}, u32[]{:S(2)}, u32[]{:S(2)}) collective-permute-start(bf16[704,128]{1,0:T(8,128)(2,1)S(1)} %get-tuple-element.93), channel_id=1, source_target_pairs={{0,6},{1,7},{2,0},{3,1},{4,2},{5,3},{6,4},{7,5},{8,14},{9,15},{10,... | collective-permute-start | bytes 540680 | tf_op jit(solution)/shard_map/ppermute | solution.py:553
  73.6 8.4 %collective-permute-start.6 = (bf16[704,128]{1,0:T(8,128)(2,1)S(1)}, bf16[704,128]{1,0:T(8,128)(2,1)S(1)}, u32[]{:S(2)}, u32[]{:S(2)}) collective-permute-start(bf16[704,128]{1,0:T(8,128)(2,1)S(1)} %get-tuple-element.94), channel_id=1, source_target_pairs={{0,4},{1,5},{2,6},{3,7},{4,0},{5,1},{6,2},{7,3},{8,12},{9,13},{10,... | collective-permute-start | bytes 540680 | tf_op jit(solution)/shard_map/ppermute | solution.py:553
  78.1 6.3 %collective-permute-start.14 = (bf16[160,128]{1,0:T(8,128)(2,1)S(1)}, bf16[160,128]{1,0:T(8,128)(2,1)S(1)}, u32[]{:S(2)}, u32[]{:S(2)}) collective-permute-start(bf16[160,128]{1,0:T(8,128)(2,1)S(1)} %get-tuple-element.67), channel_id=1, source_target_pairs={{0,2},{1,3},{2,4},{3,5},{4,6},{5,7},{6,0},{7,1},{8,10},{9,11},{10,... | collective-permute-start | bytes 122888 | tf_op jit(solution)/shard_map/ppermute | solution.py:553
  79.4 5.9 %collective-permute-start.16 = (bf16[160,128]{1,0:T(8,128)(2,1)S(1)}, bf16[160,128]{1,0:T(8,128)(2,1)S(1)}, u32[]{:S(2)}, u32[]{:S(2)}) collective-permute-start(bf16[160,128]{1,0:T(8,128)(2,1)S(1)} %get-tuple-element.68), channel_id=1, source_target_pairs={{0,6},{1,7},{2,0},{3,1},{4,2},{5,3},{6,4},{7,5},{8,14},{9,15},{10,... | collective-permute-start | bytes 122888 | tf_op jit(solution)/shard_map/ppermute | solution.py:553
  80.9 4.4 %collective-permute-start.15 = (bf16[160,128]{1,0:T(8,128)(2,1)S(1)}, bf16[160,128]{1,0:T(8,128)(2,1)S(1)}, u32[]{:S(2)}, u32[]{:S(2)}) collective-permute-start(bf16[160,128]{1,0:T(8,128)(2,1)S(1)} %get-tuple-element.69), channel_id=1, source_target_pairs={{0,4},{1,5},{2,6},{3,7},{4,0},{5,1},{6,2},{7,3},{8,12},{9,13},{10,... | collective-permute-start | bytes 122888 | tf_op jit(solution)/shard_map/ppermute | solution.py:553
  82.1 4.3 %collective-permute-start.8 = (bf16[224,128]{1,0:T(8,128)(2,1)S(1)}, bf16[224,128]{1,0:T(8,128)(2,1)S(1)}, u32[]{:S(2)}, u32[]{:S(2)}) collective-permute-start(bf16[224,128]{1,0:T(8,128)(2,1)S(1)} %get-tuple-element.89), channel_id=1, source_target_pairs={{0,32},{32,64},{64,96},{96,0},{1,33},{33,65},{65,97},{97,1},{2,34}... | collective-permute-start | bytes 172040 | tf_op jit(solution)/shard_map/ppermute | solution.py:553
  82.8 4.7 %collective-permute-start.9 = (bf16[224,128]{1,0:T(8,128)(2,1)S(1)}, bf16[224,128]{1,0:T(8,128)(2,1)S(1)}, u32[]{:S(2)}, u32[]{:S(2)}) collective-permute-start(bf16[224,128]{1,0:T(8,128)(2,1)S(1)} %get-tuple-element.90), channel_id=1, source_target_pairs={{0,64},{32,96},{64,0},{96,32},{1,65},{33,97},{65,1},{97,33},{2,66}... | collective-permute-start | bytes 172040 | tf_op jit(solution)/shard_map/ppermute | solution.py:553
  87.8 5.3 %collective-permute-start.17 = (bf16[144,128]{1,0:T(8,128)(2,1)S(1)}, bf16[144,128]{1,0:T(8,128)(2,1)S(1)}, u32[]{:S(2)}, u32[]{:S(2)}) collective-permute-start(bf16[144,128]{1,0:T(8,128)(2,1)S(1)} %get-tuple-element.86), channel_id=1, source_target_pairs={{0,8},{8,16},{16,24},{24,0},{1,9},{9,17},{17,25},{25,1},{2,10},{10... | collective-permute-start | bytes 110600 | tf_op jit(solution)/shard_map/ppermute | solution.py:553
  89.3 4.3 %collective-permute-start.18 = (bf16[144,128]{1,0:T(8,128)(2,1)S(1)}, bf16[144,128]{1,0:T(8,128)(2,1)S(1)}, u32[]{:S(2)}, u32[]{:S(2)}) collective-permute-start(bf16[144,128]{1,0:T(8,128)(2,1)S(1)} %get-tuple-element.87), channel_id=1, source_target_pairs={{0,16},{8,24},{16,0},{24,8},{1,17},{9,25},{17,1},{25,9},{2,18},{10... | collective-permute-start | bytes 110600 | tf_op jit(solution)/shard_map/ppermute | solution.py:553
  94.1 4.7 %collective-permute-start.20 = (bf16[80,128]{1,0:T(8,128)(2,1)S(1)}, bf16[80,128]{1,0:T(8,128)(2,1)S(1)}, u32[]{:S(2)}, u32[]{:S(2)}) collective-permute-start(bf16[80,128]{1,0:T(8,128)(2,1)S(1)} %get-tuple-element.50), channel_id=1, source_target_pairs={{0,8},{8,16},{16,24},{24,0},{1,9},{9,17},{17,25},{25,1},{2,10},{10... | collective-permute-start | bytes 61448 | tf_op jit(solution)/shard_map/ppermute | solution.py:553
  95.1 4.7 %collective-permute-start.21 = (bf16[80,128]{1,0:T(8,128)(2,1)S(1)}, bf16[80,128]{1,0:T(8,128)(2,1)S(1)}, u32[]{:S(2)}, u32[]{:S(2)}) collective-permute-start(bf16[80,128]{1,0:T(8,128)(2,1)S(1)} %get-tuple-element.50), channel_id=1, source_target_pairs={{0,16},{8,24},{16,0},{24,8},{1,17},{9,25},{17,1},{25,9},{2,18},{10... | collective-permute-start | bytes 61448 | tf_op jit(solution)/shard_map/ppermute | solution.py:553
  101.0 16.9 %collective-permute-start.31 = (bf16[160,128]{1,0:T(8,128)(2,1)S(1)}, bf16[160,128]{1,0:T(8,128)(2,1)S(1)}, u32[]{:S(2)}, u32[]{:S(2)}) collective-permute-start(bf16[160,128]{1,0:T(8,128)(2,1)S(1)} %bitcast.151), channel_id=1, source_target_pairs={{0,6},{1,7},{2,0},{3,1},{4,2},{5,3},{6,4},{7,5},{8,14},{9,15},{10,... | collective-permute-start | bytes 122888 | tf_op jit(solution)/shard_map/ppermute | solution.py:553
  102.4 15.5 %collective-permute-start.30 = (bf16[160,128]{1,0:T(8,128)(2,1)S(1)}, bf16[160,128]{1,0:T(8,128)(2,1)S(1)}, u32[]{:S(2)}, u32[]{:S(2)}) collective-permute-start(bf16[160,128]{1,0:T(8,128)(2,1)S(1)} %bitcast.152), channel_id=1, source_target_pairs={{0,4},{1,5},{2,6},{3,7},{4,0},{5,1},{6,2},{7,3},{8,12},{9,13},{10,... | collective-permute-start | bytes 122888 | tf_op jit(solution)/shard_map/ppermute | solution.py:553
  103.5 14.2 %collective-permute-start.29 = (bf16[160,128]{1,0:T(8,128)(2,1)S(1)}, bf16[160,128]{1,0:T(8,128)(2,1)S(1)}, u32[]{:S(2)}, u32[]{:S(2)}) collective-permute-start(bf16[160,128]{1,0:T(8,128)(2,1)S(1)} %bitcast.153), channel_id=1, source_target_pairs={{0,2},{1,3},{2,4},{3,5},{4,6},{5,7},{6,0},{7,1},{8,10},{9,11},{10,... | collective-permute-start | bytes 122888 | tf_op jit(solution)/shard_map/ppermute | solution.py:553
  103.8 10.8 %collective-permute-start.25 = (bf16[160,128]{1,0:T(8,128)(2,1)S(1)}, bf16[160,128]{1,0:T(8,128)(2,1)S(1)}, u32[]{:S(2)}, u32[]{:S(2)}) collective-permute-start(bf16[160,128]{1,0:T(8,128)(2,1)S(1)} %bitcast.155), channel_id=1, source_target_pairs={{0,96},{32,0},{64,32},{96,64},{1,97},{33,1},{65,33},{97,65},{2,98}... | collective-permute-start | bytes 122888 | tf_op jit(solution)/shard_map/ppermute | solution.py:553
  106.2 4.1 %collective-permute-start.23 = (bf16[160,128]{1,0:T(8,128)(2,1)S(1)}, bf16[160,128]{1,0:T(8,128)(2,1)S(1)}, u32[]{:S(2)}, u32[]{:S(2)}) collective-permute-start(bf16[160,128]{1,0:T(8,128)(2,1)S(1)} %bitcast.156), channel_id=1, source_target_pairs={{0,32},{32,64},{64,96},{96,0},{1,33},{33,65},{65,97},{97,1},{2,34}... | collective-permute-start | bytes 122888 | tf_op jit(solution)/shard_map/ppermute | solution.py:553
  110.2 4.4 %collective-permute-start.24 = (bf16[160,128]{1,0:T(8,128)(2,1)S(1)}, bf16[160,128]{1,0:T(8,128)(2,1)S(1)}, u32[]{:S(2)}, u32[]{:S(2)}) collective-permute-start(bf16[160,128]{1,0:T(8,128)(2,1)S(1)} %bitcast.158), channel_id=1, source_target_pairs={{0,64},{32,96},{64,0},{96,32},{1,65},{33,97},{65,1},{97,33},{2,66}... | collective-permute-start | bytes 122888 | tf_op jit(solution)/shard_map/ppermute | solution.py:553
  114.6 9.7 %collective-permute-start.28 = (bf16[640,128]{1,0:T(8,128)(2,1)S(1)}, bf16[640,128]{1,0:T(8,128)(2,1)S(1)}, u32[]{:S(2)}, u32[]{:S(2)}) collective-permute-start(bf16[640,128]{1,0:T(8,128)(2,1)S(1)} %bitcast.131), channel_id=1, source_target_pairs={{0,6},{1,7},{2,0},{3,1},{4,2},{5,3},{6,4},{7,5},{8,14},{9,15},{10,... | collective-permute-start | bytes 491528 | tf_op jit(solution)/shard_map/ppermute | solution.py:553
  116.8 7.5 %collective-permute-start.27 = (bf16[640,128]{1,0:T(8,128)(2,1)S(1)}, bf16[640,128]{1,0:T(8,128)(2,1)S(1)}, u32[]{:S(2)}, u32[]{:S(2)}) collective-permute-start(bf16[640,128]{1,0:T(8,128)(2,1)S(1)} %bitcast.132), channel_id=1, source_target_pairs={{0,4},{1,5},{2,6},{3,7},{4,0},{5,1},{6,2},{7,3},{8,12},{9,13},{10,... | collective-permute-start | bytes 491528 | tf_op jit(solution)/shard_map/ppermute | solution.py:553
  117.7 6.6 %collective-permute-start.26 = (bf16[640,128]{1,0:T(8,128)(2,1)S(1)}, bf16[640,128]{1,0:T(8,128)(2,1)S(1)}, u32[]{:S(2)}, u32[]{:S(2)}) collective-permute-start(bf16[640,128]{1,0:T(8,128)(2,1)S(1)} %bitcast.133), channel_id=1, source_target_pairs={{0,2},{1,3},{2,4},{3,5},{4,6},{5,7},{6,0},{7,1},{8,10},{9,11},{10,... | collective-permute-start | bytes 491528 | tf_op jit(solution)/shard_map/ppermute | solution.py:553
  118.0 11.8 %collective-permute-start.34 = (bf16[640,128]{1,0:T(8,128)(2,1)S(1)}, bf16[640,128]{1,0:T(8,128)(2,1)S(1)}, u32[]{:S(2)}, u32[]{:S(2)}) collective-permute-start(bf16[640,128]{1,0:T(8,128)(2,1)S(1)} %bitcast.135), channel_id=1, source_target_pairs={{0,96},{32,0},{64,32},{96,64},{1,97},{33,1},{65,33},{97,65},{2,98}... | collective-permute-start | bytes 491528 | tf_op jit(solution)/shard_map/ppermute | solution.py:553
  118.0 11.6 %collective-permute-start.33 = (bf16[640,128]{1,0:T(8,128)(2,1)S(1)}, bf16[640,128]{1,0:T(8,128)(2,1)S(1)}, u32[]{:S(2)}, u32[]{:S(2)}) collective-permute-start(bf16[640,128]{1,0:T(8,128)(2,1)S(1)} %bitcast.136), channel_id=1, source_target_pairs={{0,64},{32,96},{64,0},{96,32},{1,65},{33,97},{65,1},{97,33},{2,66}... | collective-permute-start | bytes 491528 | tf_op jit(solution)/shard_map/ppermute | solution.py:553
  124.3 5.4 %collective-permute-start.32 = (bf16[640,128]{1,0:T(8,128)(2,1)S(1)}, bf16[640,128]{1,0:T(8,128)(2,1)S(1)}, u32[]{:S(2)}, u32[]{:S(2)}) collective-permute-start(bf16[640,128]{1,0:T(8,128)(2,1)S(1)} %bitcast.138), channel_id=1, source_target_pairs={{0,32},{32,64},{64,96},{96,0},{1,33},{33,65},{65,97},{97,1},{2,34}... | collective-permute-start | bytes 491528 | tf_op jit(solution)/shard_map/ppermute | solution.py:553
  130.9 20.7 %collective-permute-start.35 = (bf16[5120,128]{1,0:T(8,128)(2,1)}, bf16[5120,128]{1,0:T(8,128)(2,1)S(1)}, u32[]{:S(2)}, u32[]{:S(2)}) collective-permute-start(bf16[5120,128]{1,0:T(8,128)(2,1)} %pad_maximum_fusion.1), channel_id=1, source_target_pairs={{0,1},{1,0},{2,3},{3,2},{4,5},{5,4},{6,7},{7,6},{8,9},{9,8},{10,11... | collective-permute-start | bytes 3932168 | tf_op jit(solution)/shard_map/ppermute | solution.py:598
  (17 other events, 54.6 us)

commit v2 on v1

--- a/solution.py
+++ b/solution.py
@@ -107,20 +107,22 @@
         for c in range(cb1):
             put(ROWS + n * step, step, x_ref[pl.ds(n * step, step), :, lanes(c)], c)
 
+    def put_sides(row, count, right, left, c):
+        at = pl.ds(row, count)
+        right, left = right.astype(F32), left.astype(F32)
+        xf[c, at, 8 + cols : 16 + cols, :] = right
+        xf[c, at, 16 + cols : 24 + cols, :] = left
+        xf[c, at, 7:8, :] = left[:, 7:8, :]
+        xf[c, at, 24 + cols : 25 + cols, :] = xf[c, at, 8:9, :]
+
     @pl.loop(0, (rows + 2 * ROWS) // step)
     def _(n):
         at = pl.ds(n * step, step)
         for c in range(cb1):
-            right = right_ref[at, :, lanes(c)].astype(F32)
-            left = left_ref[at, :, lanes(c)].astype(F32)
-            xf[c, at, 8 + cols : 16 + cols, :] = right
-            xf[c, at, 16 + cols : 24 + cols, :] = left
-            xf[c, at, 7:8, :] = left[:, 7:8, :]
-            xf[c, at, 24 + cols : 25 + cols, :] = xf[c, at, 8:9, :]
+            put_sides(n * step, step, right_ref[at, :, lanes(c)], left_ref[at, :, lanes(c)], c)
 
     def diff(first, count, block, c):
-        e = 2 * first + ROWS
-        at = pl.ds(e, 2 * count)
+        at = pl.ds(2 * first + ROWS, 2 * count)
         tf[c, 0 : 2 * count, cols - 5 : cols + 3, :] = right_ref[at, :, lanes(c)].astype(F32)
         tf[c, 0 : 2 * count, cols + 13 : cols + 21, :] = left_ref[at, :, lanes(c)].astype(F32)
         tf[c, 0 : 2 * count, 0:cols, :] = block.astype(F32)
@@ -336,7 +338,7 @@
     return pl.BlockSpec(memory_space=pltpu.SMEM)
 
 
-def tile_step(limits, x, t, top, bot, right, left, k1, p1, taps, k2, p2):
+def tile_step(limits, x, t, halos, k1, p1, taps, k2, p2):
     rows, cols, chan = x.shape
     hid = k2.shape[2]
     hr, hc = rows // 2, cols // 2
@@ -350,7 +352,7 @@
             jax.ShapeDtypeStruct((grads, LANES), BF16),
             jax.ShapeDtypeStruct((grads, LANES), BF16),
         ),
-        in_specs=[smem()] + [vmem()] * 11,
+        in_specs=[smem()] + [vmem()] * (7 + len(halos)),
         out_specs=[vmem()] * 3,
         scratch_shapes=[
             pltpu.VMEM((cb1, rows + 2 * ROWS, cols + 32, LANES), F32),
@@ -371,61 +373,80 @@
         ],
         compiler_params=pltpu.CompilerParams(vmem_limit_bytes=63 * 1024 * 1024),
         cost_estimate=pl.CostEstimate(flops=9_000_000_000, bytes_accessed=20_000_000, transcendentals=0),
-    )(limits, x, t, top, bot, right, left, k1, p1, taps, k2, p2)
-
-
-def norm_kernel(p1_ref, st_ref, p2_ref, k1_ref, k2_ref, out_ref):
-    @pl.when(pl.program_id(0) == 0)
+    )(limits, x, t, *halos, k1, p1, taps, k2, p2)
+
+
+def prepare_kernel(p1_ref, st_ref, p2_ref, k1_ref, k2_ref, lp1_ref, lst_ref, lp2_ref, out_ref, acc):
+    step = pl.program_id(0)
+
+    @pl.when(step == 0)
     def _():
         for j, ref in ((0, k1_ref), (1, p1_ref), (3, k2_ref), (4, p2_ref)):
             out_ref[j] = jnp.sum(ref[...] * ref[...])
-        out_ref[2] = 0.0
-
-    out_ref[2] += jnp.sum(st_ref[...] * st_ref[...])
-
-
-def norms(k1, p1, taps, k2, p2):
-    parts = taps.shape[0]
+        lp1_ref[...] = p1_ref[...].astype(BF16)
+        lp2_ref[...] = p2_ref[...].astype(BF16)
+        acc[...] = jnp.zeros_like(acc)
+
+    w = st_ref[0]
+    lst_ref[0] = w.astype(BF16)
+    acc[...] += jnp.sum((w * w).reshape(-1, 8, w.shape[1]), axis=0)
+
+    @pl.when(step == pl.num_programs(0) - 1)
+    def _():
+        out_ref[2] = jnp.sum(acc[...])
+
+
+def prepared(k1, p1, taps, k2, p2):
+    parts, hid = taps.shape[:2]
+    p1_spec = pl.BlockSpec(p1.shape, lambda n: (0, 0))
+    st_spec = pl.BlockSpec((1,) + taps.shape[1:], lambda n: (n, 0, 0))
+    p2_spec = pl.BlockSpec(p2.shape, lambda n: (0, 0))
     return pl.pallas_call(
-        norm_kernel,
+        prepare_kernel,
         grid=(parts,),
-        out_shape=jax.ShapeDtypeStruct((5,), F32),
+        out_shape=[jax.ShapeDtypeStruct(w.shape, BF16) for w in (p1, taps, p2)]
+        + [jax.ShapeDtypeStruct((5,), F32)],
         in_specs=[
-            pl.BlockSpec(p1.shape, lambda n: (0, 0)),
-            pl.BlockSpec((1,) + taps.shape[1:], lambda n: (n, 0, 0)),
-            pl.BlockSpec(p2.shape, lambda n: (0, 0)),
+            p1_spec,
+            st_spec,
+            p2_spec,
             pl.BlockSpec(k1.shape, lambda n: (0, 0, 0)),
             pl.BlockSpec(k2.shape, lambda n: (0, 0, 0)),
         ],
-        out_specs=smem(),
-        cost_estimate=pl.CostEstimate(flops=3_000_000, bytes_accessed=5_300_000, transcendentals=0),
+        out_specs=[p1_spec, st_spec, p2_spec, smem()],
+        scratch_shapes=[pltpu.VMEM((8, hid), F32)],
+        cost_estimate=pl.CostEstimate(flops=3_000_000, bytes_accessed=8_000_000, transcendentals=0),
     )(p1, taps, p2, k1, k2)
 
 
 def update_kernel(
     where,
     sums,
+    small_ref,
     own_ref,
     other_ref,
-    k1_ref,
-    p1_ref,
-    st_ref,
-    k2_ref,
-    p2_ref,
-    nk1_ref,
-    np1_ref,
-    nst_ref,
-    nk2_ref,
-    np2_ref,
-    sk1_ref,
-    sp1_ref,
-    sst_ref,
-    sk2_ref,
-    sp2_ref,
-    g,
-    small,
-    scale,
+    *refs,
 ):
+    (
+        k1_ref,
+        p1_ref,
+        st_ref,
+        k2_ref,
+        p2_ref,
+        nk1_ref,
+        np1_ref,
+        nst_ref,
+        nk2_ref,
+        np2_ref,
+        sk1_ref,
+        sp1_ref,
+        sst_ref,
+        sk2_ref,
+        sp2_ref,
+        g,
+        small,
+        scale,
+    ) = refs
     chan, hid = p1_ref.shape
     cb1, cb2 = chan // LANES, hid // LANES
     parts, block = 4, st_ref.shape[1]
@@ -460,9 +481,9 @@
 
     @pl.when(step == 0)
     def _():
-        g[core] = own_ref[0:small_at, :]
+        g[core] = own_ref[...]
         g[1 - core] = other_ref[...]
-        small[...] = own_ref[small_at : small_at + SMALL, :].astype(F32)
+        small[...] = small_ref[...].astype(F32)
         v = small[0 : 9 * cb1, :]
         set_scale(0, jnp.sum(v * v))
         v = small[9 * cb1 : 9 * (cb1 + cb2), :]
@@ -504,9 +525,9 @@
         nst_ref[0, :, cut] = st_ref[0, :, cut] - scale[7] * normed
 
 
-def update(where, sums, own, other, k1, p1, taps, k2, p2):
+def update(where, sums, small, own, other, k1, p1, taps, k2, p2):
     hid = taps.shape[1]
-    block = hid // 4
+    block = hid // 2
     per = hid // block
 
     def whole(w):
@@ -519,38 +540,54 @@
         update_kernel,
         grid=(4 * per,),
         out_shape=shapes + shapes,
-        in_specs=[smem(), smem(), whole(own), whole(other)] + specs,
+        in_specs=[smem(), smem(), whole(small)] + [whole(own), whole(other)] + specs,
         out_specs=specs + specs,
         scratch_shapes=[
-            pltpu.VMEM((2,) + other.shape, BF16),
+            pltpu.VMEM((2,) + own.shape, BF16),
             pltpu.VMEM((SMALL, LANES), F32),
             pltpu.SMEM((10,), F32),
         ],
         compiler_params=pltpu.CompilerParams(vmem_limit_bytes=40 * 1024 * 1024),
-    )(where, sums, own, other, k1, p1, taps, k2, p2)
-
-
-def shift(block, axis, step):
-    count = lax.axis_size(axis)
-    return lax.ppermute(
-        block, axis, [(i, i + step) for i in range(count) if 0 <= i + step < count]
-    )
+    )(where, sums, small, own, other, k1, p1, taps, k2, p2)
+
+
+def shift(block, down, right):
+    n, m = lax.axis_size("ty"), lax.axis_size("tx")
+    pairs = [
+        (i * m + j, (i + down) * m + j + right)
+        for i in range(n)
+        for j in range(m)
+        if 0 <= i + down < n and 0 <= j + right < m
+    ]
+    return lax.ppermute(block, ("ty", "tx"), pairs)
 
 
 class Ring:
-    def __init__(self, name):
-        axis = {"x": "tx", "y": "rep", "z": "ty"}[name]
-        inner = 2 if name == "x" else 1
-        self.axis, self.inner = axis, inner
-        self.count = lax.axis_size(axis) // inner
-        self.me = lax.axis_index(axis) // inner
+    def __init__(self, names):
+        sizes = {"x": lax.axis_size("tx") // 2, "y": lax.axis_size("rep"), "z": lax.axis_size("ty")}
+        place = {"x": lax.axis_index("tx") // 2, "y": lax.axis_index("rep"), "z": lax.axis_index("ty")}
+        self.names, self.sizes = names, sizes
+        self.count = sizes[names[0]]
+        assert sizes[names[1]] == self.count
+        self.me = jnp.where(lax.axis_index("tx") % 2 == 0, place[names[0]], place[names[1]])
 
     def send(self, block, step):
-        n, inner = self.count, self.inner
-        pairs = [
-            (i * inner + k, (i + step) % n * inner + k) for i in range(n) for k in range(inner)
-        ]
-        return lax.ppermute(block, self.axis, pairs)
+        sizes = self.sizes
+
+        def flat(at, core):
+            return ((at["y"] * sizes["z"] + at["z"]) * sizes["x"] + at["x"]) * 2 + core
+
+        pairs = []
+        for i in range(sizes["y"]):
+            for j in range(sizes["z"]):
+                for k in range(sizes["x"]):
+                    for core in range(2):
+                        at = {"y": i, "z": j, "x": k}
+                        to = dict(at)
+                        name = self.names[core]
+                        to[name] = (at[name] + step) % sizes[name]
+                        pairs.append((flat(at, core), flat(to, core)))
+        return lax.ppermute(block, ("rep", "ty", "tx"), pairs)
 
     def scatter(self, block, extra):
         n = self.count
@@ -560,13 +597,10 @@
         got = []
         for d in range(1, n):
             out = lax.dynamic_index_in_dim(shares, (self.me + d) % n, 0, False)
-            if extra is not None:
-                out = jnp.concatenate([out, extra], axis=0)
-            got.append(self.send(out, d))
-        total = sum([g[:cut].astype(F32) for g in got], share.astype(F32)).astype(BF16)
-        if extra is not None:
-            extra = sum([g[cut:].astype(F32) for g in got], extra.astype(F32)).astype(BF16)
-        return total, extra
+            got.append(self.send(jnp.concatenate([out, extra], axis=0), d))
+        total = sum([g[:cut].astype(F32) for g in got], share.astype(F32))
+        extra = sum([g[cut:].astype(F32) for g in got], extra.astype(F32))
+        return total.astype(BF16), extra.astype(BF16)
 
     def gather(self, share):
         n = self.count
@@ -579,24 +613,16 @@
 
 
 def reduced(keep, send):
-    x, y, z = Ring("x"), Ring("y"), Ring("z")
+    rings = (Ring("yx"), Ring("xy"), Ring("zz"))
     cores = [(i, i ^ 1) for i in range(lax.axis_size("tx"))]
     got = lax.ppermute(send, "tx", cores)
     both = (keep.astype(F32) + got.astype(F32)).astype(BF16)
-    size = both.shape[0] - SMALL
-    first, second, small = both[: size // 2], both[size // 2 : size], both[size:]
-    first, small = x.scatter(first, small)
-    second, _ = y.scatter(second, None)
-    first, small = y.scatter(first, small)
-    second, _ = x.scatter(second, None)
-    share, small = z.scatter(jnp.concatenate([first, second], axis=0), small)
-    both = z.gather(share)
-    size = both.shape[0]
-    first, second = y.gather(both[: size // 2]), x.gather(both[size // 2 :])
-    first, second = x.gather(first), y.gather(second)
-    half = jnp.concatenate([first, second], axis=0)
-    other = lax.ppermute(half, "tx", cores)
-    return jnp.concatenate([half, small], axis=0), other
+    share, small = both[: both.shape[0] - SMALL], both[both.shape[0] - SMALL :]
+    for ring in rings:
+        share, small = ring.scatter(share, small)
+    for ring in rings[::-1]:
+        share = ring.gather(share)
+    return small, share, lax.ppermute(share, "tx", cores)
 
 
 def per_device(inputs, targets, kern_one, point_one, coarsening_taps, kern_two, point_two):
@@ -605,8 +631,13 @@
     rows, cols, chan = x.shape
     hid = point_one.shape[1]
     hr, hc = rows // 2, cols // 2
-    top = shift(jnp.concatenate([x[rows - ROWS :], t[rows - 2 :]], axis=0), "ty", 1)
-    bot = shift(jnp.concatenate([x[:ROWS], t[:2]], axis=0), "ty", -1)
+    up = jnp.concatenate([x[:ROWS], t[:2]], axis=0)
+    down = jnp.concatenate([x[rows - ROWS :], t[rows - 2 :]], axis=0)
+    top, bot = shift(down, 1, 0), shift(up, -1, 0)
+    taps = coarsening_taps.reshape(4, hid, hid)
+    weights = (kern_one, point_one, taps, kern_two, point_two)
+    weights, top, bot = lax.optimization_barrier((weights, top, bot))
+    low_one, low_taps, low_two, sums = prepared(*weights)
 
     def edge(cut):
         e = jnp.concatenate([top[:ROWS, cut], x[:, cut], bot[:ROWS, cut]], axis=0)
@@ -615,9 +646,10 @@
         return e, f
 
     e, f = edge(slice(0, 8))
-    right = shift(jnp.concatenate([e[:, :5], f[:, :2], e[:, 7:]], axis=1), "tx", -1)
+    right = shift(jnp.concatenate([e[:, :5], f[:, :2], e[:, 7:]], axis=1), 0, -1)
     e, f = edge(slice(cols - 8, cols))
-    left = shift(jnp.concatenate([e[:, :1], f[:, 6:], e[:, 3:]], axis=1), "tx", 1)
+    left = shift(jnp.concatenate([e[:, :1], f[:, 6:], e[:, 3:]], axis=1), 0, 1)
+    halos = [top, bot, right, left]
     ty, tx = lax.axis_index("ty"), lax.axis_index("tx")
     big = 1 << 20
     limits = jnp.stack(
@@ -629,25 +661,11 @@
             tx % 2,
         ]
     ).astype(jnp.int32)
-    taps = coarsening_taps.reshape(4, hid, hid)
     pred, keep, send = tile_step(
-        limits,
-        x,
-        t,
-        top,
-        bot,
-        right,
-        left,
-        kern_one,
-        point_one.astype(BF16),
-        taps.astype(BF16),
-        kern_two,
-        point_two.astype(BF16),
+        limits, x, t, halos, kern_one, low_one, low_taps, kern_two, low_two
     )
-    weights, send = lax.optimization_barrier(((kern_one, point_one, taps, kern_two, point_two), send))
-    sums = norms(*weights)
-    own, other = reduced(keep, send)
-    outs = update((tx % 2)[None].astype(jnp.int32), sums, own, other, *weights)
+    small, own, other = reduced(keep, send)
+    outs = update((tx % 2)[None].astype(jnp.int32), sums, small, own, other, *weights)
     outs = [o.reshape(coarsening_taps.shape) if o.shape == taps.shape else o for o in outs]
     return (jnp.transpose(pred, (2, 0, 1))[None], *outs)
 

time: 166 us -> 145 us (0.87)
  starting transfers between devices: 62.9 us -> 46.9 us
  waiting for transfers between devices: 34.2 us -> 38.1 us
  other arithmetic: 9.21 us -> 5.47 us
  local copies, waits for them, and re-layouts: 9.48 us -> 5.8 us
  Pallas kernels: 48.8 us -> 46.9 us
    ppermute x35 -> x23, starting transfers between devices: 62.9 us -> 46.9 us  [the longest x18 25.2 us: send(): return lax.ppermute(block, ('rep', 'ty', 'tx'), pairs)]
    ppermute x35 -> x23, waiting for transfers between devices: 31 us -> 34.8 us  [the longest x18 28.4 us: send(): return lax.ppermute(block, ('rep', 'ty', 'tx'), pairs)]
    unnamed x30 -> x26, local copies, waits for them, and re-layouts: 4.83 us -> 1.24 us
    convert_element_type x10 -> x5, other arithmetic: 5.52 us -> 2.07 us  [scatter(): return (total.astype(BF16), extra.astype(BF16))]
    pallas_call x1, Pallas kernels: 11 us -> 8.73 us  [update(): pl.pallas_call(update_kernel, grid=(4 * per,), out_shape=shapes + shapes,...]
  transfers between devices with their start and end apart: 36 -> 24, of which waited for: 15 -> 14; matrix products, arithmetic and copies ran while one was open for 5% -> 2% of each run, Pallas kernels for 3% -> 4%
where the time goes in v2:
time: 145 us; the launch traced here: 144 us
  starting transfers between devices  46.9 us (32%)
  Pallas kernels  46.9 us (32%)
  waiting for transfers between devices  38.1 us (26%)
  local copies, waits for them, and re-layouts  5.8 us (4%)
  other arithmetic  5.47 us (4%)
    pallas_call x1, Pallas kernels, tile_step(): pl.pallas_call(tile_kernel, out_shape=(jax.ShapeDtypeStruct(x.shape, BF16...  33 us
    ppermute x18, waiting for transfers between devices, send(): return lax.ppermute(block, ('rep', 'ty', 'tx'), pairs)  28.4 us
    ppermute x18, starting transfers between devices, send(): return lax.ppermute(block, ('rep', 'ty', 'tx'), pairs)  25.2 us
    ppermute x4, starting transfers between devices, shift(): return lax.ppermute(block, ('ty', 'tx'), pairs)  12.3 us
    ppermute x1, starting transfers between devices, reduced(): return (small, share, lax.ppermute(share, 'tx', cores))  9.49 us
    pallas_call x1, Pallas kernels, update(): pl.pallas_call(update_kernel, grid=(4 * per,), out_shape=shapes + shapes,...  8.73 us
    pallas_call x1, Pallas kernels, prepared(): pl.pallas_call(prepare_kernel, grid=(parts,), out_shape=[jax.ShapeDtypeSt...  5.18 us
    ppermute x4, waiting for transfers between devices, shift(): return lax.ppermute(block, ('ty', 'tx'), pairs)  3.81 us
  transfers between devices with their start and end apart: 24, of which 14 were waited for; matrix products, arithmetic and copies ran while one was open for 2% of the time, Pallas kernels for 4%

profile of v2, /device:TPU:1, one launch (start us, length us, event | category | flops | bytes accessed | tf_op | source)
XLA Modules:
  0.0 144.3 jit_solution(149431381898307068)
XLA Ops:
  1.4 1.1 fusion.29
  2.5 4.4 %collective-permute-start = (bf16[8,32,256]{2,1,0:T(8,128)(2,1)S(1)}, bf16[8,32,256]{2,1,0:T(8,128)(2,1)S(1)}, u32[]{:S(2)}, u32[]{:S(2)}) collective-permute-start(bf16[8,32,256]{2,1,0:T(8,128)(2,1)S(1)} %pad_maximum_fusion.8), channel_id=1, source_target_pairs={{0,8},{1,9},{2,10},{3,11},{4,12},{5,13},{6,14},{7,15},{8,16},{9,17... | collective-permute-start | bytes 393224 | tf_op jit(solution)/shard_map/ppermute | solution.py:562
  6.9 1.3 collective-permute-start.1
  8.2 1.2 fusion.28
  9.4 3.8 %collective-permute-done.1.bot_ref = bf16[8,32,256]{2,1,0:T(8,128)(2,1)S(1)} collective-permute-done((bf16[8,32,256]{2,1,0:T(8,128)(2,1)S(1)}, bf16[8,32,256]{2,1,0:T(8,128)(2,1)S(1)}, u32[]{:S(2)}, u32[]{:S(2)}) %collective-permute-start.1) | collective-permute-done | bytes 131104 | tf_op jit(solution)/shard_map/ppermute | solution.py:562
  14.2 3.6 %collective-permute-start.2 = (bf16[108,8,256]{2,1,0:T(8,128)(2,1)S(1)}, bf16[108,8,256]{2,1,0:T(8,128)(2,1)S(1)}, u32[]{:S(2)}, u32[]{:S(2)}) collective-permute-start(bf16[108,8,256]{2,1,0:T(8,128)(2,1)S(1)} %fusion.14), channel_id=1, source_target_pairs={{1,0},{2,1},{3,2},{4,3},{5,4},{6,5},{7,6},{9,8},{10,9},{11,10},{12... | collective-permute-start | bytes 1327112 | tf_op jit(solution)/shard_map/ppermute | solution.py:562
  18.1 3.0 %collective-permute-start.3 = (bf16[108,8,256]{2,1,0:T(8,128)(2,1)S(1)}, bf16[108,8,256]{2,1,0:T(8,128)(2,1)S(1)}, u32[]{:S(2)}, u32[]{:S(2)}) collective-permute-start(bf16[108,8,256]{2,1,0:T(8,128)(2,1)S(1)} %fusion.18), channel_id=1, source_target_pairs={{0,1},{1,2},{2,3},{3,4},{4,5},{5,6},{6,7},{8,9},{9,10},{10,11},{11... | collective-permute-start | bytes 1327112 | tf_op jit(solution)/shard_map/ppermute | solution.py:562
  21.8 5.2 %shard_map.158 = (bf16[256,512]{1,0:T(8,128)(2,1)}, bf16[4,512,512]{2,1,0:T(8,128)(2,1)}, bf16[512,256]{1,0:T(8,128)(2,1)}, f32[5]{0:T(128)}) custom-call(f32[256,512]{1,0:T(8,128)} %refs_1_, f32[4,512,512]{2,1,0:T(8,128)} %bitcast.78, f32[512,256]{1,0:T(8,128)} %refs_4_, f32[3,3,256]{2,1,0:T(4,128)} %refs_0_, f32[3,3,512]{2,1,0:T(4,128)} %refs_3_), custom_call_target="tpu_custom_call" | custom-call | flops 3000000 | bytes 8000000 | tf_op jit(solution)/shard_map/pallas_call | solution.py:404
  27.9 33.0 %shard_map.159 = (bf16[96,32,256]{2,1,0:T(8,128)(2,1)}, bf16[5184,128]{1,0:T(8,128)(2,1)}, bf16[5184,128]{1,0:T(8,128)(2,1)}) custom-call(s32[5]{0:T(128)} %stack.23.limits, bf16[96,32,256]{2,1,0:T(8,128)(2,1)} %bitcast.93, bf16[96,32,256]{2,1,0:T(8,128)(2,1)} %bitcast.95, bf16[8,32,256]{2,1,0:T(8,128)(2,1)} %copy-done.7, bf16[8,32,256]{2,1,0:T(8,128)(2,1)} %copy-done.8, ...), custom_call_target="tpu_custom_call" | custom-call | flops 8999999488 | bytes 20000000 | tf_op jit(solution)/shard_map/pallas_call | solution.py:348
  60.9 3.3 %collective-permute-done.4 = bf16[5184,128]{1,0:T(8,128)(2,1)S(1)} collective-permute-done((bf16[5184,128]{1,0:T(8,128)(2,1)}, bf16[5184,128]{1,0:T(8,128)(2,1)S(1)}, u32[]{:S(2)}, u32[]{:S(2)}) %collective-permute-start.4) | collective-permute-done | bytes 1327136 | tf_op jit(solution)/shard_map/ppermute | solution.py:618
  64.1 1.7 %add_convert_fusion = bf16[5184,128]{1,0:T(8,128)(2,1)S(1)} fusion(bf16[5184,128]{1,0:T(8,128)(2,1)S(1)} %collective-permute-done.4, bf16[5184,128]{1,0:T(8,128)(2,1)} %get-tuple-element.47), kind=kLoop, calls=%fused_computation | loop fusion | flops 2654208 | bytes 3981312 | tf_op jit(solution)/shard_map/convert_element_type | solution.py:619
  67.0 1.5 %collective-permute-start.5 = (bf16[1344,128]{1,0:T(8,128)(2,1)}, bf16[1344,128]{1,0:T(8,128)(2,1)S(1)}, u32[]{:S(2)}, u32[]{:S(2)}) collective-permute-start(bf16[1344,128]{1,0:T(8,128)(2,1)} %get-tuple-element.92), channel_id=1, source_target_pairs={{0,32},{1,3},{2,34},{3,5},{4,36},{5,7},{6,38},{7,1},{8,40},{9,11},... | collective-permute-start | bytes 1032200 | tf_op jit(solution)/shard_map/ppermute | solution.py:590
  68.4 1.3 collective-permute-start.7
  69.7 1.7 %collective-permute-start.6 = (bf16[1344,128]{1,0:T(8,128)(2,1)}, bf16[1344,128]{1,0:T(8,128)(2,1)}, u32[]{:S(2)}, u32[]{:S(2)}) collective-permute-start(bf16[1344,128]{1,0:T(8,128)(2,1)} %get-tuple-element.94), channel_id=1, source_target_pairs={{0,64},{1,5},{2,66},{3,7},{4,68},{5,1},{6,70},{7,3},{8,72},{9,13},... | collective-permute-start | bytes 1032200 | tf_op jit(solution)/shard_map/ppermute | solution.py:590
  71.4 3.4 %collective-permute-done.5 = bf16[1344,128]{1,0:T(8,128)(2,1)S(1)} collective-permute-done((bf16[1344,128]{1,0:T(8,128)(2,1)}, bf16[1344,128]{1,0:T(8,128)(2,1)S(1)}, u32[]{:S(2)}, u32[]{:S(2)}) %collective-permute-start.5) | collective-permute-done | bytes 344096 | tf_op jit(solution)/shard_map/ppermute | solution.py:590
  75.1 4.7 %collective-permute-done.6 = bf16[1344,128]{1,0:T(8,128)(2,1)} collective-permute-done((bf16[1344,128]{1,0:T(8,128)(2,1)}, bf16[1344,128]{1,0:T(8,128)(2,1)}, u32[]{:S(2)}, u32[]{:S(2)}) %collective-permute-start.6) | collective-permute-done | bytes 344096 | tf_op jit(solution)/shard_map/ppermute | solution.py:590
  79.8 1.2 fusion.11
  83.0 2.6 %collective-permute-start.9 = (bf16[384,128]{1,0:T(8,128)(2,1)S(1)}, bf16[384,128]{1,0:T(8,128)(2,1)S(1)}, u32[]{:S(2)}, u32[]{:S(2)}) collective-permute-start(bf16[384,128]{1,0:T(8,128)(2,1)S(1)} %get-tuple-element.90), channel_id=1, source_target_pairs={{0,4},{1,65},{2,6},{3,67},{4,0},{5,69},{6,2},{7,71},{8,12},{9,73},... | collective-permute-start | bytes 294920 | tf_op jit(solution)/shard_map/ppermute | solution.py:590
  86.7 2.0 %collective-permute-done.9 = bf16[384,128]{1,0:T(8,128)(2,1)S(1)} collective-permute-done((bf16[384,128]{1,0:T(8,128)(2,1)S(1)}, bf16[384,128]{1,0:T(8,128)(2,1)S(1)}, u32[]{:S(2)}, u32[]{:S(2)}) %collective-permute-start.9) | collective-permute-done | bytes 98336 | tf_op jit(solution)/shard_map/ppermute | solution.py:590
  89.2 1.5 %collective-permute-start.11 = (bf16[144,128]{1,0:T(8,128)(2,1)S(1)}, bf16[144,128]{1,0:T(8,128)(2,1)S(1)}, u32[]{:S(2)}, u32[]{:S(2)}) collective-permute-start(bf16[144,128]{1,0:T(8,128)(2,1)S(1)} %get-tuple-element.86), channel_id=1, source_target_pairs={{0,8},{1,9},{2,10},{3,11},{4,12},{5,13},{6,14},{7,15},{8,16},{9,17... | collective-permute-start | bytes 110600 | tf_op jit(solution)/shard_map/ppermute | solution.py:590
  90.7 1.8 %collective-permute-start.12 = (bf16[144,128]{1,0:T(8,128)(2,1)S(1)}, bf16[144,128]{1,0:T(8,128)(2,1)S(1)}, u32[]{:S(2)}, u32[]{:S(2)}) collective-permute-start(bf16[144,128]{1,0:T(8,128)(2,1)S(1)} %get-tuple-element.87), channel_id=1, source_target_pairs={{0,16},{1,17},{2,18},{3,19},{4,20},{5,21},{6,22},{7,23},{8,24},{9,... | collective-permute-start | bytes 110600 | tf_op jit(solution)/shard_map/ppermute | solution.py:590
  92.5 2.0 %collective-permute-start.13 = (bf16[144,128]{1,0:T(8,128)(2,1)S(1)}, bf16[144,128]{1,0:T(8,128)(2,1)S(1)}, u32[]{:S(2)}, u32[]{:S(2)}) collective-permute-start(bf16[144,128]{1,0:T(8,128)(2,1)S(1)} %get-tuple-element.88), channel_id=1, source_target_pairs={{0,24},{1,25},{2,26},{3,27},{4,28},{5,29},{6,30},{7,31},{8,0},{9,1... | collective-permute-start | bytes 110600 | tf_op jit(solution)/shard_map/ppermute | solution.py:590
  96.5 3.3 %collective-permute-start.15 = (bf16[80,128]{1,0:T(8,128)(2,1)S(1)}, bf16[80,128]{1,0:T(8,128)(2,1)S(1)}, u32[]{:S(2)}, u32[]{:S(2)}) collective-permute-start(bf16[80,128]{1,0:T(8,128)(2,1)S(1)} %get-tuple-element.60), channel_id=1, source_target_pairs={{0,16},{1,17},{2,18},{3,19},{4,20},{5,21},{6,22},{7,23},{8,24},{9,... | collective-permute-start | bytes 61448 | tf_op jit(solution)/shard_map/ppermute | solution.py:590
  99.8 1.4 collective-permute-done.15
  101.2 1.2 collective-permute-done.16
  102.4 2.6 %collective-permute-start.19 = (bf16[320,128]{1,0:T(8,128)(2,1)S(1)}, bf16[320,128]{1,0:T(8,128)(2,1)S(1)}, u32[]{:S(2)}, u32[]{:S(2)}) collective-permute-start(bf16[320,128]{1,0:T(8,128)(2,1)S(1)} %bitcast.97), channel_id=1, source_target_pairs={{0,6},{1,97},{2,0},{3,99},{4,2},{5,101},{6,4},{7,103},{8,14},{9,10... | collective-permute-start | bytes 245768 | tf_op jit(solution)/shard_map/ppermute | solution.py:590
  106.2 4.4 %collective-permute-done.17 = bf16[320,128]{1,0:T(8,128)(2,1)S(1)} collective-permute-done((bf16[320,128]{1,0:T(8,128)(2,1)S(1)}, bf16[320,128]{1,0:T(8,128)(2,1)S(1)}, u32[]{:S(2)}, u32[]{:S(2)}) %collective-permute-start.17) | collective-permute-done | bytes 81952 | tf_op jit(solution)/shard_map/ppermute | solution.py:590
  111.4 2.1 %collective-permute-start.22 = (bf16[1280,128]{1,0:T(8,128)(2,1)S(1)}, bf16[1280,128]{1,0:T(8,128)(2,1)S(1)}, u32[]{:S(2)}, u32[]{:S(2)}) collective-permute-start(bf16[1280,128]{1,0:T(8,128)(2,1)S(1)} %bitcast.86), channel_id=1, source_target_pairs={{0,96},{1,7},{2,98},{3,1},{4,100},{5,3},{6,102},{7,5},{8,104},{9,1... | collective-permute-start | bytes 983048 | tf_op jit(solution)/shard_map/ppermute | solution.py:590
  113.8 9.5 %collective-permute-done.20 = bf16[1280,128]{1,0:T(8,128)(2,1)S(1)} collective-permute-done((bf16[1280,128]{1,0:T(8,128)(2,1)S(1)}, bf16[1280,128]{1,0:T(8,128)(2,1)S(1)}, u32[]{:S(2)}, u32[]{:S(2)}) %collective-permute-start.20) | collective-permute-done | bytes 327712 | tf_op jit(solution)/shard_map/ppermute | solution.py:590
  123.4 9.5 %collective-permute-start.23 = (bf16[5120,128]{1,0:T(8,128)(2,1)S(1)}, bf16[5120,128]{1,0:T(8,128)(2,1)S(1)}, u32[]{:S(2)}, u32[]{:S(2)}) collective-permute-start(bf16[5120,128]{1,0:T(8,128)(2,1)S(1)} %bitcast.80), channel_id=1, source_target_pairs={{0,1},{1,0},{2,3},{3,2},{4,5},{5,4},{6,7},{7,6},{8,9},{9,8},{10,11... | collective-permute-start | bytes 3932168 | tf_op jit(solution)/shard_map/ppermute | solution.py:625
  132.9 2.6 %collective-permute-done.23.other_ref = bf16[5120,128]{1,0:T(8,128)(2,1)S(1)} collective-permute-done((bf16[5120,128]{1,0:T(8,128)(2,1)S(1)}, bf16[5120,128]{1,0:T(8,128)(2,1)S(1)}, u32[]{:S(2)}, u32[]{:S(2)}) %collective-permute-start.23) | collective-permute-done | bytes 1310752 | tf_op jit(solution)/shard_map/ppermute | solution.py:625
  135.6 8.7 %shard_map.160 = (f32[3,3,256]{2,1,0:T(4,128)}, f32[256,512]{1,0:T(8,128)}, f32[4,512,512]{2,1,0:T(8,128)}, f32[3,3,512]{2,1,0:T(4,128)}, f32[512,256]{1,0:T(8,1...) custom-call(s32[1]{0:T(128)} %bitcast.4.where, ...), custom_call_target="tpu_custom_call" | custom-call | tf_op jit(solution)/shard_map/pallas_call | solution.py:539
  (88 shorter events, 12.8 us)
Async XLA Ops:
  1.4 11.9 %copy-start.6 = (bf16[1,256,96,32]{1,3,2,0:T(8,128)(2,1)S(1)}, bf16[1,256,96,32]{1,3,2,0:T(8,128)(2,1)}, u32[]{:S(2)}) copy-start(bf16[1,256,96,32]{1,3,2,0:T(8,128)(2,1)} %param.8) | copy-start | bytes 4718596
  2.5 6.9 %collective-permute-start = (bf16[8,32,256]{2,1,0:T(8,128)(2,1)S(1)}, bf16[8,32,256]{2,1,0:T(8,128)(2,1)S(1)}, u32[]{:S(2)}, u32[]{:S(2)}) collective-permute-start(bf16[8,32,256]{2,1,0:T(8,128)(2,1)S(1)} %pad_maximum_fusion.8), channel_id=1, source_target_pairs={{0,8},{1,9},{2,10},{3,11},{4,12},{5,13},{6,14},{7,15},{8,16},{9,17... | collective-permute-start | bytes 393224 | tf_op jit(solution)/shard_map/ppermute | solution.py:562
  6.9 6.3 %collective-permute-start.1 = (bf16[8,32,256]{2,1,0:T(8,128)(2,1)S(1)}, bf16[8,32,256]{2,1,0:T(8,128)(2,1)S(1)}, u32[]{:S(2)}, u32[]{:S(2)}) collective-permute-start(bf16[8,32,256]{2,1,0:T(8,128)(2,1)S(1)} %pad_maximum_fusion.9), channel_id=1, source_target_pairs={{8,0},{9,1},{10,2},{11,3},{12,4},{13,5},{14,6},{15,7},{16,8},{17,9... | collective-permute-start | bytes 393224 | tf_op jit(solution)/shard_map/ppermute | solution.py:562
  9.4 4.2 %copy-start.7 = (bf16[8,32,256]{2,1,0:T(8,128)(2,1)}, bf16[8,32,256]{2,1,0:T(8,128)(2,1)S(1)}, u32[]{:S(2)}) copy-start(bf16[8,32,256]{2,1,0:T(8,128)(2,1)S(1)} %collective-permute-done.top_ref) | copy-start | bytes 393220
  14.2 12.7 %collective-permute-start.2 = (bf16[108,8,256]{2,1,0:T(8,128)(2,1)S(1)}, bf16[108,8,256]{2,1,0:T(8,128)(2,1)S(1)}, u32[]{:S(2)}, u32[]{:S(2)}) collective-permute-start(bf16[108,8,256]{2,1,0:T(8,128)(2,1)S(1)} %fusion.14), channel_id=1, source_target_pairs={{1,0},{2,1},{3,2},{4,3},{5,4},{6,5},{7,6},{9,8},{10,9},{11,10},{12... | collective-permute-start | bytes 1327112 | tf_op jit(solution)/shard_map/ppermute | solution.py:562
  18.1 8.9 %collective-permute-start.3 = (bf16[108,8,256]{2,1,0:T(8,128)(2,1)S(1)}, bf16[108,8,256]{2,1,0:T(8,128)(2,1)S(1)}, u32[]{:S(2)}, u32[]{:S(2)}) collective-permute-start(bf16[108,8,256]{2,1,0:T(8,128)(2,1)S(1)} %fusion.18), channel_id=1, source_target_pairs={{0,1},{1,2},{2,3},{3,4},{4,5},{5,6},{6,7},{8,9},{9,10},{10,11},{11... | collective-permute-start | bytes 1327112 | tf_op jit(solution)/shard_map/ppermute | solution.py:562
  60.9 3.3 %collective-permute-start.4 = (bf16[5184,128]{1,0:T(8,128)(2,1)}, bf16[5184,128]{1,0:T(8,128)(2,1)S(1)}, u32[]{:S(2)}, u32[]{:S(2)}) collective-permute-start(bf16[5184,128]{1,0:T(8,128)(2,1)} %get-tuple-element.48), channel_id=1, source_target_pairs={{0,1},{1,0},{2,3},{3,2},{4,5},{5,4},{6,7},{7,6},{8,9},{9,8},{10,11... | collective-permute-start | bytes 3981320 | tf_op jit(solution)/shard_map/ppermute | solution.py:618
  67.0 7.9 %collective-permute-start.5 = (bf16[1344,128]{1,0:T(8,128)(2,1)}, bf16[1344,128]{1,0:T(8,128)(2,1)S(1)}, u32[]{:S(2)}, u32[]{:S(2)}) collective-permute-start(bf16[1344,128]{1,0:T(8,128)(2,1)} %get-tuple-element.92), channel_id=1, source_target_pairs={{0,32},{1,3},{2,34},{3,5},{4,36},{5,7},{6,38},{7,1},{8,40},{9,11},... | collective-permute-start | bytes 1032200 | tf_op jit(solution)/shard_map/ppermute | solution.py:590
  68.4 6.7 %collective-permute-start.7 = (bf16[1344,128]{1,0:T(8,128)(2,1)}, bf16[1344,128]{1,0:T(8,128)(2,1)}, u32[]{:S(2)}, u32[]{:S(2)}) collective-permute-start(bf16[1344,128]{1,0:T(8,128)(2,1)} %get-tuple-element.93), channel_id=1, source_target_pairs={{0,96},{1,7},{2,98},{3,1},{4,100},{5,3},{6,102},{7,5},{8,104},{9,1... | collective-permute-start | bytes 1032200 | tf_op jit(solution)/shard_map/ppermute | solution.py:590
  69.7 10.1 %collective-permute-start.6 = (bf16[1344,128]{1,0:T(8,128)(2,1)}, bf16[1344,128]{1,0:T(8,128)(2,1)}, u32[]{:S(2)}, u32[]{:S(2)}) collective-permute-start(bf16[1344,128]{1,0:T(8,128)(2,1)} %get-tuple-element.94), channel_id=1, source_target_pairs={{0,64},{1,5},{2,66},{3,7},{4,68},{5,1},{6,70},{7,3},{8,72},{9,13},... | collective-permute-start | bytes 1032200 | tf_op jit(solution)/shard_map/ppermute | solution.py:590
  81.9 4.8 %collective-permute-start.8 = (bf16[384,128]{1,0:T(8,128)(2,1)S(1)}, bf16[384,128]{1,0:T(8,128)(2,1)S(1)}, u32[]{:S(2)}, u32[]{:S(2)}) collective-permute-start(bf16[384,128]{1,0:T(8,128)(2,1)S(1)} %get-tuple-element.89), channel_id=1, source_target_pairs={{0,2},{1,33},{2,4},{3,35},{4,6},{5,37},{6,0},{7,39},{8,10},{9,41},... | collective-permute-start | bytes 294920 | tf_op jit(solution)/shard_map/ppermute | solution.py:590
  83.0 5.7 %collective-permute-start.9 = (bf16[384,128]{1,0:T(8,128)(2,1)S(1)}, bf16[384,128]{1,0:T(8,128)(2,1)S(1)}, u32[]{:S(2)}, u32[]{:S(2)}) collective-permute-start(bf16[384,128]{1,0:T(8,128)(2,1)S(1)} %get-tuple-element.90), channel_id=1, source_target_pairs={{0,4},{1,65},{2,6},{3,67},{4,0},{5,69},{6,2},{7,71},{8,12},{9,73},... | collective-permute-start | bytes 294920 | tf_op jit(solution)/shard_map/ppermute | solution.py:590
  85.6 3.5 %collective-permute-start.10 = (bf16[384,128]{1,0:T(8,128)(2,1)S(1)}, bf16[384,128]{1,0:T(8,128)(2,1)S(1)}, u32[]{:S(2)}, u32[]{:S(2)}) collective-permute-start(bf16[384,128]{1,0:T(8,128)(2,1)S(1)} %get-tuple-element.91), channel_id=1, source_target_pairs={{0,6},{1,97},{2,0},{3,99},{4,2},{5,101},{6,4},{7,103},{8,14},{9,10... | collective-permute-start | bytes 294920 | tf_op jit(solution)/shard_map/ppermute | solution.py:590
  89.1 46.5 %copy-start.2 = (f32[512,256]{1,0:T(8,128)S(1)}, f32[512,256]{1,0:T(8,128)}, u32[]{:S(2)}) copy-start(f32[512,256]{1,0:T(8,128)} %refs_4_) | copy-start | bytes 1572868
  89.2 5.3 %collective-permute-start.11 = (bf16[144,128]{1,0:T(8,128)(2,1)S(1)}, bf16[144,128]{1,0:T(8,128)(2,1)S(1)}, u32[]{:S(2)}, u32[]{:S(2)}) collective-permute-start(bf16[144,128]{1,0:T(8,128)(2,1)S(1)} %get-tuple-element.86), channel_id=1, source_target_pairs={{0,8},{1,9},{2,10},{3,11},{4,12},{5,13},{6,14},{7,15},{8,16},{9,17... | collective-permute-start | bytes 110600 | tf_op jit(solution)/shard_map/ppermute | solution.py:590
  90.7 4.3 %collective-permute-start.12 = (bf16[144,128]{1,0:T(8,128)(2,1)S(1)}, bf16[144,128]{1,0:T(8,128)(2,1)S(1)}, u32[]{:S(2)}, u32[]{:S(2)}) collective-permute-start(bf16[144,128]{1,0:T(8,128)(2,1)S(1)} %get-tuple-element.87), channel_id=1, source_target_pairs={{0,16},{1,17},{2,18},{3,19},{4,20},{5,21},{6,22},{7,23},{8,24},{9,... | collective-permute-start | bytes 110600 | tf_op jit(solution)/shard_map/ppermute | solution.py:590
  92.5 3.0 %collective-permute-start.13 = (bf16[144,128]{1,0:T(8,128)(2,1)S(1)}, bf16[144,128]{1,0:T(8,128)(2,1)S(1)}, u32[]{:S(2)}, u32[]{:S(2)}) collective-permute-start(bf16[144,128]{1,0:T(8,128)(2,1)S(1)} %get-tuple-element.88), channel_id=1, source_target_pairs={{0,24},{1,25},{2,26},{3,27},{4,28},{5,29},{6,30},{7,31},{8,0},{9,1... | collective-permute-start | bytes 110600 | tf_op jit(solution)/shard_map/ppermute | solution.py:590
  95.6 4.2 %collective-permute-start.14 = (bf16[80,128]{1,0:T(8,128)(2,1)S(1)}, bf16[80,128]{1,0:T(8,128)(2,1)S(1)}, u32[]{:S(2)}, u32[]{:S(2)}) collective-permute-start(bf16[80,128]{1,0:T(8,128)(2,1)S(1)} %get-tuple-element.60), channel_id=1, source_target_pairs={{0,8},{1,9},{2,10},{3,11},{4,12},{5,13},{6,14},{7,15},{8,16},{9,17... | collective-permute-start | bytes 61448 | tf_op jit(solution)/shard_map/ppermute | solution.py:590
  96.5 4.7 %collective-permute-start.15 = (bf16[80,128]{1,0:T(8,128)(2,1)S(1)}, bf16[80,128]{1,0:T(8,128)(2,1)S(1)}, u32[]{:S(2)}, u32[]{:S(2)}) collective-permute-start(bf16[80,128]{1,0:T(8,128)(2,1)S(1)} %get-tuple-element.60), channel_id=1, source_target_pairs={{0,16},{1,17},{2,18},{3,19},{4,20},{5,21},{6,22},{7,23},{8,24},{9,... | collective-permute-start | bytes 61448 | tf_op jit(solution)/shard_map/ppermute | solution.py:590
  99.8 2.6 %collective-permute-start.16 = (bf16[80,128]{1,0:T(8,128)(2,1)S(1)}, bf16[80,128]{1,0:T(8,128)(2,1)S(1)}, u32[]{:S(2)}, u32[]{:S(2)}) collective-permute-start(bf16[80,128]{1,0:T(8,128)(2,1)S(1)} %get-tuple-element.60), channel_id=1, source_target_pairs={{0,24},{1,25},{2,26},{3,27},{4,28},{5,29},{6,30},{7,31},{8,0},{9,1... | collective-permute-start | bytes 61448 | tf_op jit(solution)/shard_map/ppermute | solution.py:590
  102.4 8.3 %collective-permute-start.19 = (bf16[320,128]{1,0:T(8,128)(2,1)S(1)}, bf16[320,128]{1,0:T(8,128)(2,1)S(1)}, u32[]{:S(2)}, u32[]{:S(2)}) collective-permute-start(bf16[320,128]{1,0:T(8,128)(2,1)S(1)} %bitcast.97), channel_id=1, source_target_pairs={{0,6},{1,97},{2,0},{3,99},{4,2},{5,101},{6,4},{7,103},{8,14},{9,10... | collective-permute-start | bytes 245768 | tf_op jit(solution)/shard_map/ppermute | solution.py:590
  105.0 5.7 %collective-permute-start.18 = (bf16[320,128]{1,0:T(8,128)(2,1)S(1)}, bf16[320,128]{1,0:T(8,128)(2,1)S(1)}, u32[]{:S(2)}, u32[]{:S(2)}) collective-permute-start(bf16[320,128]{1,0:T(8,128)(2,1)S(1)} %bitcast.98), channel_id=1, source_target_pairs={{0,4},{1,65},{2,6},{3,67},{4,0},{5,69},{6,2},{7,71},{8,12},{9,73},... | collective-permute-start | bytes 245768 | tf_op jit(solution)/shard_map/ppermute | solution.py:590
  105.4 5.3 %collective-permute-start.17 = (bf16[320,128]{1,0:T(8,128)(2,1)S(1)}, bf16[320,128]{1,0:T(8,128)(2,1)S(1)}, u32[]{:S(2)}, u32[]{:S(2)}) collective-permute-start(bf16[320,128]{1,0:T(8,128)(2,1)S(1)} %bitcast.99), channel_id=1, source_target_pairs={{0,2},{1,33},{2,4},{3,35},{4,6},{5,37},{6,0},{7,39},{8,10},{9,41},... | collective-permute-start | bytes 245768 | tf_op jit(solution)/shard_map/ppermute | solution.py:590
  106.1 29.4 %copy-start.1 = (f32[256,512]{1,0:T(8,128)S(1)}, f32[256,512]{1,0:T(8,128)}, u32[]{:S(2)}) copy-start(f32[256,512]{1,0:T(8,128)} %refs_1_) | copy-start | bytes 1572868
  110.7 24.9 %copy-start = (f32[2,2,512,512]{3,2,1,0:T(8,128)S(1)}, f32[2,2,512,512]{3,2,1,0:T(8,128)}, u32[]{:S(2)}) copy-start(f32[2,2,512,512]{3,2,1,0:T(8,128)} %param.11) | copy-start | bytes 12582916
  110.8 12.5 %collective-permute-start.20 = (bf16[1280,128]{1,0:T(8,128)(2,1)S(1)}, bf16[1280,128]{1,0:T(8,128)(2,1)S(1)}, u32[]{:S(2)}, u32[]{:S(2)}) collective-permute-start(bf16[1280,128]{1,0:T(8,128)(2,1)S(1)} %bitcast.85), channel_id=1, source_target_pairs={{0,32},{1,3},{2,34},{3,5},{4,36},{5,7},{6,38},{7,1},{8,40},{9,11},... | collective-permute-start | bytes 983048 | tf_op jit(solution)/shard_map/ppermute | solution.py:590
  111.4 12.0 %collective-permute-start.22 = (bf16[1280,128]{1,0:T(8,128)(2,1)S(1)}, bf16[1280,128]{1,0:T(8,128)(2,1)S(1)}, u32[]{:S(2)}, u32[]{:S(2)}) collective-permute-start(bf16[1280,128]{1,0:T(8,128)(2,1)S(1)} %bitcast.86), channel_id=1, source_target_pairs={{0,96},{1,7},{2,98},{3,1},{4,100},{5,3},{6,102},{7,5},{8,104},{9,1... | collective-permute-start | bytes 983048 | tf_op jit(solution)/shard_map/ppermute | solution.py:590
  113.5 9.8 %collective-permute-start.21 = (bf16[1280,128]{1,0:T(8,128)(2,1)S(1)}, bf16[1280,128]{1,0:T(8,128)(2,1)S(1)}, u32[]{:S(2)}, u32[]{:S(2)}) collective-permute-start(bf16[1280,128]{1,0:T(8,128)(2,1)S(1)} %bitcast.87), channel_id=1, source_target_pairs={{0,64},{1,5},{2,66},{3,7},{4,68},{5,1},{6,70},{7,3},{8,72},{9,13},... | collective-permute-start | bytes 983048 | tf_op jit(solution)/shard_map/ppermute | solution.py:590
  113.7 21.9 %copy-start.3 = (f32[3,3,512]{2,1,0:T(4,128)S(1)}, f32[3,3,512]{2,1,0:T(4,128)}, u32[]{:S(2)}) copy-start(f32[3,3,512]{2,1,0:T(4,128)} %refs_3_) | copy-start | bytes 55300
  113.7 21.9 %copy-start.4 = (f32[3,3,256]{2,1,0:T(4,128)S(1)}, f32[3,3,256]{2,1,0:T(4,128)}, u32[]{:S(2)}) copy-start(f32[3,3,256]{2,1,0:T(4,128)} %refs_0_) | copy-start | bytes 27652
  113.7 21.9 %copy-start.5 = (f32[5]{0:T(128)S(1)}, f32[5]{0:T(128)}, u32[]{:S(2)}) copy-start(f32[5]{0:T(128)} %get-tuple-element.46.sums) | copy-start | bytes 64
  123.4 12.2 %collective-permute-start.23 = (bf16[5120,128]{1,0:T(8,128)(2,1)S(1)}, bf16[5120,128]{1,0:T(8,128)(2,1)S(1)}, u32[]{:S(2)}, u32[]{:S(2)}) collective-permute-start(bf16[5120,128]{1,0:T(8,128)(2,1)S(1)} %bitcast.80), channel_id=1, source_target_pairs={{0,1},{1,0},{2,3},{3,2},{4,5},{5,4},{6,7},{7,6},{8,9},{9,8},{10,11... | collective-permute-start | bytes 3932168 | tf_op jit(solution)/shard_map/ppermute | solution.py:625
  (3 other events, 2.3 us)

commit v3 on v2

--- a/solution.py
+++ b/solution.py
@@ -34,19 +34,29 @@
 def tile_kernel(
     limits,
     x_ref,
-    t_ref,
+    t_hbm,
     top_ref,
     bot_ref,
     right_ref,
     left_ref,
+    right_ends,
+    left_ends,
     k1_ref,
+    p1_full,
+    taps_hbm,
+    k2_ref,
+    p2_full,
+    pred_hbm,
+    keep_ref,
+    send_ref,
+    sums_ref,
+    t_ref,
+    taps_full,
     p1_ref,
     taps_ref,
-    k2_ref,
     p2_ref,
     pred_ref,
-    keep_ref,
-    send_ref,
+    sems,
     xf,
     tf,
     d2,
@@ -91,7 +101,16 @@
         def _():
             send_ref[at : at + value.shape[0], :] = value
 
+    copies = [
+        pltpu.make_async_copy(t_hbm, t_ref, sems.at[0]),
+        pltpu.make_async_copy(taps_hbm, taps_full, sems.at[1]),
+        pltpu.make_async_copy(pred_ref, pred_hbm, sems.at[2]),
+    ]
+    copies[0].start()
+    copies[1].start()
     small[...] = jnp.zeros_like(small)
+    p1_ref[...] = p1_full[...].astype(BF16)
+    p2_ref[...] = p2_full[...].astype(BF16)
 
     def put(row, count, block, c):
         xf[c, pl.ds(row, count), 8 : 8 + cols, :] = block.astype(F32)
@@ -115,16 +134,24 @@
         xf[c, at, 7:8, :] = left[:, 7:8, :]
         xf[c, at, 24 + cols : 25 + cols, :] = xf[c, at, 8:9, :]
 
-    @pl.loop(0, (rows + 2 * ROWS) // step)
+    for c in range(cb1):
+        put_sides(0, ROWS, right_ends[0:ROWS, :, lanes(c)], left_ends[0:ROWS, :, lanes(c)], c)
+        cut = (slice(ROWS + 2, 2 * ROWS + 2), slice(None), lanes(c))
+        put_sides(rows + ROWS, ROWS, right_ends[cut], left_ends[cut], c)
+
+    @pl.loop(0, rows // step)
     def _(n):
         at = pl.ds(n * step, step)
         for c in range(cb1):
-            put_sides(n * step, step, right_ref[at, :, lanes(c)], left_ref[at, :, lanes(c)], c)
-
-    def diff(first, count, block, c):
+            put_sides(ROWS + n * step, step, right_ref[at, :, lanes(c)], left_ref[at, :, lanes(c)], c)
+
+    copies[0].wait()
+
+    def diff(first, count, block, right, left, ends, c):
         at = pl.ds(2 * first + ROWS, 2 * count)
-        tf[c, 0 : 2 * count, cols - 5 : cols + 3, :] = right_ref[at, :, lanes(c)].astype(F32)
-        tf[c, 0 : 2 * count, cols + 13 : cols + 21, :] = left_ref[at, :, lanes(c)].astype(F32)
+        rcol, lcol = (cols, cols + 8) if ends else (cols - 5, cols + 13)
+        tf[c, 0 : 2 * count, rcol : rcol + 8, :] = right.astype(F32)
+        tf[c, 0 : 2 * count, lcol : lcol + 8, :] = left.astype(F32)
         tf[c, 0 : 2 * count, 0:cols, :] = block.astype(F32)
         both = xf[c, at, 8 : 24 + cols, :] - tf[c, 0 : 2 * count, 0 : 16 + cols, :]
         both = both.reshape(count, 2, 16 + cols, LANES)
@@ -134,13 +161,16 @@
         d2[c, pl.ds(first + 1, count), :, :] = (even + odd) * 0.25
 
     for c in range(cb1):
-        diff(-1, 1, top_ref[ROWS : ROWS + 2, :, lanes(c)], c)
-        diff(hr, 1, bot_ref[ROWS : ROWS + 2, :, lanes(c)], c)
+        own = (slice(ROWS, ROWS + 2), slice(None), lanes(c))
+        diff(-1, 1, top_ref[own], right_ends[own], left_ends[own], True, c)
+        cut = (slice(2 * ROWS + 2, 2 * ROWS + 4), slice(None), lanes(c))
+        diff(hr, 1, bot_ref[own], right_ends[cut], left_ends[cut], True, c)
 
     @pl.loop(0, hr // 4)
     def _(n):
         for c in range(cb1):
-            diff(n * 4, 4, t_ref[pl.ds(n * 8, 8), :, lanes(c)], c)
+            cut = (pl.ds(n * 8, 8), slice(None), lanes(c))
+            diff(n * 4, 4, t_ref[cut], right_ref[cut], left_ref[cut], False, c)
 
     take = 4
 
@@ -194,6 +224,19 @@
         ref[c, at, 7:8, :] = value[:, slots - 1 : slots, :]
         ref[c, at, 8 + slots : 9 + slots, :] = value[:, 0:1, :]
 
+    copies[1].wait()
+
+    piece = 128
+
+    def cast(n, acc):
+        ph, at = n // (hid // piece), pl.ds(n % (hid // piece) * piece, piece)
+        w = taps_full[ph, at, :]
+        taps_ref[ph, at, :] = w.astype(BF16)
+        return acc + jnp.sum((w * w).reshape(piece // 8, 8, hid), axis=0)
+
+    sums_ref[2] = jnp.sum(lax.fori_loop(0, 4 * hid // piece, cast, jnp.zeros((8, hid), F32)))
+    for j, ref in ((0, k1_ref), (1, p1_full), (3, k2_ref), (4, p2_full)):
+        sums_ref[j] = jnp.sum(ref[...] * ref[...])
     half = er // 2
 
     @pl.loop(0, 2)
@@ -263,6 +306,8 @@
             fine = xf[c, pl.ds(n * 8 + ROWS, 8), 8 : 8 + cols, :]
             pred_ref[pl.ds(n * 8, 8), :, lanes(c)] = (wide + fine).astype(BF16)
 
+    copies[2].start()
+
     for c in range(cb2):
         def body(n, acc, c=c):
             acc = list(acc)
@@ -307,31 +352,37 @@
 
         def body(n, acc, c=c):
             acc = list(acc)
-            grads = [bp[ph, c, n] for ph in range(4)]
-            for s in range(4):
-                e = 2 * n + ROWS + s - 1
+            grads = [[bp[ph, c, 2 * n + i] for ph in range(4)] for i in range(2)]
+            for s in range(6):
+                e = 4 * n + ROWS + s - 1
                 col = [xf[c, e, pl.ds(7 + o, hc, stride=2), :] for o in range(4)]
-                for r in range(2):
-                    a = s - r
-                    if 0 <= a < 3:
-                        for q in range(2):
-                            for b in range(3):
-                                p = grads[2 * r + q] * col[q + b]
-                                acc[3 * a + b] = acc[3 * a + b] + (p[0:8] + p[8:16])
+                for i in range(2):
+                    for r in range(2):
+                        a = s - 2 * i - r
+                        if 0 <= a < 3:
+                            for q in range(2):
+                                for b in range(3):
+                                    p = grads[i][2 * r + q] * col[q + b]
+                                    acc[3 * a + b] = acc[3 * a + b] + (p[0:8] + p[8:16])
             return tuple(acc)
 
-        acc = lax.fori_loop(0, hr, body, tuple(jnp.zeros((8, LANES), F32) for _ in range(9)))
+        acc = lax.fori_loop(0, hr // 2, body, tuple(jnp.zeros((8, LANES), F32) for _ in range(9)))
         for j in range(9):
             at = 9 * c + j
             small[at : at + 1, :] = jnp.sum(acc[j], axis=0, keepdims=True)
 
 
+    copies[2].wait()
     for ref in (keep_ref, send_ref):
         ref[small_at : small_at + SMALL, :] = small[...].astype(BF16)
 
 
 def vmem():
     return pl.BlockSpec(memory_space=pltpu.VMEM)
+
+
+def hbm():
+    return pl.BlockSpec(memory_space=pl.ANY)
 
 
 def smem():
@@ -351,10 +402,20 @@
             jax.ShapeDtypeStruct(x.shape, BF16),
             jax.ShapeDtypeStruct((grads, LANES), BF16),
             jax.ShapeDtypeStruct((grads, LANES), BF16),
+            jax.ShapeDtypeStruct((5,), F32),
         ),
-        in_specs=[smem()] + [vmem()] * (7 + len(halos)),
-        out_specs=[vmem()] * 3,
+        in_specs=[smem(), vmem(), hbm()]
+        + [vmem()] * (len(halos) + 2)
+        + [hbm(), vmem(), vmem()],
+        out_specs=[hbm(), vmem(), vmem(), smem()],
         scratch_shapes=[
+            pltpu.VMEM(t.shape, BF16),
+            pltpu.VMEM(taps.shape, F32),
+            pltpu.VMEM(p1.shape, BF16),
+            pltpu.VMEM(taps.shape, BF16),
+            pltpu.VMEM(p2.shape, BF16),
+            pltpu.VMEM(x.shape, BF16),
+            pltpu.SemaphoreType.DMA((3,)),
             pltpu.VMEM((cb1, rows + 2 * ROWS, cols + 32, LANES), F32),
             pltpu.VMEM((cb1, 8, cols + 32, LANES), F32),
             pltpu.VMEM((cb1, hr + 2, slots, LANES), F32),
@@ -376,47 +437,32 @@
     )(limits, x, t, *halos, k1, p1, taps, k2, p2)
 
 
-def prepare_kernel(p1_ref, st_ref, p2_ref, k1_ref, k2_ref, lp1_ref, lst_ref, lp2_ref, out_ref, acc):
-    step = pl.program_id(0)
-
-    @pl.when(step == 0)
-    def _():
-        for j, ref in ((0, k1_ref), (1, p1_ref), (3, k2_ref), (4, p2_ref)):
-            out_ref[j] = jnp.sum(ref[...] * ref[...])
-        lp1_ref[...] = p1_ref[...].astype(BF16)
-        lp2_ref[...] = p2_ref[...].astype(BF16)
-        acc[...] = jnp.zeros_like(acc)
-
-    w = st_ref[0]
-    lst_ref[0] = w.astype(BF16)
-    acc[...] += jnp.sum((w * w).reshape(-1, 8, w.shape[1]), axis=0)
-
-    @pl.when(step == pl.num_programs(0) - 1)
-    def _():
-        out_ref[2] = jnp.sum(acc[...])
-
-
-def prepared(k1, p1, taps, k2, p2):
-    parts, hid = taps.shape[:2]
-    p1_spec = pl.BlockSpec(p1.shape, lambda n: (0, 0))
-    st_spec = pl.BlockSpec((1,) + taps.shape[1:], lambda n: (n, 0, 0))
-    p2_spec = pl.BlockSpec(p2.shape, lambda n: (0, 0))
+def edges_kernel(xt, tt, xb, tb, xl, tl, xr, tr, up, down, ahead, back):
+    up[...] = jnp.concatenate([xt[0:ROWS], tt[0:2]], axis=0)
+    down[...] = jnp.concatenate([xb[8 - ROWS : 8], tb[6:8]], axis=0)
+    col = lax.broadcasted_iota(jnp.int32, ahead.shape, 1)
+    x, t = xl[...].astype(F32)[:, 0:8], tl[...].astype(F32)[:, 0:8]
+    ahead[...] = jnp.where((col >= 5) & (col < 7), pltpu.roll(t, 5, 1), x).astype(BF16)
+    x, t = xr[...].astype(F32)[:, 8:16], tr[...].astype(F32)[:, 8:16]
+    back[...] = jnp.where((col >= 1) & (col < 3), pltpu.roll(t, 3, 1), x).astype(BF16)
+
+
+def edges(x, t):
+    rows, cols, chan = x.shape
+    specs = [
+        pl.BlockSpec((8, cols, chan), lambda n: (0, 0, 0)),
+        pl.BlockSpec((8, cols, chan), lambda n: (rows // 8 - 1, 0, 0)),
+        pl.BlockSpec((rows, 16, chan), lambda n: (0, 0, 0)),
+        pl.BlockSpec((rows, 16, chan), lambda n: (0, cols // 16 - 1, 0)),
+    ]
+    shapes = [(ROWS + 2, cols, chan)] * 2 + [(rows, 8, chan)] * 2
     return pl.pallas_call(
-        prepare_kernel,
-        grid=(parts,),
-        out_shape=[jax.ShapeDtypeStruct(w.shape, BF16) for w in (p1, taps, p2)]
-        + [jax.ShapeDtypeStruct((5,), F32)],
-        in_specs=[
-            p1_spec,
-            st_spec,
-            p2_spec,
-            pl.BlockSpec(k1.shape, lambda n: (0, 0, 0)),
-            pl.BlockSpec(k2.shape, lambda n: (0, 0, 0)),
-        ],
-        out_specs=[p1_spec, st_spec, p2_spec, smem()],
-        scratch_shapes=[pltpu.VMEM((8, hid), F32)],
-        cost_estimate=pl.CostEstimate(flops=3_000_000, bytes_accessed=8_000_000, transcendentals=0),
-    )(p1, taps, p2, k1, k2)
+        edges_kernel,
+        grid=(1,),
+        out_shape=[jax.ShapeDtypeStruct(s, BF16) for s in shapes],
+        in_specs=[s for s in specs for _ in range(2)],
+        out_specs=[pl.BlockSpec(s, lambda n: (0, 0, 0)) for s in shapes],
+    )(*[x, t] * 4)
 
 
 def update_kernel(
@@ -430,7 +476,7 @@
     (
         k1_ref,
         p1_ref,
-        st_ref,
+        st_hbm,
         k2_ref,
         p2_ref,
         nk1_ref,
@@ -446,11 +492,19 @@
         g,
         small,
         scale,
+        st_ref,
+        sems,
     ) = refs
     chan, hid = p1_ref.shape
     cb1, cb2 = chan // LANES, hid // LANES
     parts, block = 4, st_ref.shape[1]
     step = pl.program_id(0)
+    per = hid // block
+
+    def fetch(n):
+        at = pl.ds(n % per * block, block)
+        return pltpu.make_async_copy(st_hbm.at[n // per, at, :], st_ref.at[n], sems.at[n])
+
     core = where[0]
     st_rows, p1_rows, p2_rows = hid * cb2, chan * cb2, hid * cb1
     p1_at = 2 * st_rows
@@ -481,6 +535,8 @@
 
     @pl.when(step == 0)
     def _():
+        for n in range(parts * per):
+            fetch(n).start()
         g[core] = own_ref[...]
         g[1 - core] = other_ref[...]
         small[...] = small_ref[...].astype(F32)
@@ -515,14 +571,14 @@
             sp2_ref[:, cut] = normed
             np2_ref[:, cut] = p2_ref[:, cut] - scale[9] * normed
 
-    per = hid // block
+    fetch(step).wait()
     ph = step // per
     for c in range(cb2):
         cut = slice(c * LANES, (c + 1) * LANES)
         at = (ph % 2) * st_rows + c * hid + (step % per) * block
         normed = g[ph // 2, pl.ds(at, block), :].astype(F32) * scale[2]
         sst_ref[0, :, cut] = normed
-        nst_ref[0, :, cut] = st_ref[0, :, cut] - scale[7] * normed
+        nst_ref[0, :, cut] = st_ref[step, :, cut] - scale[7] * normed
 
 
 def update(where, sums, small, own, other, k1, p1, taps, k2, p2):
@@ -540,12 +596,17 @@
         update_kernel,
         grid=(4 * per,),
         out_shape=shapes + shapes,
-        in_specs=[smem(), smem(), whole(small)] + [whole(own), whole(other)] + specs,
+        in_specs=[smem(), smem(), whole(small)] + [whole(own), whole(other)]
+        + specs[:2]
+        + [hbm()]
+        + specs[3:],
         out_specs=specs + specs,
         scratch_shapes=[
             pltpu.VMEM((2,) + own.shape, BF16),
             pltpu.VMEM((SMALL, LANES), F32),
             pltpu.SMEM((10,), F32),
+            pltpu.VMEM((4 * per, block, hid), F32),
+            pltpu.SemaphoreType.DMA((4 * per,)),
         ],
         compiler_params=pltpu.CompilerParams(vmem_limit_bytes=40 * 1024 * 1024),
     )(where, sums, small, own, other, k1, p1, taps, k2, p2)
@@ -599,8 +660,19 @@
             out = lax.dynamic_index_in_dim(shares, (self.me + d) % n, 0, False)
             got.append(self.send(jnp.concatenate([out, extra], axis=0), d))
         total = sum([g[:cut].astype(F32) for g in got], share.astype(F32))
-        extra = sum([g[cut:].astype(F32) for g in got], extra.astype(F32))
-        return total.astype(BF16), extra.astype(BF16)
+        return total.astype(BF16), self.added([extra] + [g[cut:] for g in got])
+
+    def added(self, parts):
+        n = self.count
+        parts = jnp.stack(parts)
+        total = None
+        for k in range(n):
+            part = lax.dynamic_index_in_dim(parts, (self.me + n - k) % n, 0, False).astype(F32)
+            total = part if total is None else total + part
+        return total.astype(BF16)
+
+    def reduce(self, block):
+        return self.added([block] + [self.send(block, d) for d in range(1, self.count)])
 
     def gather(self, share):
         n = self.count
@@ -613,13 +685,15 @@
 
 
 def reduced(keep, send):
-    rings = (Ring("yx"), Ring("xy"), Ring("zz"))
+    rings = (Ring("yx"), Ring("xy"))
     cores = [(i, i ^ 1) for i in range(lax.axis_size("tx"))]
     got = lax.ppermute(send, "tx", cores)
     both = (keep.astype(F32) + got.astype(F32)).astype(BF16)
     share, small = both[: both.shape[0] - SMALL], both[both.shape[0] - SMALL :]
     for ring in rings:
         share, small = ring.scatter(share, small)
+    both = Ring("zz").reduce(jnp.concatenate([share, small], axis=0))
+    share, small = both[: share.shape[0]], both[share.shape[0] :]
     for ring in rings[::-1]:
         share = ring.gather(share)
     return small, share, lax.ppermute(share, "tx", cores)
@@ -631,25 +705,17 @@
     rows, cols, chan = x.shape
     hid = point_one.shape[1]
     hr, hc = rows // 2, cols // 2
-    up = jnp.concatenate([x[:ROWS], t[:2]], axis=0)
-    down = jnp.concatenate([x[rows - ROWS :], t[rows - 2 :]], axis=0)
+    up, down, ahead, back = edges(x, t)
     top, bot = shift(down, 1, 0), shift(up, -1, 0)
-    taps = coarsening_taps.reshape(4, hid, hid)
-    weights = (kern_one, point_one, taps, kern_two, point_two)
-    weights, top, bot = lax.optimization_barrier((weights, top, bot))
-    low_one, low_taps, low_two, sums = prepared(*weights)
-
-    def edge(cut):
-        e = jnp.concatenate([top[:ROWS, cut], x[:, cut], bot[:ROWS, cut]], axis=0)
-        z = jnp.zeros((ROWS - 2,) + e.shape[1:], BF16)
-        f = jnp.concatenate([z, top[ROWS:, cut], t[:, cut], bot[ROWS:, cut], z], axis=0)
-        return e, f
-
-    e, f = edge(slice(0, 8))
-    right = shift(jnp.concatenate([e[:, :5], f[:, :2], e[:, 7:]], axis=1), 0, -1)
-    e, f = edge(slice(cols - 8, cols))
-    left = shift(jnp.concatenate([e[:, :1], f[:, 6:], e[:, 3:]], axis=1), 0, 1)
-    halos = [top, bot, right, left]
+    ends = jnp.concatenate([top, bot], axis=0)
+    halos = [
+        top,
+        bot,
+        shift(ahead, 0, -1),
+        shift(back, 0, 1),
+        shift(ends[:, :8], 0, -1),
+        shift(ends[:, cols - 8 :], 0, 1),
+    ]
     ty, tx = lax.axis_index("ty"), lax.axis_index("tx")
     big = 1 << 20
     limits = jnp.stack(
@@ -661,9 +727,9 @@
             tx % 2,
         ]
     ).astype(jnp.int32)
-    pred, keep, send = tile_step(
-        limits, x, t, halos, kern_one, low_one, low_taps, kern_two, low_two
-    )
+    taps = coarsening_taps.reshape(4, hid, hid)
+    weights = (kern_one, point_one, taps, kern_two, point_two)
+    pred, keep, send, sums = tile_step(limits, x, t, halos, *weights)
     small, own, other = reduced(keep, send)
     outs = update((tx % 2)[None].astype(jnp.int32), sums, small, own, other, *weights)
     outs = [o.reshape(coarsening_taps.shape) if o.shape == taps.shape else o for o in outs]

time: 145 us -> 130 us (0.90)
  waiting for transfers between devices: 38.1 us -> 34.3 us
  local copies, waits for them, and re-layouts: 5.8 us -> 2.09 us
  other arithmetic: 5.47 us -> 2.21 us
  starting transfers between devices: 46.9 us -> 44.4 us
  Pallas kernels: 46.9 us -> 45.3 us
    ppermute x4 -> x6, starting transfers between devices: 12.3 us -> 17.4 us  [shift(): return lax.ppermute(block, ('ty', 'tx'), pairs)]
    ppermute x1, starting transfers between devices: 9.49 us -> 5.34 us  [reduced(): return (small, share, lax.ppermute(share, 'tx', cores))]
    ppermute x18 -> x15, starting transfers between devices: 25.2 us -> 21.5 us  [send(): return lax.ppermute(block, ('rep', 'ty', 'tx'), pairs)]
    slice x6 -> x3, local copies, waits for them, and re-layouts: 3.22 us -> 0.04 us  [the longest x2 0.03 us: reduced(): share, small = (both[:share.shape[0]], both[share.shape[0]:])]
    ppermute x18 -> x15, waiting for transfers between devices: 28.4 us -> 25.5 us  [send(): return lax.ppermute(block, ('rep', 'ty', 'tx'), pairs)]
    pallas_call x1, Pallas kernels: 5.18 us -> 3.17 us  [edges(): pl.pallas_call(edges_kernel, grid=(1,), out_shape=[jax.ShapeDtypeStruct(s...]
    convert_element_type x5 -> x2, other arithmetic: 2.07 us -> 0.23 us  [scatter(): return (total.astype(BF16), self.added([extra] + [g[cut:] for g in got]))]
    ppermute x4 -> x6, waiting for transfers between devices: 3.81 us -> 3.04 us  [shift(): return lax.ppermute(block, ('ty', 'tx'), pairs)]
  transfers between devices with their start and end apart: 24 -> 23, of which waited for: 14 -> 11; matrix products, arithmetic and copies ran while one was open for 2% -> 1% of each run, Pallas kernels for 4% -> 0%
where the time goes in v3:
time: 130 us
  Pallas kernels  45.3 us (35%)
  starting transfers between devices  44.4 us (34%)
  waiting for transfers between devices  34.3 us (26%)
  other arithmetic  2.21 us (2%)
  local copies, waits for them, and re-layouts  2.09 us (2%)
  between operations  1.34 us (1%)
    pallas_call x1, Pallas kernels, tile_step(): pl.pallas_call(tile_kernel, out_shape=(jax.ShapeDtypeStruct(x.shape, BF16...  33 us
    ppermute x15, waiting for transfers between devices, send(): return lax.ppermute(block, ('rep', 'ty', 'tx'), pairs)  25.5 us
    ppermute x15, starting transfers between devices, send(): return lax.ppermute(block, ('rep', 'ty', 'tx'), pairs)  21.5 us
    ppermute x6, starting transfers between devices, shift(): return lax.ppermute(block, ('ty', 'tx'), pairs)  17.4 us
    pallas_call x1, Pallas kernels, update(): pl.pallas_call(update_kernel, grid=(4 * per,), out_shape=shapes + shapes,...  9.11 us
    ppermute x1, starting transfers between devices, reduced(): return (small, share, lax.ppermute(share, 'tx', cores))  5.34 us
    pallas_call x1, Pallas kernels, edges(): pl.pallas_call(edges_kernel, grid=(1,), out_shape=[jax.ShapeDtypeStruct(s...  3.17 us
    ppermute x1, waiting for transfers between devices, reduced(): got = lax.ppermute(send, 'tx', cores)  3.17 us
  transfers between devices with their start and end apart: 23, of which 11 were waited for; matrix products, arithmetic and copies ran while one was open for 1% of the time, Pallas kernels for 0%

profile of v3, /device:TPU:1, one launch (start us, length us, event | category | flops | bytes accessed | tf_op | source)
XLA Modules:
  0.0 129.6 jit_solution(5706897013247937454)
XLA Ops:
  0.6 3.2 %shard_map.158 = (bf16[8,32,256]{2,1,0:T(8,128)(2,1)}, bf16[8,32,256]{2,1,0:T(8,128)(2,1)}, bf16[96,8,256]{2,1,0:T(8,128)(2,1)}, bf16[96,8,256]{2,1,0:T(8,128)(2,1)}) custom-call(bf16[96,32,256]{2,1,0:T(8,128)(2,1)} %bitcast.85, bf16[96,32,256]{2,1,0:T(8,128)(2,1)} %bitcast.90, bf16[96,32,256]{2,1,0:T(8,128)(2,1)} %bitcast.86, ...), custom_call_target="tpu_custom_call" | custom-call | tf_op jit(solution)/shard_map/pallas_call | solution.py:459
  3.8 4.4 %collective-permute-start = (bf16[8,32,256]{2,1,0:T(8,128)(2,1)}, bf16[8,32,256]{2,1,0:T(8,128)(2,1)S(1)}, u32[]{:S(2)}, u32[]{:S(2)}) collective-permute-start(bf16[8,32,256]{2,1,0:T(8,128)(2,1)} %get-tuple-element.29), channel_id=1, source_target_pairs={{0,8},{1,9},{2,10},{3,11},{4,12},{5,13},{6,14},{7,15},{8,16},{9,17... | collective-permute-start | bytes 393224 | tf_op jit(solution)/shard_map/ppermute | solution.py:623
  8.2 1.3 collective-permute-start.1
  9.5 2.9 %collective-permute-start.2 = (bf16[96,8,256]{2,1,0:T(8,128)(2,1)}, bf16[96,8,256]{2,1,0:T(8,128)(2,1)S(1)}, u32[]{:S(2)}, u32[]{:S(2)}) collective-permute-start(bf16[96,8,256]{2,1,0:T(8,128)(2,1)} %get-tuple-element.31), channel_id=1, source_target_pairs={{1,0},{2,1},{3,2},{4,3},{5,4},{6,5},{7,6},{9,8},{10,9},{11,10},{12... | collective-permute-start | bytes 1179656 | tf_op jit(solution)/shard_map/ppermute | solution.py:623
  12.4 3.0 %collective-permute-start.3 = (bf16[96,8,256]{2,1,0:T(8,128)(2,1)}, bf16[96,8,256]{2,1,0:T(8,128)(2,1)}, u32[]{:S(2)}, u32[]{:S(2)}) collective-permute-start(bf16[96,8,256]{2,1,0:T(8,128)(2,1)} %get-tuple-element.32), channel_id=1, source_target_pairs={{0,1},{1,2},{2,3},{3,4},{4,5},{5,6},{6,7},{8,9},{9,10},{10,11},{11... | collective-permute-start | bytes 1179656 | tf_op jit(solution)/shard_map/ppermute | solution.py:623
  15.5 3.9 %collective-permute-start.5 = (bf16[16,8,256]{2,1,0:T(8,128)(2,1)S(1)}, bf16[16,8,256]{2,1,0:T(8,128)(2,1)S(1)}, u32[]{:S(2)}, u32[]{:S(2)}) collective-permute-start(bf16[16,8,256]{2,1,0:T(8,128)(2,1)S(1)} %get-tuple-element.55), channel_id=1, source_target_pairs={{0,1},{1,2},{2,3},{3,4},{4,5},{5,6},{6,7},{8,9},{9,10},{10,11},{11... | collective-permute-start | bytes 196616 | tf_op jit(solution)/shard_map/ppermute | solution.py:623
  19.4 1.9 %collective-permute-start.4 = (bf16[16,8,256]{2,1,0:T(8,128)(2,1)S(1)}, bf16[16,8,256]{2,1,0:T(8,128)(2,1)S(1)}, u32[]{:S(2)}, u32[]{:S(2)}) collective-permute-start(bf16[16,8,256]{2,1,0:T(8,128)(2,1)S(1)} %get-tuple-element.56), channel_id=1, source_target_pairs={{1,0},{2,1},{3,2},{4,3},{5,4},{6,5},{7,6},{9,8},{10,9},{11,10},{12... | collective-permute-start | bytes 196616 | tf_op jit(solution)/shard_map/ppermute | solution.py:623
  22.0 3.0 %collective-permute-done.4.right_ends = bf16[16,8,256]{2,1,0:T(8,128)(2,1)S(1)} collective-permute-done((bf16[16,8,256]{2,1,0:T(8,128)(2,1)S(1)}, bf16[16,8,256]{2,1,0:T(8,128)(2,1)S(1)}, u32[]{:S(2)}, u32[]{:S(2)}) %collective-permute-start.4) | collective-permute-done | bytes 65568 | tf_op jit(solution)/shard_map/ppermute | solution.py:623
  25.8 33.0 %shard_map.159 = (bf16[96,32,256]{2,1,0:T(8,128)(2,1)}, bf16[5184,128]{1,0:T(8,128)(2,1)}, bf16[5184,128]{1,0:T(8,128)(2,1)}, f32[5]{0:T(128)}) custom-call(s32[5]{0:T(128)} %stack.66.limits, bf16[96,32,256]{2,1,0:T(8,128)(2,1)} %bitcast.89, bf16[96,32,256]{2,1,0:T(8,128)(2,1)} %bitcast.94, bf16[8,32,256]{2,1,0:T(8,128)(2,1)} %copy-done.6, ...), custom_call_target="tpu_custom_call" | custom-call | flops 8999999488 | bytes 20000000 | tf_op jit(solution)/shard_map/pallas_call | solution.py:399
  59.0 3.2 %collective-permute-done.6 = bf16[5184,128]{1,0:T(8,128)(2,1)S(1)} collective-permute-done((bf16[5184,128]{1,0:T(8,128)(2,1)}, bf16[5184,128]{1,0:T(8,128)(2,1)S(1)}, u32[]{:S(2)}, u32[]{:S(2)}) %collective-permute-start.6) | collective-permute-done | bytes 1327136 | tf_op jit(solution)/shard_map/ppermute | solution.py:690
  62.1 1.7 %add_convert_fusion = bf16[5184,128]{1,0:T(8,128)(2,1)S(1)} fusion(bf16[5184,128]{1,0:T(8,128)(2,1)S(1)} %collective-permute-done.6, bf16[5184,128]{1,0:T(8,128)(2,1)} %get-tuple-element.35), kind=kLoop, calls=%fused_computation | loop fusion | flops 2654208 | bytes 3981312 | tf_op jit(solution)/shard_map/convert_element_type | solution.py:691
  64.1 1.5 %collective-permute-start.7 = (bf16[1344,128]{1,0:T(8,128)(2,1)S(1)}, bf16[1344,128]{1,0:T(8,128)(2,1)S(1)}, u32[]{:S(2)}, u32[]{:S(2)}) collective-permute-start(bf16[1344,128]{1,0:T(8,128)(2,1)S(1)} %get-tuple-element.64), channel_id=1, source_target_pairs={{0,32},{1,3},{2,34},{3,5},{4,36},{5,7},{6,38},{7,1},{8,40},{9,11},... | collective-permute-start | bytes 1032200 | tf_op jit(solution)/shard_map/ppermute | solution.py:651
  65.6 1.5 %collective-permute-start.9 = (bf16[1344,128]{1,0:T(8,128)(2,1)S(1)}, bf16[1344,128]{1,0:T(8,128)(2,1)S(1)}, u32[]{:S(2)}, u32[]{:S(2)}) collective-permute-start(bf16[1344,128]{1,0:T(8,128)(2,1)S(1)} %get-tuple-element.65), channel_id=1, source_target_pairs={{0,96},{1,7},{2,98},{3,1},{4,100},{5,3},{6,102},{7,5},{8,104},{9,1... | collective-permute-start | bytes 1032200 | tf_op jit(solution)/shard_map/ppermute | solution.py:651
  67.0 1.2 collective-permute-start.8
  68.3 7.4 %collective-permute-done.7 = bf16[1344,128]{1,0:T(8,128)(2,1)S(1)} collective-permute-done((bf16[1344,128]{1,0:T(8,128)(2,1)S(1)}, bf16[1344,128]{1,0:T(8,128)(2,1)S(1)}, u32[]{:S(2)}, u32[]{:S(2)}) %collective-permute-start.7) | collective-permute-done | bytes 344096 | tf_op jit(solution)/shard_map/ppermute | solution.py:651
  76.0 1.2 collective-permute-start.10
  77.2 2.8 %collective-permute-start.11 = (bf16[384,128]{1,0:T(8,128)(2,1)S(1)}, bf16[384,128]{1,0:T(8,128)(2,1)S(1)}, u32[]{:S(2)}, u32[]{:S(2)}) collective-permute-start(bf16[384,128]{1,0:T(8,128)(2,1)S(1)} %get-tuple-element.62), channel_id=1, source_target_pairs={{0,4},{1,65},{2,6},{3,67},{4,0},{5,69},{6,2},{7,71},{8,12},{9,73},... | collective-permute-start | bytes 294920 | tf_op jit(solution)/shard_map/ppermute | solution.py:651
  80.0 0.8 collective-permute-start.12
  80.8 2.2 %collective-permute-done.11 = bf16[384,128]{1,0:T(8,128)(2,1)S(1)} collective-permute-done((bf16[384,128]{1,0:T(8,128)(2,1)S(1)}, bf16[384,128]{1,0:T(8,128)(2,1)S(1)}, u32[]{:S(2)}, u32[]{:S(2)}) %collective-permute-start.11) | collective-permute-done | bytes 98336 | tf_op jit(solution)/shard_map/ppermute | solution.py:651
  83.8 3.2 %collective-permute-start.14 = (bf16[384,128]{1,0:T(8,128)(2,1)S(1)}, bf16[384,128]{1,0:T(8,128)(2,1)S(1)}, u32[]{:S(2)}, u32[]{:S(2)}) collective-permute-start(bf16[384,128]{1,0:T(8,128)(2,1)S(1)} %get-tuple-element.60), channel_id=1, source_target_pairs={{0,16},{1,17},{2,18},{3,19},{4,20},{5,21},{6,22},{7,23},{8,24},{9,... | collective-permute-start | bytes 294920 | tf_op jit(solution)/shard_map/ppermute | solution.py:651
  87.4 2.3 %collective-permute-start.15 = (bf16[384,128]{1,0:T(8,128)(2,1)S(1)}, bf16[384,128]{1,0:T(8,128)(2,1)S(1)}, u32[]{:S(2)}, u32[]{:S(2)}) collective-permute-start(bf16[384,128]{1,0:T(8,128)(2,1)S(1)} %get-tuple-element.60), channel_id=1, source_target_pairs={{0,24},{1,25},{2,26},{3,27},{4,28},{5,29},{6,30},{7,31},{8,0},{9,1... | collective-permute-start | bytes 294920 | tf_op jit(solution)/shard_map/ppermute | solution.py:651
  89.7 3.0 %collective-permute-done.13 = bf16[384,128]{1,0:T(8,128)(2,1)S(1)} collective-permute-done((bf16[384,128]{1,0:T(8,128)(2,1)S(1)}, bf16[384,128]{1,0:T(8,128)(2,1)S(1)}, u32[]{:S(2)}, u32[]{:S(2)}) %collective-permute-start.13) | collective-permute-done | bytes 98336 | tf_op jit(solution)/shard_map/ppermute | solution.py:651
  93.6 2.0 %collective-permute-start.18 = (bf16[320,128]{1,0:T(8,128)(2,1)S(1)}, bf16[320,128]{1,0:T(8,128)(2,1)S(1)}, u32[]{:S(2)}, u32[]{:S(2)}) collective-permute-start(bf16[320,128]{1,0:T(8,128)(2,1)S(1)} %get-tuple-element.57), channel_id=1, source_target_pairs={{0,6},{1,97},{2,0},{3,99},{4,2},{5,101},{6,4},{7,103},{8,14},{9,10... | collective-permute-start | bytes 245768 | tf_op jit(solution)/shard_map/ppermute | solution.py:651
  95.9 1.6 %collective-permute-done.16 = bf16[320,128]{1,0:T(8,128)(2,1)S(1)} collective-permute-done((bf16[320,128]{1,0:T(8,128)(2,1)S(1)}, bf16[320,128]{1,0:T(8,128)(2,1)S(1)}, u32[]{:S(2)}, u32[]{:S(2)}) %collective-permute-start.16) | collective-permute-done | bytes 81952 | tf_op jit(solution)/shard_map/ppermute | solution.py:651
  97.5 3.0 %collective-permute-done.17 = bf16[320,128]{1,0:T(8,128)(2,1)S(1)} collective-permute-done((bf16[320,128]{1,0:T(8,128)(2,1)S(1)}, bf16[320,128]{1,0:T(8,128)(2,1)S(1)}, u32[]{:S(2)}, u32[]{:S(2)}) %collective-permute-start.17) | collective-permute-done | bytes 81952 | tf_op jit(solution)/shard_map/ppermute | solution.py:651
  100.7 2.5 %collective-permute-start.21 = (bf16[1280,128]{1,0:T(8,128)(2,1)S(1)}, bf16[1280,128]{1,0:T(8,128)(2,1)S(1)}, u32[]{:S(2)}, u32[]{:S(2)}) collective-permute-start(bf16[1280,128]{1,0:T(8,128)(2,1)S(1)} %bitcast.98), channel_id=1, source_target_pairs={{0,96},{1,7},{2,98},{3,1},{4,100},{5,3},{6,102},{7,5},{8,104},{9,1... | collective-permute-start | bytes 983048 | tf_op jit(solution)/shard_map/ppermute | solution.py:651
  103.3 1.0 collective-permute-start.20
  104.5 3.5 %collective-permute-done.19 = bf16[1280,128]{1,0:T(8,128)(2,1)S(1)} collective-permute-done((bf16[1280,128]{1,0:T(8,128)(2,1)S(1)}, bf16[1280,128]{1,0:T(8,128)(2,1)S(1)}, u32[]{:S(2)}, u32[]{:S(2)}) %collective-permute-start.19) | collective-permute-done | bytes 327712 | tf_op jit(solution)/shard_map/ppermute | solution.py:651
  108.1 4.1 %collective-permute-done.20 = bf16[1280,128]{1,0:T(8,128)(2,1)S(1)} collective-permute-done((bf16[1280,128]{1,0:T(8,128)(2,1)S(1)}, bf16[1280,128]{1,0:T(8,128)(2,1)S(1)}, u32[]{:S(2)}, u32[]{:S(2)}) %collective-permute-start.20) | collective-permute-done | bytes 327712 | tf_op jit(solution)/shard_map/ppermute | solution.py:651
  112.3 5.3 %collective-permute-start.22 = (bf16[5120,128]{1,0:T(8,128)(2,1)S(1)}, bf16[5120,128]{1,0:T(8,128)(2,1)S(1)}, u32[]{:S(2)}, u32[]{:S(2)}) collective-permute-start(bf16[5120,128]{1,0:T(8,128)(2,1)S(1)} %bitcast.81), channel_id=1, source_target_pairs={{0,1},{1,0},{2,3},{3,2},{4,5},{5,4},{6,7},{7,6},{8,9},{9,8},{10,11... | collective-permute-start | bytes 3932168 | tf_op jit(solution)/shard_map/ppermute | solution.py:699
  117.7 2.7 %collective-permute-done.22.other_ref = bf16[5120,128]{1,0:T(8,128)(2,1)S(1)} collective-permute-done((bf16[5120,128]{1,0:T(8,128)(2,1)S(1)}, bf16[5120,128]{1,0:T(8,128)(2,1)S(1)}, u32[]{:S(2)}, u32[]{:S(2)}) %collective-permute-start.22) | collective-permute-done | bytes 1310752 | tf_op jit(solution)/shard_map/ppermute | solution.py:699
  120.4 9.1 %shard_map.160 = (f32[3,3,256]{2,1,0:T(4,128)}, f32[256,512]{1,0:T(8,128)}, f32[4,512,512]{2,1,0:T(8,128)}, f32[3,3,512]{2,1,0:T(4,128)}, f32[512,256]{1,0:T(8,1...) custom-call(s32[1]{0:T(128)} %bitcast.4.where, ...), custom_call_target="tpu_custom_call" | custom-call | tf_op jit(solution)/shard_map/pallas_call | solution.py:595
  (77 shorter events, 5.0 us)
Async XLA Ops:
  3.8 11.6 %collective-permute-start = (bf16[8,32,256]{2,1,0:T(8,128)(2,1)}, bf16[8,32,256]{2,1,0:T(8,128)(2,1)S(1)}, u32[]{:S(2)}, u32[]{:S(2)}) collective-permute-start(bf16[8,32,256]{2,1,0:T(8,128)(2,1)} %get-tuple-element.29), channel_id=1, source_target_pairs={{0,8},{1,9},{2,10},{3,11},{4,12},{5,13},{6,14},{7,15},{8,16},{9,17... | collective-permute-start | bytes 393224 | tf_op jit(solution)/shard_map/ppermute | solution.py:623
  8.2 7.2 %collective-permute-start.1 = (bf16[8,32,256]{2,1,0:T(8,128)(2,1)}, bf16[8,32,256]{2,1,0:T(8,128)(2,1)S(1)}, u32[]{:S(2)}, u32[]{:S(2)}) collective-permute-start(bf16[8,32,256]{2,1,0:T(8,128)(2,1)} %get-tuple-element.30), channel_id=1, source_target_pairs={{8,0},{9,1},{10,2},{11,3},{12,4},{13,5},{14,6},{15,7},{16,8},{17,9... | collective-permute-start | bytes 393224 | tf_op jit(solution)/shard_map/ppermute | solution.py:623
  9.5 15.5 %collective-permute-start.2 = (bf16[96,8,256]{2,1,0:T(8,128)(2,1)}, bf16[96,8,256]{2,1,0:T(8,128)(2,1)S(1)}, u32[]{:S(2)}, u32[]{:S(2)}) collective-permute-start(bf16[96,8,256]{2,1,0:T(8,128)(2,1)} %get-tuple-element.31), channel_id=1, source_target_pairs={{1,0},{2,1},{3,2},{4,3},{5,4},{6,5},{7,6},{9,8},{10,9},{11,10},{12... | collective-permute-start | bytes 1179656 | tf_op jit(solution)/shard_map/ppermute | solution.py:623
  12.4 12.7 %collective-permute-start.3 = (bf16[96,8,256]{2,1,0:T(8,128)(2,1)}, bf16[96,8,256]{2,1,0:T(8,128)(2,1)}, u32[]{:S(2)}, u32[]{:S(2)}) collective-permute-start(bf16[96,8,256]{2,1,0:T(8,128)(2,1)} %get-tuple-element.32), channel_id=1, source_target_pairs={{0,1},{1,2},{2,3},{3,4},{4,5},{5,6},{6,7},{8,9},{9,10},{10,11},{11... | collective-permute-start | bytes 1179656 | tf_op jit(solution)/shard_map/ppermute | solution.py:623
  15.4 9.6 %copy-start.6 = (bf16[8,32,256]{2,1,0:T(8,128)(2,1)}, bf16[8,32,256]{2,1,0:T(8,128)(2,1)S(1)}, u32[]{:S(2)}) copy-start(bf16[8,32,256]{2,1,0:T(8,128)(2,1)S(1)} %collective-permute-done.top_ref) | copy-start | bytes 393220
  15.4 9.6 %copy-start.7 = (bf16[8,32,256]{2,1,0:T(8,128)(2,1)}, bf16[8,32,256]{2,1,0:T(8,128)(2,1)S(1)}, u32[]{:S(2)}) copy-start(bf16[8,32,256]{2,1,0:T(8,128)(2,1)S(1)} %collective-permute-done.1.bot_ref) | copy-start | bytes 393220
  15.5 6.5 %collective-permute-start.5 = (bf16[16,8,256]{2,1,0:T(8,128)(2,1)S(1)}, bf16[16,8,256]{2,1,0:T(8,128)(2,1)S(1)}, u32[]{:S(2)}, u32[]{:S(2)}) collective-permute-start(bf16[16,8,256]{2,1,0:T(8,128)(2,1)S(1)} %get-tuple-element.55), channel_id=1, source_target_pairs={{0,1},{1,2},{2,3},{3,4},{4,5},{5,6},{6,7},{8,9},{9,10},{10,11},{11... | collective-permute-start | bytes 196616 | tf_op jit(solution)/shard_map/ppermute | solution.py:623
  19.4 5.6 %collective-permute-start.4 = (bf16[16,8,256]{2,1,0:T(8,128)(2,1)S(1)}, bf16[16,8,256]{2,1,0:T(8,128)(2,1)S(1)}, u32[]{:S(2)}, u32[]{:S(2)}) collective-permute-start(bf16[16,8,256]{2,1,0:T(8,128)(2,1)S(1)} %get-tuple-element.56), channel_id=1, source_target_pairs={{1,0},{2,1},{3,2},{4,3},{5,4},{6,5},{7,6},{9,8},{10,9},{11,10},{12... | collective-permute-start | bytes 196616 | tf_op jit(solution)/shard_map/ppermute | solution.py:623
  22.0 3.1 %copy-start.9 = (bf16[16,8,256]{2,1,0:T(8,128)(2,1)}, bf16[16,8,256]{2,1,0:T(8,128)(2,1)S(1)}, u32[]{:S(2)}) copy-start(bf16[16,8,256]{2,1,0:T(8,128)(2,1)S(1)} %collective-permute-done.5.left_ends) | copy-start | bytes 196612
  58.8 3.3 %collective-permute-start.6 = (bf16[5184,128]{1,0:T(8,128)(2,1)}, bf16[5184,128]{1,0:T(8,128)(2,1)S(1)}, u32[]{:S(2)}, u32[]{:S(2)}) collective-permute-start(bf16[5184,128]{1,0:T(8,128)(2,1)} %get-tuple-element.36), channel_id=1, source_target_pairs={{0,1},{1,0},{2,3},{3,2},{4,5},{5,4},{6,7},{7,6},{8,9},{9,8},{10,11... | collective-permute-start | bytes 3981320 | tf_op jit(solution)/shard_map/ppermute | solution.py:690
  64.1 11.5 %collective-permute-start.7 = (bf16[1344,128]{1,0:T(8,128)(2,1)S(1)}, bf16[1344,128]{1,0:T(8,128)(2,1)S(1)}, u32[]{:S(2)}, u32[]{:S(2)}) collective-permute-start(bf16[1344,128]{1,0:T(8,128)(2,1)S(1)} %get-tuple-element.64), channel_id=1, source_target_pairs={{0,32},{1,3},{2,34},{3,5},{4,36},{5,7},{6,38},{7,1},{8,40},{9,11},... | collective-permute-start | bytes 1032200 | tf_op jit(solution)/shard_map/ppermute | solution.py:651
  65.6 10.1 %collective-permute-start.9 = (bf16[1344,128]{1,0:T(8,128)(2,1)S(1)}, bf16[1344,128]{1,0:T(8,128)(2,1)S(1)}, u32[]{:S(2)}, u32[]{:S(2)}) collective-permute-start(bf16[1344,128]{1,0:T(8,128)(2,1)S(1)} %get-tuple-element.65), channel_id=1, source_target_pairs={{0,96},{1,7},{2,98},{3,1},{4,100},{5,3},{6,102},{7,5},{8,104},{9,1... | collective-permute-start | bytes 1032200 | tf_op jit(solution)/shard_map/ppermute | solution.py:651
  67.0 8.6 %collective-permute-start.8 = (bf16[1344,128]{1,0:T(8,128)(2,1)S(1)}, bf16[1344,128]{1,0:T(8,128)(2,1)S(1)}, u32[]{:S(2)}, u32[]{:S(2)}) collective-permute-start(bf16[1344,128]{1,0:T(8,128)(2,1)S(1)} %get-tuple-element.66), channel_id=1, source_target_pairs={{0,64},{1,5},{2,66},{3,7},{4,68},{5,1},{6,70},{7,3},{8,72},{9,13},... | collective-permute-start | bytes 1032200 | tf_op jit(solution)/shard_map/ppermute | solution.py:651
  76.0 4.8 %collective-permute-start.10 = (bf16[384,128]{1,0:T(8,128)(2,1)S(1)}, bf16[384,128]{1,0:T(8,128)(2,1)S(1)}, u32[]{:S(2)}, u32[]{:S(2)}) collective-permute-start(bf16[384,128]{1,0:T(8,128)(2,1)S(1)} %get-tuple-element.61), channel_id=1, source_target_pairs={{0,2},{1,33},{2,4},{3,35},{4,6},{5,37},{6,0},{7,39},{8,10},{9,41},... | collective-permute-start | bytes 294920 | tf_op jit(solution)/shard_map/ppermute | solution.py:651
  77.2 5.8 %collective-permute-start.11 = (bf16[384,128]{1,0:T(8,128)(2,1)S(1)}, bf16[384,128]{1,0:T(8,128)(2,1)S(1)}, u32[]{:S(2)}, u32[]{:S(2)}) collective-permute-start(bf16[384,128]{1,0:T(8,128)(2,1)S(1)} %get-tuple-element.62), channel_id=1, source_target_pairs={{0,4},{1,65},{2,6},{3,67},{4,0},{5,69},{6,2},{7,71},{8,12},{9,73},... | collective-permute-start | bytes 294920 | tf_op jit(solution)/shard_map/ppermute | solution.py:651
  80.0 3.7 %collective-permute-start.12 = (bf16[384,128]{1,0:T(8,128)(2,1)S(1)}, bf16[384,128]{1,0:T(8,128)(2,1)S(1)}, u32[]{:S(2)}, u32[]{:S(2)}) collective-permute-start(bf16[384,128]{1,0:T(8,128)(2,1)S(1)} %get-tuple-element.63), channel_id=1, source_target_pairs={{0,6},{1,97},{2,0},{3,99},{4,2},{5,101},{6,4},{7,103},{8,14},{9,10... | collective-permute-start | bytes 294920 | tf_op jit(solution)/shard_map/ppermute | solution.py:651
  83.8 5.9 %collective-permute-start.14 = (bf16[384,128]{1,0:T(8,128)(2,1)S(1)}, bf16[384,128]{1,0:T(8,128)(2,1)S(1)}, u32[]{:S(2)}, u32[]{:S(2)}) collective-permute-start(bf16[384,128]{1,0:T(8,128)(2,1)S(1)} %get-tuple-element.60), channel_id=1, source_target_pairs={{0,16},{1,17},{2,18},{3,19},{4,20},{5,21},{6,22},{7,23},{8,24},{9,... | collective-permute-start | bytes 294920 | tf_op jit(solution)/shard_map/ppermute | solution.py:651
  87.0 5.7 %collective-permute-start.13 = (bf16[384,128]{1,0:T(8,128)(2,1)S(1)}, bf16[384,128]{1,0:T(8,128)(2,1)S(1)}, u32[]{:S(2)}, u32[]{:S(2)}) collective-permute-start(bf16[384,128]{1,0:T(8,128)(2,1)S(1)} %get-tuple-element.60), channel_id=1, source_target_pairs={{0,8},{1,9},{2,10},{3,11},{4,12},{5,13},{6,14},{7,15},{8,16},{9,17... | collective-permute-start | bytes 294920 | tf_op jit(solution)/shard_map/ppermute | solution.py:651
  87.4 5.3 %collective-permute-start.15 = (bf16[384,128]{1,0:T(8,128)(2,1)S(1)}, bf16[384,128]{1,0:T(8,128)(2,1)S(1)}, u32[]{:S(2)}, u32[]{:S(2)}) collective-permute-start(bf16[384,128]{1,0:T(8,128)(2,1)S(1)} %get-tuple-element.60), channel_id=1, source_target_pairs={{0,24},{1,25},{2,26},{3,27},{4,28},{5,29},{6,30},{7,31},{8,0},{9,1... | collective-permute-start | bytes 294920 | tf_op jit(solution)/shard_map/ppermute | solution.py:651
  92.7 27.6 %copy-start.1 = (f32[256,512]{1,0:T(8,128)S(1)}, f32[256,512]{1,0:T(8,128)}, u32[]{:S(2)}) copy-start(f32[256,512]{1,0:T(8,128)} %refs_1_.1) | copy-start | bytes 1572868
  92.8 27.6 %copy-start.2 = (f32[512,256]{1,0:T(8,128)S(1)}, f32[512,256]{1,0:T(8,128)}, u32[]{:S(2)}) copy-start(f32[512,256]{1,0:T(8,128)} %refs_4_.1) | copy-start | bytes 1572868
  92.9 4.6 %collective-permute-start.16 = (bf16[320,128]{1,0:T(8,128)(2,1)S(1)}, bf16[320,128]{1,0:T(8,128)(2,1)S(1)}, u32[]{:S(2)}, u32[]{:S(2)}) collective-permute-start(bf16[320,128]{1,0:T(8,128)(2,1)S(1)} %get-tuple-element.57), channel_id=1, source_target_pairs={{0,2},{1,33},{2,4},{3,35},{4,6},{5,37},{6,0},{7,39},{8,10},{9,41},... | collective-permute-start | bytes 245768 | tf_op jit(solution)/shard_map/ppermute | solution.py:651
  93.6 6.8 %collective-permute-start.18 = (bf16[320,128]{1,0:T(8,128)(2,1)S(1)}, bf16[320,128]{1,0:T(8,128)(2,1)S(1)}, u32[]{:S(2)}, u32[]{:S(2)}) collective-permute-start(bf16[320,128]{1,0:T(8,128)(2,1)S(1)} %get-tuple-element.57), channel_id=1, source_target_pairs={{0,6},{1,97},{2,0},{3,99},{4,2},{5,101},{6,4},{7,103},{8,14},{9,10... | collective-permute-start | bytes 245768 | tf_op jit(solution)/shard_map/ppermute | solution.py:651
  95.7 4.8 %collective-permute-start.17 = (bf16[320,128]{1,0:T(8,128)(2,1)S(1)}, bf16[320,128]{1,0:T(8,128)(2,1)S(1)}, u32[]{:S(2)}, u32[]{:S(2)}) collective-permute-start(bf16[320,128]{1,0:T(8,128)(2,1)S(1)} %get-tuple-element.57), channel_id=1, source_target_pairs={{0,4},{1,65},{2,6},{3,67},{4,0},{5,69},{6,2},{7,71},{8,12},{9,73},... | collective-permute-start | bytes 245768 | tf_op jit(solution)/shard_map/ppermute | solution.py:651
  100.5 19.9 %copy-start = (f32[2,2,512,512]{3,2,1,0:T(8,128)S(1)}, f32[2,2,512,512]{3,2,1,0:T(8,128)}, u32[]{:S(2)}) copy-start(f32[2,2,512,512]{3,2,1,0:T(8,128)} %param.11) | copy-start | bytes 12582916
  100.5 7.5 %collective-permute-start.19 = (bf16[1280,128]{1,0:T(8,128)(2,1)S(1)}, bf16[1280,128]{1,0:T(8,128)(2,1)S(1)}, u32[]{:S(2)}, u32[]{:S(2)}) collective-permute-start(bf16[1280,128]{1,0:T(8,128)(2,1)S(1)} %bitcast.97), channel_id=1, source_target_pairs={{0,32},{1,3},{2,34},{3,5},{4,36},{5,7},{6,38},{7,1},{8,40},{9,11},... | collective-permute-start | bytes 983048 | tf_op jit(solution)/shard_map/ppermute | solution.py:651
  100.7 11.5 %collective-permute-start.21 = (bf16[1280,128]{1,0:T(8,128)(2,1)S(1)}, bf16[1280,128]{1,0:T(8,128)(2,1)S(1)}, u32[]{:S(2)}, u32[]{:S(2)}) collective-permute-start(bf16[1280,128]{1,0:T(8,128)(2,1)S(1)} %bitcast.98), channel_id=1, source_target_pairs={{0,96},{1,7},{2,98},{3,1},{4,100},{5,3},{6,102},{7,5},{8,104},{9,1... | collective-permute-start | bytes 983048 | tf_op jit(solution)/shard_map/ppermute | solution.py:651
  103.3 8.9 %collective-permute-start.20 = (bf16[1280,128]{1,0:T(8,128)(2,1)S(1)}, bf16[1280,128]{1,0:T(8,128)(2,1)S(1)}, u32[]{:S(2)}, u32[]{:S(2)}) collective-permute-start(bf16[1280,128]{1,0:T(8,128)(2,1)S(1)} %bitcast.99), channel_id=1, source_target_pairs={{0,64},{1,5},{2,66},{3,7},{4,68},{5,1},{6,70},{7,3},{8,72},{9,13},... | collective-permute-start | bytes 983048 | tf_op jit(solution)/shard_map/ppermute | solution.py:651
  104.4 15.9 %copy-start.3 = (f32[3,3,512]{2,1,0:T(4,128)S(1)}, f32[3,3,512]{2,1,0:T(4,128)}, u32[]{:S(2)}) copy-start(f32[3,3,512]{2,1,0:T(4,128)} %refs_3_.1) | copy-start | bytes 55300
  104.4 15.9 %copy-start.4 = (f32[3,3,256]{2,1,0:T(4,128)S(1)}, f32[3,3,256]{2,1,0:T(4,128)}, u32[]{:S(2)}) copy-start(f32[3,3,256]{2,1,0:T(4,128)} %refs_0_.1) | copy-start | bytes 27652
  104.4 15.9 %copy-start.5 = (f32[5]{0:T(128)S(1)}, f32[5]{0:T(128)}, u32[]{:S(2)}) copy-start(f32[5]{0:T(128)} %get-tuple-element.34.sums) | copy-start | bytes 64
  112.3 8.0 %collective-permute-start.22 = (bf16[5120,128]{1,0:T(8,128)(2,1)S(1)}, bf16[5120,128]{1,0:T(8,128)(2,1)S(1)}, u32[]{:S(2)}, u32[]{:S(2)}) collective-permute-start(bf16[5120,128]{1,0:T(8,128)(2,1)S(1)} %bitcast.81), channel_id=1, source_target_pairs={{0,1},{1,0},{2,3},{3,2},{4,5},{5,4},{6,7},{7,6},{8,9},{9,8},{10,11... | collective-permute-start | bytes 3932168 | tf_op jit(solution)/shard_map/ppermute | solution.py:699
  (2 other events, 1.4 us)

commit v4 on v3

--- a/solution.py
+++ b/solution.py
@@ -33,7 +33,7 @@
 
 def tile_kernel(
     limits,
-    x_ref,
+    x_hbm,
     t_hbm,
     top_ref,
     bot_ref,
@@ -47,12 +47,16 @@
     k2_ref,
     p2_full,
     pred_hbm,
+    keep_hbm,
+    send_hbm,
+    sums_ref,
     keep_ref,
     send_ref,
-    sums_ref,
+    x_ref,
     t_ref,
     taps_full,
     p1_ref,
+    p1_half,
     taps_ref,
     p2_ref,
     pred_ref,
@@ -101,30 +105,30 @@
         def _():
             send_ref[at : at + value.shape[0], :] = value
 
-    copies = [
-        pltpu.make_async_copy(t_hbm, t_ref, sems.at[0]),
-        pltpu.make_async_copy(taps_hbm, taps_full, sems.at[1]),
-        pltpu.make_async_copy(pred_ref, pred_hbm, sems.at[2]),
+    large, last = slice(0, small_at), slice(small_at, small_at + SMALL)
+    pairs = [
+        (t_hbm, t_ref),
+        (taps_hbm, taps_full),
+        (pred_ref, pred_hbm),
+        (x_hbm, x_ref),
+        (keep_ref.at[large], keep_hbm.at[large]),
+        (send_ref.at[large], send_hbm.at[large]),
+        (keep_ref.at[last], keep_hbm.at[last]),
+        (send_ref.at[last], send_hbm.at[last]),
     ]
+    copies = [pltpu.make_async_copy(*pair, sems.at[j]) for j, pair in enumerate(pairs)]
+    copies[3].start()
     copies[0].start()
     copies[1].start()
     small[...] = jnp.zeros_like(small)
     p1_ref[...] = p1_full[...].astype(BF16)
+    p1_half[...] = (p1_full[...].astype(BF16).astype(F32) * 0.5).astype(BF16)
     p2_ref[...] = p2_full[...].astype(BF16)
 
     def put(row, count, block, c):
-        xf[c, pl.ds(row, count), 8 : 8 + cols, :] = block.astype(F32)
-
-    for c in range(cb1):
-        put(0, ROWS, top_ref[0:ROWS, :, lanes(c)], c)
-        put(rows + ROWS, ROWS, bot_ref[0:ROWS, :, lanes(c)], c)
-
-    step = 12
-
-    @pl.loop(0, rows // step)
-    def _(n):
-        for c in range(cb1):
-            put(ROWS + n * step, step, x_ref[pl.ds(n * step, step), :, lanes(c)], c)
+        block = block.astype(F32)
+        xf[c, pl.ds(row, count), 8 : 8 + cols, :] = block
+        xf[c, pl.ds(row, count), 24 + cols : 25 + cols, :] = block[:, 0:1, :]
 
     def put_sides(row, count, right, left, c):
         at = pl.ds(row, count)
@@ -132,17 +136,22 @@
         xf[c, at, 8 + cols : 16 + cols, :] = right
         xf[c, at, 16 + cols : 24 + cols, :] = left
         xf[c, at, 7:8, :] = left[:, 7:8, :]
-        xf[c, at, 24 + cols : 25 + cols, :] = xf[c, at, 8:9, :]
-
+
+    step = 12
     for c in range(cb1):
+        put(0, ROWS, top_ref[0:ROWS, :, lanes(c)], c)
+        put(rows + ROWS, ROWS, bot_ref[0:ROWS, :, lanes(c)], c)
         put_sides(0, ROWS, right_ends[0:ROWS, :, lanes(c)], left_ends[0:ROWS, :, lanes(c)], c)
         cut = (slice(ROWS + 2, 2 * ROWS + 2), slice(None), lanes(c))
         put_sides(rows + ROWS, ROWS, right_ends[cut], left_ends[cut], c)
+
+    copies[3].wait()
 
     @pl.loop(0, rows // step)
     def _(n):
         at = pl.ds(n * step, step)
         for c in range(cb1):
+            put(ROWS + n * step, step, x_ref[at, :, lanes(c)], c)
             put_sides(ROWS + n * step, step, right_ref[at, :, lanes(c)], left_ref[at, :, lanes(c)], c)
 
     copies[0].wait()
@@ -181,14 +190,16 @@
             per = [[None] * take for _ in range(4)]
             for i in range(take):
                 e = 2 * (n * take + i) + ROWS - 4
+                near = [
+                    [xf[c, e + s - 1, pl.ds(7 + o, slots, stride=2), :] for o in range(4)]
+                    for s in range(4)
+                ]
                 for r in range(2):
                     total = [None, None]
                     for a in range(3):
-                        at = e + r + a - 1
-                        col = [xf[c, at, pl.ds(7 + o, slots, stride=2), :] for o in range(4)]
                         for q in range(2):
                             for b in range(3):
-                                term = k1_ref[a, b : b + 1, lanes(c)] * col[q + b]
+                                term = k1_ref[a, b : b + 1, lanes(c)] * near[r + a][q + b]
                                 total[q] = term if total[q] is None else total[q] + term
                     for q in range(2):
                         per[2 * r + q][i] = total[q]
@@ -204,8 +215,8 @@
             for ph in range(4)
         ]
         for ph in range(4):
-            act = mm(low[ph], p1_ref[...])
-            out = act * sigmoid(act)
+            act = mm(low[ph], p1_half[...])
+            out = act + act * jnp.tanh(act)
             out_e[ph, pl.ds(n * (take * slots), take * slots), :] = out.astype(BF16)
             own = out.reshape(take, slots, hid)[:, 0:hc, :].reshape(take * hc, hid)
             out_own[ph, pl.ds(n * (take * hc), take * hc), :] = own.astype(BF16)
@@ -260,12 +271,16 @@
     def _(n):
         pre = []
         for c in range(cb2):
-            total = None
-            for a in range(3):
+            subs = []
+            for first in range(0, part, 5):
+                total = None
                 for b in range(3):
-                    at = pl.ds(n * part + a, part)
-                    term = k2_ref[a, b : b + 1, lanes(c)] * co[c, at, 7 + b : 7 + b + slots, :]
-                    total = term if total is None else total + term
+                    col = co[c, pl.ds(n * part + first, 7), 7 + b : 7 + b + slots, :]
+                    for a in range(3):
+                        term = k2_ref[a, b : b + 1, lanes(c)] * col[a : a + 5]
+                        total = term if total is None else total + term
+                subs.append(total)
+            total = jnp.concatenate(subs, axis=0)
             pre.append(total.reshape(part * slots, LANES))
         gate = [sigmoid(p) for p in pre]
         out = [p * g for p, g in zip(pre, gate)]
@@ -336,9 +351,9 @@
         for c in range(cb2):
             emit(ph // 2, (ph % 2) * st_rows + c * hid, gst[:, lanes(c)])
         back = mm_t(bc[...], taps_ref[ph])
-        act = mm(pre_own[ph, own_rows, :], p1_ref[...])
-        gate = sigmoid(act)
-        slope = (back * (gate * (1.0 + act * (1.0 - gate)))).astype(BF16)
+        act = mm(pre_own[ph, own_rows, :], p1_half[...])
+        turn = jnp.tanh(act)
+        slope = (back * ((0.5 + 0.5 * turn) * (1.0 + act * (1.0 - turn)))).astype(BF16)
         term = t_mm(pre_own[ph, own_rows, :], slope)
         gp1 = term if ph == 0 else gp1 + term
         back_pre = mm_t(slope, p1_ref[...])
@@ -347,16 +362,18 @@
 
     for c in range(cb2):
         emit(2 * c // cb2, p1_at + (c % (cb2 // 2)) * chan, gp1[:, lanes(c)])
+    copies[4].start()
+    copies[5].start()
 
     for c in range(cb1):
 
         def body(n, acc, c=c):
             acc = list(acc)
-            grads = [[bp[ph, c, 2 * n + i] for ph in range(4)] for i in range(2)]
-            for s in range(6):
-                e = 4 * n + ROWS + s - 1
+            grads = [[bp[ph, c, 4 * n + i] for ph in range(4)] for i in range(4)]
+            for s in range(10):
+                e = 8 * n + ROWS + s - 1
                 col = [xf[c, e, pl.ds(7 + o, hc, stride=2), :] for o in range(4)]
-                for i in range(2):
+                for i in range(4):
                     for r in range(2):
                         a = s - 2 * i - r
                         if 0 <= a < 3:
@@ -366,15 +383,18 @@
                                     acc[3 * a + b] = acc[3 * a + b] + (p[0:8] + p[8:16])
             return tuple(acc)
 
-        acc = lax.fori_loop(0, hr // 2, body, tuple(jnp.zeros((8, LANES), F32) for _ in range(9)))
+        acc = lax.fori_loop(0, hr // 4, body, tuple(jnp.zeros((8, LANES), F32) for _ in range(9)))
         for j in range(9):
             at = 9 * c + j
             small[at : at + 1, :] = jnp.sum(acc[j], axis=0, keepdims=True)
 
 
-    copies[2].wait()
     for ref in (keep_ref, send_ref):
         ref[small_at : small_at + SMALL, :] = small[...].astype(BF16)
+    copies[6].start()
+    copies[7].start()
+    for j in (2, 4, 5, 6, 7):
+        copies[j].wait()
 
 
 def vmem():
@@ -404,18 +424,22 @@
             jax.ShapeDtypeStruct((grads, LANES), BF16),
             jax.ShapeDtypeStruct((5,), F32),
         ),
-        in_specs=[smem(), vmem(), hbm()]
+        in_specs=[smem(), hbm(), hbm()]
         + [vmem()] * (len(halos) + 2)
         + [hbm(), vmem(), vmem()],
-        out_specs=[hbm(), vmem(), vmem(), smem()],
+        out_specs=[hbm(), hbm(), hbm(), smem()],
         scratch_shapes=[
+            pltpu.VMEM((grads, LANES), BF16),
+            pltpu.VMEM((grads, LANES), BF16),
+            pltpu.VMEM(x.shape, BF16),
             pltpu.VMEM(t.shape, BF16),
             pltpu.VMEM(taps.shape, F32),
+            pltpu.VMEM(p1.shape, BF16),
             pltpu.VMEM(p1.shape, BF16),
             pltpu.VMEM(taps.shape, BF16),
             pltpu.VMEM(p2.shape, BF16),
             pltpu.VMEM(x.shape, BF16),
-            pltpu.SemaphoreType.DMA((3,)),
+            pltpu.SemaphoreType.DMA((8,)),
             pltpu.VMEM((cb1, rows + 2 * ROWS, cols + 32, LANES), F32),
             pltpu.VMEM((cb1, 8, cols + 32, LANES), F32),
             pltpu.VMEM((cb1, hr + 2, slots, LANES), F32),
@@ -441,9 +465,9 @@
     up[...] = jnp.concatenate([xt[0:ROWS], tt[0:2]], axis=0)
     down[...] = jnp.concatenate([xb[8 - ROWS : 8], tb[6:8]], axis=0)
     col = lax.broadcasted_iota(jnp.int32, ahead.shape, 1)
-    x, t = xl[...].astype(F32)[:, 0:8], tl[...].astype(F32)[:, 0:8]
+    x, t = xl[:, 0:8, :].astype(F32), tl[:, 0:8, :].astype(F32)
     ahead[...] = jnp.where((col >= 5) & (col < 7), pltpu.roll(t, 5, 1), x).astype(BF16)
-    x, t = xr[...].astype(F32)[:, 8:16], tr[...].astype(F32)[:, 8:16]
+    x, t = xr[:, 8:16, :].astype(F32), tr[:, 8:16, :].astype(F32)
     back[...] = jnp.where((col >= 1) & (col < 3), pltpu.roll(t, 3, 1), x).astype(BF16)
 
 
@@ -513,40 +537,44 @@
     sizes = (9 * chan, chan * hid, parts * hid * hid, 9 * hid, chan * hid)
 
     def root(v):
-        v = jnp.full((8, LANES), v, F32)
         r = lax.rsqrt(v)
-        r = r * (1.5 - 0.5 * v * r * r)
-        return (v * r)[0, 0]
+        return v * (r * (1.5 - 0.5 * v * r * r))
 
     def squares(at, count):
-        acc = jnp.zeros((8, LANES), F32)
-        for half in range(2):
-
-            def body(n, acc, half=half):
-                v = g[half, pl.ds(at + n * 128, 128), :].astype(F32)
-                return acc + jnp.sum((v * v).reshape(16, 8, LANES), axis=0)
-
-            acc = lax.fori_loop(0, count // 128, body, acc)
-        return jnp.sum(acc)
+        block = 256
+
+        def body(n, acc):
+            rows = pl.ds(pl.multiple_of(at + n * block, block), block)
+            out = []
+            for half, ref, a in ((core, own_ref, acc[0]), (1 - core, other_ref, acc[1])):
+                v = ref[rows, :]
+                g[half, rows, :] = v
+                v = v.astype(F32)
+                out.append(a + jnp.sum((v * v).reshape(block // 8, 8, LANES), axis=0))
+            return tuple(out)
+
+        zero = jnp.zeros((8, LANES), F32)
+        both = lax.fori_loop(0, count // block, body, (zero, zero))
+        return jnp.sum(both[0] + both[1], keepdims=True)
 
     def set_scale(j, total):
-        scale[j] = 1.0 / root(total / sizes[j] + EPS)
-        scale[5 + j] = RATE * root(sums[j] / sizes[j] + EPS)
+        mean = jnp.broadcast_to(total, (1, LANES)) / sizes[j]
+        scale[j : j + 1, :] = 1.0 / root(mean + EPS)
+        mean = jnp.full((1, LANES), sums[j] / sizes[j], F32)
+        scale[5 + j : 6 + j, :] = RATE * root(mean + EPS)
 
     @pl.when(step == 0)
     def _():
         for n in range(parts * per):
             fetch(n).start()
-        g[core] = own_ref[...]
-        g[1 - core] = other_ref[...]
         small[...] = small_ref[...].astype(F32)
         v = small[0 : 9 * cb1, :]
-        set_scale(0, jnp.sum(v * v))
+        set_scale(0, jnp.sum(v * v, keepdims=True))
         v = small[9 * cb1 : 9 * (cb1 + cb2), :]
-        set_scale(3, jnp.sum(v * v))
+        set_scale(3, jnp.sum(v * v, keepdims=True))
         set_scale(1, squares(p1_at, p1_rows // 2))
+        set_scale(4, squares(p2_at, p2_rows // 2))
         set_scale(2, squares(0, 2 * st_rows))
-        set_scale(4, squares(p2_at, p2_rows // 2))
         for j, first, blocks, w, new, out in (
             (0, 0, cb1, k1_ref, nk1_ref, sk1_ref),
             (3, 9 * cb1, cb2, k2_ref, nk2_ref, sk2_ref),
@@ -555,30 +583,30 @@
                 cut = slice(c * LANES, (c + 1) * LANES)
                 for r in range(3):
                     at = first + 9 * c + 3 * r
-                    normed = small[at : at + 3, :] * scale[j]
+                    normed = small[at : at + 3, :] * scale[j : j + 1, :]
                     out[r, :, cut] = normed
-                    new[r, :, cut] = w[r, :, cut] - scale[5 + j] * normed
+                    new[r, :, cut] = w[r, :, cut] - scale[5 + j : 6 + j, :] * normed
         for c in range(cb2):
             cut = slice(c * LANES, (c + 1) * LANES)
             at = p1_at + (c % (cb2 // 2)) * chan
-            normed = g[2 * c // cb2, at : at + chan, :].astype(F32) * scale[1]
+            normed = g[2 * c // cb2, at : at + chan, :].astype(F32) * scale[1:2, :]
             sp1_ref[:, cut] = normed
-            np1_ref[:, cut] = p1_ref[:, cut] - scale[6] * normed
+            np1_ref[:, cut] = p1_ref[:, cut] - scale[6:7, :] * normed
         for c in range(cb1):
             cut = slice(c * LANES, (c + 1) * LANES)
             at = p2_at + (c % (cb1 // 2)) * hid
-            normed = g[2 * c // cb1, at : at + hid, :].astype(F32) * scale[4]
+            normed = g[2 * c // cb1, at : at + hid, :].astype(F32) * scale[4:5, :]
             sp2_ref[:, cut] = normed
-            np2_ref[:, cut] = p2_ref[:, cut] - scale[9] * normed
+            np2_ref[:, cut] = p2_ref[:, cut] - scale[9:10, :] * normed
 
     fetch(step).wait()
     ph = step // per
     for c in range(cb2):
         cut = slice(c * LANES, (c + 1) * LANES)
         at = (ph % 2) * st_rows + c * hid + (step % per) * block
-        normed = g[ph // 2, pl.ds(at, block), :].astype(F32) * scale[2]
+        normed = g[ph // 2, pl.ds(at, block), :].astype(F32) * scale[2:3, :]
         sst_ref[0, :, cut] = normed
-        nst_ref[0, :, cut] = st_ref[step, :, cut] - scale[7] * normed
+        nst_ref[0, :, cut] = st_ref[step, :, cut] - scale[7:8, :] * normed
 
 
 def update(where, sums, small, own, other, k1, p1, taps, k2, p2):
@@ -604,7 +632,7 @@
         scratch_shapes=[
             pltpu.VMEM((2,) + own.shape, BF16),
             pltpu.VMEM((SMALL, LANES), F32),
-            pltpu.SMEM((10,), F32),
+            pltpu.VMEM((16, LANES), F32),
             pltpu.VMEM((4 * per, block, hid), F32),
             pltpu.SemaphoreType.DMA((4 * per,)),
         ],
@@ -630,6 +658,7 @@
         self.names, self.sizes = names, sizes
         self.count = sizes[names[0]]
         assert sizes[names[1]] == self.count
+        self.steps = range(1, self.count)
         self.me = jnp.where(lax.axis_index("tx") % 2 == 0, place[names[0]], place[names[1]])
 
     def send(self, block, step):
@@ -655,12 +684,12 @@
         shares = block.reshape((n, -1, LANES))
         share = lax.dynamic_index_in_dim(shares, self.me, 0, False)
         cut = share.shape[0]
-        got = []
-        for d in range(1, n):
+        got = {}
+        for d in self.steps:
             out = lax.dynamic_index_in_dim(shares, (self.me + d) % n, 0, False)
-            got.append(self.send(jnp.concatenate([out, extra], axis=0), d))
-        total = sum([g[:cut].astype(F32) for g in got], share.astype(F32))
-        return total.astype(BF16), self.added([extra] + [g[cut:] for g in got])
+            got[d] = self.send(jnp.concatenate([out, extra], axis=0), d)
+        total = sum([g[:cut].astype(F32) for g in got.values()], share.astype(F32))
+        return total.astype(BF16), self.added([extra] + [got[d][cut:] for d in range(1, n)])
 
     def added(self, parts):
         n = self.count
@@ -672,13 +701,14 @@
         return total.astype(BF16)
 
     def reduce(self, block):
-        return self.added([block] + [self.send(block, d) for d in range(1, self.count)])
+        got = {d: self.send(block, d) for d in self.steps}
+        return self.added([block] + [got[d] for d in range(1, self.count)])
 
     def gather(self, share):
         n = self.count
         out = jnp.zeros((n,) + share.shape, share.dtype)
         out = lax.dynamic_update_index_in_dim(out, share, self.me, 0)
-        for d in range(1, n):
+        for d in self.steps:
             got = self.send(share, d)
             out = lax.dynamic_update_index_in_dim(out, got, (self.me + n - d) % n, 0)
         return out.reshape(-1, LANES)

time: 130 us -> 128 us (0.985)
  Pallas kernels: 45.3 us -> 43.6 us
where the time goes in v4:
time: 128 us
  starting transfers between devices  44.2 us (35%)
  Pallas kernels  43.6 us (34%)
  waiting for transfers between devices  34.3 us (27%)
  other arithmetic  2.21 us (2%)
  local copies, waits for them, and re-layouts  2.09 us (2%)
  between operations  1.34 us (1%)
    pallas_call x1, Pallas kernels, tile_step(): pl.pallas_call(tile_kernel, out_shape=(jax.ShapeDtypeStruct(x.shape, BF16...  32.2 us
    ppermute x15, waiting for transfers between devices, send(): return lax.ppermute(block, ('rep', 'ty', 'tx'), pairs)  25.4 us
    ppermute x15, starting transfers between devices, send(): return lax.ppermute(block, ('rep', 'ty', 'tx'), pairs)  21.4 us
    ppermute x6, starting transfers between devices, shift(): return lax.ppermute(block, ('ty', 'tx'), pairs)  17.4 us
    pallas_call x1, Pallas kernels, update(): pl.pallas_call(update_kernel, grid=(4 * per,), out_shape=shapes + shapes,...  8.23 us
    ppermute x1, starting transfers between devices, reduced(): return (small, share, lax.ppermute(share, 'tx', cores))  5.39 us
    pallas_call x1, Pallas kernels, edges(): pl.pallas_call(edges_kernel, grid=(1,), out_shape=[jax.ShapeDtypeStruct(s...  3.17 us
    ppermute x1, waiting for transfers between devices, reduced(): got = lax.ppermute(send, 'tx', cores)  3.17 us
  transfers between devices with their start and end apart: 23, of which 11 were waited for; matrix products, arithmetic and copies ran while one was open for 1% of the time, Pallas kernels for 0%

profile of v4, /device:TPU:1, one launch (start us, length us, event | category | flops | bytes accessed | tf_op | source)
XLA Modules:
  0.0 127.8 jit_solution(1991503817225122791)
XLA Ops:
  0.6 3.2 %shard_map.158 = (bf16[8,32,256]{2,1,0:T(8,128)(2,1)}, bf16[8,32,256]{2,1,0:T(8,128)(2,1)}, bf16[96,8,256]{2,1,0:T(8,128)(2,1)}, bf16[96,8,256]{2,1,0:T(8,128)(2,1)}) custom-call(bf16[96,32,256]{2,1,0:T(8,128)(2,1)} %bitcast.85, bf16[96,32,256]{2,1,0:T(8,128)(2,1)} %bitcast.90, bf16[96,32,256]{2,1,0:T(8,128)(2,1)} %bitcast.86, ...), custom_call_target="tpu_custom_call" | custom-call | tf_op jit(solution)/shard_map/pallas_call | solution.py:483
  3.8 4.4 %collective-permute-start = (bf16[8,32,256]{2,1,0:T(8,128)(2,1)}, bf16[8,32,256]{2,1,0:T(8,128)(2,1)S(1)}, u32[]{:S(2)}, u32[]{:S(2)}) collective-permute-start(bf16[8,32,256]{2,1,0:T(8,128)(2,1)} %get-tuple-element.29), channel_id=1, source_target_pairs={{0,8},{1,9},{2,10},{3,11},{4,12},{5,13},{6,14},{7,15},{8,16},{9,17... | collective-permute-start | bytes 393224 | tf_op jit(solution)/shard_map/ppermute | solution.py:651
  8.2 1.3 %collective-permute-start.1 = (bf16[8,32,256]{2,1,0:T(8,128)(2,1)}, bf16[8,32,256]{2,1,0:T(8,128)(2,1)S(1)}, u32[]{:S(2)}, u32[]{:S(2)}) collective-permute-start(bf16[8,32,256]{2,1,0:T(8,128)(2,1)} %get-tuple-element.30), channel_id=1, source_target_pairs={{8,0},{9,1},{10,2},{11,3},{12,4},{13,5},{14,6},{15,7},{16,8},{17,9... | collective-permute-start | bytes 393224 | tf_op jit(solution)/shard_map/ppermute | solution.py:651
  9.5 2.9 %collective-permute-start.2 = (bf16[96,8,256]{2,1,0:T(8,128)(2,1)}, bf16[96,8,256]{2,1,0:T(8,128)(2,1)S(1)}, u32[]{:S(2)}, u32[]{:S(2)}) collective-permute-start(bf16[96,8,256]{2,1,0:T(8,128)(2,1)} %get-tuple-element.31), channel_id=1, source_target_pairs={{1,0},{2,1},{3,2},{4,3},{5,4},{6,5},{7,6},{9,8},{10,9},{11,10},{12... | collective-permute-start | bytes 1179656 | tf_op jit(solution)/shard_map/ppermute | solution.py:651
  12.4 3.0 %collective-permute-start.3 = (bf16[96,8,256]{2,1,0:T(8,128)(2,1)}, bf16[96,8,256]{2,1,0:T(8,128)(2,1)}, u32[]{:S(2)}, u32[]{:S(2)}) collective-permute-start(bf16[96,8,256]{2,1,0:T(8,128)(2,1)} %get-tuple-element.32), channel_id=1, source_target_pairs={{0,1},{1,2},{2,3},{3,4},{4,5},{5,6},{6,7},{8,9},{9,10},{10,11},{11... | collective-permute-start | bytes 1179656 | tf_op jit(solution)/shard_map/ppermute | solution.py:651
  15.5 3.9 %collective-permute-start.5 = (bf16[16,8,256]{2,1,0:T(8,128)(2,1)S(1)}, bf16[16,8,256]{2,1,0:T(8,128)(2,1)S(1)}, u32[]{:S(2)}, u32[]{:S(2)}) collective-permute-start(bf16[16,8,256]{2,1,0:T(8,128)(2,1)S(1)} %get-tuple-element.55), channel_id=1, source_target_pairs={{0,1},{1,2},{2,3},{3,4},{4,5},{5,6},{6,7},{8,9},{9,10},{10,11},{11... | collective-permute-start | bytes 196616 | tf_op jit(solution)/shard_map/ppermute | solution.py:651
  19.4 1.9 %collective-permute-start.4 = (bf16[16,8,256]{2,1,0:T(8,128)(2,1)S(1)}, bf16[16,8,256]{2,1,0:T(8,128)(2,1)S(1)}, u32[]{:S(2)}, u32[]{:S(2)}) collective-permute-start(bf16[16,8,256]{2,1,0:T(8,128)(2,1)S(1)} %get-tuple-element.56), channel_id=1, source_target_pairs={{1,0},{2,1},{3,2},{4,3},{5,4},{6,5},{7,6},{9,8},{10,9},{11,10},{12... | collective-permute-start | bytes 196616 | tf_op jit(solution)/shard_map/ppermute | solution.py:651
  22.0 3.0 %collective-permute-done.4.right_ends = bf16[16,8,256]{2,1,0:T(8,128)(2,1)S(1)} collective-permute-done((bf16[16,8,256]{2,1,0:T(8,128)(2,1)S(1)}, bf16[16,8,256]{2,1,0:T(8,128)(2,1)S(1)}, u32[]{:S(2)}, u32[]{:S(2)}) %collective-permute-start.4) | collective-permute-done | bytes 65568 | tf_op jit(solution)/shard_map/ppermute | solution.py:651
  25.8 32.2 %shard_map.159 = (bf16[96,32,256]{2,1,0:T(8,128)(2,1)}, bf16[5184,128]{1,0:T(8,128)(2,1)}, bf16[5184,128]{1,0:T(8,128)(2,1)}, f32[5]{0:T(128)}) custom-call(s32[5]{0:T(128)} %stack.66.limits, bf16[96,32,256]{2,1,0:T(8,128)(2,1)} %bitcast.89, bf16[96,32,256]{2,1,0:T(8,128)(2,1)} %bitcast.94, bf16[8,32,256]{2,1,0:T(8,128)(2,1)} %copy-done.6, ...), custom_call_target="tpu_custom_call" | custom-call | flops 8999999488 | bytes 20000000 | tf_op jit(solution)/shard_map/pallas_call | solution.py:419
  58.2 3.2 %collective-permute-done.6 = bf16[5184,128]{1,0:T(8,128)(2,1)S(1)} collective-permute-done((bf16[5184,128]{1,0:T(8,128)(2,1)}, bf16[5184,128]{1,0:T(8,128)(2,1)S(1)}, u32[]{:S(2)}, u32[]{:S(2)}) %collective-permute-start.6) | collective-permute-done | bytes 1327136 | tf_op jit(solution)/shard_map/ppermute | solution.py:720
  61.3 1.7 %add_convert_fusion = bf16[5184,128]{1,0:T(8,128)(2,1)S(1)} fusion(bf16[5184,128]{1,0:T(8,128)(2,1)S(1)} %collective-permute-done.6, bf16[5184,128]{1,0:T(8,128)(2,1)} %get-tuple-element.35), kind=kLoop, calls=%fused_computation | loop fusion | flops 2654208 | bytes 3981312 | tf_op jit(solution)/shard_map/convert_element_type | solution.py:721
  63.3 1.3 %collective-permute-start.7 = (bf16[1344,128]{1,0:T(8,128)(2,1)S(1)}, bf16[1344,128]{1,0:T(8,128)(2,1)S(1)}, u32[]{:S(2)}, u32[]{:S(2)}) collective-permute-start(bf16[1344,128]{1,0:T(8,128)(2,1)S(1)} %get-tuple-element.64), channel_id=1, source_target_pairs={{0,32},{1,3},{2,34},{3,5},{4,36},{5,7},{6,38},{7,1},{8,40},{9,11},... | collective-permute-start | bytes 1032200 | tf_op jit(solution)/shard_map/ppermute | solution.py:680
  64.5 1.5 %collective-permute-start.9 = (bf16[1344,128]{1,0:T(8,128)(2,1)S(1)}, bf16[1344,128]{1,0:T(8,128)(2,1)S(1)}, u32[]{:S(2)}, u32[]{:S(2)}) collective-permute-start(bf16[1344,128]{1,0:T(8,128)(2,1)S(1)} %get-tuple-element.65), channel_id=1, source_target_pairs={{0,96},{1,7},{2,98},{3,1},{4,100},{5,3},{6,102},{7,5},{8,104},{9,1... | collective-permute-start | bytes 1032200 | tf_op jit(solution)/shard_map/ppermute | solution.py:680
  66.0 1.2 collective-permute-start.8
  67.3 7.4 %collective-permute-done.7 = bf16[1344,128]{1,0:T(8,128)(2,1)S(1)} collective-permute-done((bf16[1344,128]{1,0:T(8,128)(2,1)S(1)}, bf16[1344,128]{1,0:T(8,128)(2,1)S(1)}, u32[]{:S(2)}, u32[]{:S(2)}) %collective-permute-start.7) | collective-permute-done | bytes 344096 | tf_op jit(solution)/shard_map/ppermute | solution.py:680
  75.0 1.2 collective-permute-start.10
  76.2 2.8 %collective-permute-start.11 = (bf16[384,128]{1,0:T(8,128)(2,1)S(1)}, bf16[384,128]{1,0:T(8,128)(2,1)S(1)}, u32[]{:S(2)}, u32[]{:S(2)}) collective-permute-start(bf16[384,128]{1,0:T(8,128)(2,1)S(1)} %get-tuple-element.62), channel_id=1, source_target_pairs={{0,4},{1,65},{2,6},{3,67},{4,0},{5,69},{6,2},{7,71},{8,12},{9,73},... | collective-permute-start | bytes 294920 | tf_op jit(solution)/shard_map/ppermute | solution.py:680
  79.0 0.8 collective-permute-start.12
  79.8 2.2 %collective-permute-done.11 = bf16[384,128]{1,0:T(8,128)(2,1)S(1)} collective-permute-done((bf16[384,128]{1,0:T(8,128)(2,1)S(1)}, bf16[384,128]{1,0:T(8,128)(2,1)S(1)}, u32[]{:S(2)}, u32[]{:S(2)}) %collective-permute-start.11) | collective-permute-done | bytes 98336 | tf_op jit(solution)/shard_map/ppermute | solution.py:680
  82.8 3.2 %collective-permute-start.14 = (bf16[384,128]{1,0:T(8,128)(2,1)S(1)}, bf16[384,128]{1,0:T(8,128)(2,1)S(1)}, u32[]{:S(2)}, u32[]{:S(2)}) collective-permute-start(bf16[384,128]{1,0:T(8,128)(2,1)S(1)} %get-tuple-element.60), channel_id=1, source_target_pairs={{0,16},{1,17},{2,18},{3,19},{4,20},{5,21},{6,22},{7,23},{8,24},{9,... | collective-permute-start | bytes 294920 | tf_op jit(solution)/shard_map/ppermute | solution.py:680
  86.4 2.3 %collective-permute-start.15 = (bf16[384,128]{1,0:T(8,128)(2,1)S(1)}, bf16[384,128]{1,0:T(8,128)(2,1)S(1)}, u32[]{:S(2)}, u32[]{:S(2)}) collective-permute-start(bf16[384,128]{1,0:T(8,128)(2,1)S(1)} %get-tuple-element.60), channel_id=1, source_target_pairs={{0,24},{1,25},{2,26},{3,27},{4,28},{5,29},{6,30},{7,31},{8,0},{9,1... | collective-permute-start | bytes 294920 | tf_op jit(solution)/shard_map/ppermute | solution.py:680
  88.7 3.0 %collective-permute-done.13 = bf16[384,128]{1,0:T(8,128)(2,1)S(1)} collective-permute-done((bf16[384,128]{1,0:T(8,128)(2,1)S(1)}, bf16[384,128]{1,0:T(8,128)(2,1)S(1)}, u32[]{:S(2)}, u32[]{:S(2)}) %collective-permute-start.13) | collective-permute-done | bytes 98336 | tf_op jit(solution)/shard_map/ppermute | solution.py:680
  92.6 2.0 %collective-permute-start.18 = (bf16[320,128]{1,0:T(8,128)(2,1)S(1)}, bf16[320,128]{1,0:T(8,128)(2,1)S(1)}, u32[]{:S(2)}, u32[]{:S(2)}) collective-permute-start(bf16[320,128]{1,0:T(8,128)(2,1)S(1)} %get-tuple-element.57), channel_id=1, source_target_pairs={{0,6},{1,97},{2,0},{3,99},{4,2},{5,101},{6,4},{7,103},{8,14},{9,10... | collective-permute-start | bytes 245768 | tf_op jit(solution)/shard_map/ppermute | solution.py:680
  94.9 1.5 %collective-permute-done.16 = bf16[320,128]{1,0:T(8,128)(2,1)S(1)} collective-permute-done((bf16[320,128]{1,0:T(8,128)(2,1)S(1)}, bf16[320,128]{1,0:T(8,128)(2,1)S(1)}, u32[]{:S(2)}, u32[]{:S(2)}) %collective-permute-start.16) | collective-permute-done | bytes 81952 | tf_op jit(solution)/shard_map/ppermute | solution.py:680
  96.5 3.0 %collective-permute-done.17 = bf16[320,128]{1,0:T(8,128)(2,1)S(1)} collective-permute-done((bf16[320,128]{1,0:T(8,128)(2,1)S(1)}, bf16[320,128]{1,0:T(8,128)(2,1)S(1)}, u32[]{:S(2)}, u32[]{:S(2)}) %collective-permute-start.17) | collective-permute-done | bytes 81952 | tf_op jit(solution)/shard_map/ppermute | solution.py:680
  99.8 2.5 %collective-permute-start.21 = (bf16[1280,128]{1,0:T(8,128)(2,1)S(1)}, bf16[1280,128]{1,0:T(8,128)(2,1)S(1)}, u32[]{:S(2)}, u32[]{:S(2)}) collective-permute-start(bf16[1280,128]{1,0:T(8,128)(2,1)S(1)} %bitcast.98), channel_id=1, source_target_pairs={{0,96},{1,7},{2,98},{3,1},{4,100},{5,3},{6,102},{7,5},{8,104},{9,1... | collective-permute-start | bytes 983048 | tf_op jit(solution)/shard_map/ppermute | solution.py:680
  102.3 1.0 collective-permute-start.20
  103.5 3.5 %collective-permute-done.19 = bf16[1280,128]{1,0:T(8,128)(2,1)S(1)} collective-permute-done((bf16[1280,128]{1,0:T(8,128)(2,1)S(1)}, bf16[1280,128]{1,0:T(8,128)(2,1)S(1)}, u32[]{:S(2)}, u32[]{:S(2)}) %collective-permute-start.19) | collective-permute-done | bytes 327712 | tf_op jit(solution)/shard_map/ppermute | solution.py:680
  107.1 4.1 %collective-permute-done.20 = bf16[1280,128]{1,0:T(8,128)(2,1)S(1)} collective-permute-done((bf16[1280,128]{1,0:T(8,128)(2,1)S(1)}, bf16[1280,128]{1,0:T(8,128)(2,1)S(1)}, u32[]{:S(2)}, u32[]{:S(2)}) %collective-permute-start.20) | collective-permute-done | bytes 327712 | tf_op jit(solution)/shard_map/ppermute | solution.py:680
  111.3 5.4 %collective-permute-start.22 = (bf16[5120,128]{1,0:T(8,128)(2,1)S(1)}, bf16[5120,128]{1,0:T(8,128)(2,1)S(1)}, u32[]{:S(2)}, u32[]{:S(2)}) collective-permute-start(bf16[5120,128]{1,0:T(8,128)(2,1)S(1)} %bitcast.81), channel_id=1, source_target_pairs={{0,1},{1,0},{2,3},{3,2},{4,5},{5,4},{6,7},{7,6},{8,9},{9,8},{10,11... | collective-permute-start | bytes 3932168 | tf_op jit(solution)/shard_map/ppermute | solution.py:729
  116.7 2.7 %collective-permute-done.22.other_ref = bf16[5120,128]{1,0:T(8,128)(2,1)S(1)} collective-permute-done((bf16[5120,128]{1,0:T(8,128)(2,1)S(1)}, bf16[5120,128]{1,0:T(8,128)(2,1)S(1)}, u32[]{:S(2)}, u32[]{:S(2)}) %collective-permute-start.22) | collective-permute-done | bytes 1310752 | tf_op jit(solution)/shard_map/ppermute | solution.py:729
  119.4 8.2 %shard_map.160 = (f32[3,3,256]{2,1,0:T(4,128)}, f32[256,512]{1,0:T(8,128)}, f32[4,512,512]{2,1,0:T(8,128)}, f32[3,3,512]{2,1,0:T(4,128)}, f32[512,256]{1,0:T(8,1...) custom-call(s32[1]{0:T(128)} %bitcast.4.where, ...), custom_call_target="tpu_custom_call" | custom-call | tf_op jit(solution)/shard_map/pallas_call | solution.py:623
  (77 shorter events, 5.1 us)
Async XLA Ops:
  3.8 11.6 %collective-permute-start = (bf16[8,32,256]{2,1,0:T(8,128)(2,1)}, bf16[8,32,256]{2,1,0:T(8,128)(2,1)S(1)}, u32[]{:S(2)}, u32[]{:S(2)}) collective-permute-start(bf16[8,32,256]{2,1,0:T(8,128)(2,1)} %get-tuple-element.29), channel_id=1, source_target_pairs={{0,8},{1,9},{2,10},{3,11},{4,12},{5,13},{6,14},{7,15},{8,16},{9,17... | collective-permute-start | bytes 393224 | tf_op jit(solution)/shard_map/ppermute | solution.py:651
  8.2 7.2 %collective-permute-start.1 = (bf16[8,32,256]{2,1,0:T(8,128)(2,1)}, bf16[8,32,256]{2,1,0:T(8,128)(2,1)S(1)}, u32[]{:S(2)}, u32[]{:S(2)}) collective-permute-start(bf16[8,32,256]{2,1,0:T(8,128)(2,1)} %get-tuple-element.30), channel_id=1, source_target_pairs={{8,0},{9,1},{10,2},{11,3},{12,4},{13,5},{14,6},{15,7},{16,8},{17,9... | collective-permute-start | bytes 393224 | tf_op jit(solution)/shard_map/ppermute | solution.py:651
  9.5 15.5 %collective-permute-start.2 = (bf16[96,8,256]{2,1,0:T(8,128)(2,1)}, bf16[96,8,256]{2,1,0:T(8,128)(2,1)S(1)}, u32[]{:S(2)}, u32[]{:S(2)}) collective-permute-start(bf16[96,8,256]{2,1,0:T(8,128)(2,1)} %get-tuple-element.31), channel_id=1, source_target_pairs={{1,0},{2,1},{3,2},{4,3},{5,4},{6,5},{7,6},{9,8},{10,9},{11,10},{12... | collective-permute-start | bytes 1179656 | tf_op jit(solution)/shard_map/ppermute | solution.py:651
  12.4 12.7 %collective-permute-start.3 = (bf16[96,8,256]{2,1,0:T(8,128)(2,1)}, bf16[96,8,256]{2,1,0:T(8,128)(2,1)}, u32[]{:S(2)}, u32[]{:S(2)}) collective-permute-start(bf16[96,8,256]{2,1,0:T(8,128)(2,1)} %get-tuple-element.32), channel_id=1, source_target_pairs={{0,1},{1,2},{2,3},{3,4},{4,5},{5,6},{6,7},{8,9},{9,10},{10,11},{11... | collective-permute-start | bytes 1179656 | tf_op jit(solution)/shard_map/ppermute | solution.py:651
  15.4 9.6 %copy-start.6 = (bf16[8,32,256]{2,1,0:T(8,128)(2,1)}, bf16[8,32,256]{2,1,0:T(8,128)(2,1)S(1)}, u32[]{:S(2)}) copy-start(bf16[8,32,256]{2,1,0:T(8,128)(2,1)S(1)} %collective-permute-done.top_ref) | copy-start | bytes 393220
  15.4 9.6 %copy-start.7 = (bf16[8,32,256]{2,1,0:T(8,128)(2,1)}, bf16[8,32,256]{2,1,0:T(8,128)(2,1)S(1)}, u32[]{:S(2)}) copy-start(bf16[8,32,256]{2,1,0:T(8,128)(2,1)S(1)} %collective-permute-done.1.bot_ref) | copy-start | bytes 393220
  15.5 6.5 %collective-permute-start.5 = (bf16[16,8,256]{2,1,0:T(8,128)(2,1)S(1)}, bf16[16,8,256]{2,1,0:T(8,128)(2,1)S(1)}, u32[]{:S(2)}, u32[]{:S(2)}) collective-permute-start(bf16[16,8,256]{2,1,0:T(8,128)(2,1)S(1)} %get-tuple-element.55), channel_id=1, source_target_pairs={{0,1},{1,2},{2,3},{3,4},{4,5},{5,6},{6,7},{8,9},{9,10},{10,11},{11... | collective-permute-start | bytes 196616 | tf_op jit(solution)/shard_map/ppermute | solution.py:651
  19.4 5.6 %collective-permute-start.4 = (bf16[16,8,256]{2,1,0:T(8,128)(2,1)S(1)}, bf16[16,8,256]{2,1,0:T(8,128)(2,1)S(1)}, u32[]{:S(2)}, u32[]{:S(2)}) collective-permute-start(bf16[16,8,256]{2,1,0:T(8,128)(2,1)S(1)} %get-tuple-element.56), channel_id=1, source_target_pairs={{1,0},{2,1},{3,2},{4,3},{5,4},{6,5},{7,6},{9,8},{10,9},{11,10},{12... | collective-permute-start | bytes 196616 | tf_op jit(solution)/shard_map/ppermute | solution.py:651
  22.0 3.1 %copy-start.9 = (bf16[16,8,256]{2,1,0:T(8,128)(2,1)}, bf16[16,8,256]{2,1,0:T(8,128)(2,1)S(1)}, u32[]{:S(2)}) copy-start(bf16[16,8,256]{2,1,0:T(8,128)(2,1)S(1)} %collective-permute-done.5.left_ends) | copy-start | bytes 196612
  58.0 3.3 %collective-permute-start.6 = (bf16[5184,128]{1,0:T(8,128)(2,1)}, bf16[5184,128]{1,0:T(8,128)(2,1)S(1)}, u32[]{:S(2)}, u32[]{:S(2)}) collective-permute-start(bf16[5184,128]{1,0:T(8,128)(2,1)} %get-tuple-element.36), channel_id=1, source_target_pairs={{0,1},{1,0},{2,3},{3,2},{4,5},{5,4},{6,7},{7,6},{8,9},{9,8},{10,11... | collective-permute-start | bytes 3981320 | tf_op jit(solution)/shard_map/ppermute | solution.py:720
  63.3 11.4 %collective-permute-start.7 = (bf16[1344,128]{1,0:T(8,128)(2,1)S(1)}, bf16[1344,128]{1,0:T(8,128)(2,1)S(1)}, u32[]{:S(2)}, u32[]{:S(2)}) collective-permute-start(bf16[1344,128]{1,0:T(8,128)(2,1)S(1)} %get-tuple-element.64), channel_id=1, source_target_pairs={{0,32},{1,3},{2,34},{3,5},{4,36},{5,7},{6,38},{7,1},{8,40},{9,11},... | collective-permute-start | bytes 1032200 | tf_op jit(solution)/shard_map/ppermute | solution.py:680
  64.5 10.1 %collective-permute-start.9 = (bf16[1344,128]{1,0:T(8,128)(2,1)S(1)}, bf16[1344,128]{1,0:T(8,128)(2,1)S(1)}, u32[]{:S(2)}, u32[]{:S(2)}) collective-permute-start(bf16[1344,128]{1,0:T(8,128)(2,1)S(1)} %get-tuple-element.65), channel_id=1, source_target_pairs={{0,96},{1,7},{2,98},{3,1},{4,100},{5,3},{6,102},{7,5},{8,104},{9,1... | collective-permute-start | bytes 1032200 | tf_op jit(solution)/shard_map/ppermute | solution.py:680
  66.0 8.6 %collective-permute-start.8 = (bf16[1344,128]{1,0:T(8,128)(2,1)S(1)}, bf16[1344,128]{1,0:T(8,128)(2,1)S(1)}, u32[]{:S(2)}, u32[]{:S(2)}) collective-permute-start(bf16[1344,128]{1,0:T(8,128)(2,1)S(1)} %get-tuple-element.66), channel_id=1, source_target_pairs={{0,64},{1,5},{2,66},{3,7},{4,68},{5,1},{6,70},{7,3},{8,72},{9,13},... | collective-permute-start | bytes 1032200 | tf_op jit(solution)/shard_map/ppermute | solution.py:680
  75.0 4.8 %collective-permute-start.10 = (bf16[384,128]{1,0:T(8,128)(2,1)S(1)}, bf16[384,128]{1,0:T(8,128)(2,1)S(1)}, u32[]{:S(2)}, u32[]{:S(2)}) collective-permute-start(bf16[384,128]{1,0:T(8,128)(2,1)S(1)} %get-tuple-element.61), channel_id=1, source_target_pairs={{0,2},{1,33},{2,4},{3,35},{4,6},{5,37},{6,0},{7,39},{8,10},{9,41},... | collective-permute-start | bytes 294920 | tf_op jit(solution)/shard_map/ppermute | solution.py:680
  76.2 5.8 %collective-permute-start.11 = (bf16[384,128]{1,0:T(8,128)(2,1)S(1)}, bf16[384,128]{1,0:T(8,128)(2,1)S(1)}, u32[]{:S(2)}, u32[]{:S(2)}) collective-permute-start(bf16[384,128]{1,0:T(8,128)(2,1)S(1)} %get-tuple-element.62), channel_id=1, source_target_pairs={{0,4},{1,65},{2,6},{3,67},{4,0},{5,69},{6,2},{7,71},{8,12},{9,73},... | collective-permute-start | bytes 294920 | tf_op jit(solution)/shard_map/ppermute | solution.py:680
  79.0 3.7 %collective-permute-start.12 = (bf16[384,128]{1,0:T(8,128)(2,1)S(1)}, bf16[384,128]{1,0:T(8,128)(2,1)S(1)}, u32[]{:S(2)}, u32[]{:S(2)}) collective-permute-start(bf16[384,128]{1,0:T(8,128)(2,1)S(1)} %get-tuple-element.63), channel_id=1, source_target_pairs={{0,6},{1,97},{2,0},{3,99},{4,2},{5,101},{6,4},{7,103},{8,14},{9,10... | collective-permute-start | bytes 294920 | tf_op jit(solution)/shard_map/ppermute | solution.py:680
  82.8 5.9 %collective-permute-start.14 = (bf16[384,128]{1,0:T(8,128)(2,1)S(1)}, bf16[384,128]{1,0:T(8,128)(2,1)S(1)}, u32[]{:S(2)}, u32[]{:S(2)}) collective-permute-start(bf16[384,128]{1,0:T(8,128)(2,1)S(1)} %get-tuple-element.60), channel_id=1, source_target_pairs={{0,16},{1,17},{2,18},{3,19},{4,20},{5,21},{6,22},{7,23},{8,24},{9,... | collective-permute-start | bytes 294920 | tf_op jit(solution)/shard_map/ppermute | solution.py:680
  86.0 5.7 %collective-permute-start.13 = (bf16[384,128]{1,0:T(8,128)(2,1)S(1)}, bf16[384,128]{1,0:T(8,128)(2,1)S(1)}, u32[]{:S(2)}, u32[]{:S(2)}) collective-permute-start(bf16[384,128]{1,0:T(8,128)(2,1)S(1)} %get-tuple-element.60), channel_id=1, source_target_pairs={{0,8},{1,9},{2,10},{3,11},{4,12},{5,13},{6,14},{7,15},{8,16},{9,17... | collective-permute-start | bytes 294920 | tf_op jit(solution)/shard_map/ppermute | solution.py:680
  86.4 5.3 %collective-permute-start.15 = (bf16[384,128]{1,0:T(8,128)(2,1)S(1)}, bf16[384,128]{1,0:T(8,128)(2,1)S(1)}, u32[]{:S(2)}, u32[]{:S(2)}) collective-permute-start(bf16[384,128]{1,0:T(8,128)(2,1)S(1)} %get-tuple-element.60), channel_id=1, source_target_pairs={{0,24},{1,25},{2,26},{3,27},{4,28},{5,29},{6,30},{7,31},{8,0},{9,1... | collective-permute-start | bytes 294920 | tf_op jit(solution)/shard_map/ppermute | solution.py:680
  91.7 27.6 %copy-start.1 = (f32[256,512]{1,0:T(8,128)S(1)}, f32[256,512]{1,0:T(8,128)}, u32[]{:S(2)}) copy-start(f32[256,512]{1,0:T(8,128)} %refs_1_.1) | copy-start | bytes 1572868
  91.8 27.6 %copy-start.2 = (f32[512,256]{1,0:T(8,128)S(1)}, f32[512,256]{1,0:T(8,128)}, u32[]{:S(2)}) copy-start(f32[512,256]{1,0:T(8,128)} %refs_4_.1) | copy-start | bytes 1572868
  91.9 4.6 %collective-permute-start.16 = (bf16[320,128]{1,0:T(8,128)(2,1)S(1)}, bf16[320,128]{1,0:T(8,128)(2,1)S(1)}, u32[]{:S(2)}, u32[]{:S(2)}) collective-permute-start(bf16[320,128]{1,0:T(8,128)(2,1)S(1)} %get-tuple-element.57), channel_id=1, source_target_pairs={{0,2},{1,33},{2,4},{3,35},{4,6},{5,37},{6,0},{7,39},{8,10},{9,41},... | collective-permute-start | bytes 245768 | tf_op jit(solution)/shard_map/ppermute | solution.py:680
  92.6 6.8 %collective-permute-start.18 = (bf16[320,128]{1,0:T(8,128)(2,1)S(1)}, bf16[320,128]{1,0:T(8,128)(2,1)S(1)}, u32[]{:S(2)}, u32[]{:S(2)}) collective-permute-start(bf16[320,128]{1,0:T(8,128)(2,1)S(1)} %get-tuple-element.57), channel_id=1, source_target_pairs={{0,6},{1,97},{2,0},{3,99},{4,2},{5,101},{6,4},{7,103},{8,14},{9,10... | collective-permute-start | bytes 245768 | tf_op jit(solution)/shard_map/ppermute | solution.py:680
  94.7 4.8 %collective-permute-start.17 = (bf16[320,128]{1,0:T(8,128)(2,1)S(1)}, bf16[320,128]{1,0:T(8,128)(2,1)S(1)}, u32[]{:S(2)}, u32[]{:S(2)}) collective-permute-start(bf16[320,128]{1,0:T(8,128)(2,1)S(1)} %get-tuple-element.57), channel_id=1, source_target_pairs={{0,4},{1,65},{2,6},{3,67},{4,0},{5,69},{6,2},{7,71},{8,12},{9,73},... | collective-permute-start | bytes 245768 | tf_op jit(solution)/shard_map/ppermute | solution.py:680
  99.5 19.9 %copy-start = (f32[2,2,512,512]{3,2,1,0:T(8,128)S(1)}, f32[2,2,512,512]{3,2,1,0:T(8,128)}, u32[]{:S(2)}) copy-start(f32[2,2,512,512]{3,2,1,0:T(8,128)} %param.11) | copy-start | bytes 12582916
  99.5 7.5 %collective-permute-start.19 = (bf16[1280,128]{1,0:T(8,128)(2,1)S(1)}, bf16[1280,128]{1,0:T(8,128)(2,1)S(1)}, u32[]{:S(2)}, u32[]{:S(2)}) collective-permute-start(bf16[1280,128]{1,0:T(8,128)(2,1)S(1)} %bitcast.97), channel_id=1, source_target_pairs={{0,32},{1,3},{2,34},{3,5},{4,36},{5,7},{6,38},{7,1},{8,40},{9,11},... | collective-permute-start | bytes 983048 | tf_op jit(solution)/shard_map/ppermute | solution.py:680
  99.8 11.5 %collective-permute-start.21 = (bf16[1280,128]{1,0:T(8,128)(2,1)S(1)}, bf16[1280,128]{1,0:T(8,128)(2,1)S(1)}, u32[]{:S(2)}, u32[]{:S(2)}) collective-permute-start(bf16[1280,128]{1,0:T(8,128)(2,1)S(1)} %bitcast.98), channel_id=1, source_target_pairs={{0,96},{1,7},{2,98},{3,1},{4,100},{5,3},{6,102},{7,5},{8,104},{9,1... | collective-permute-start | bytes 983048 | tf_op jit(solution)/shard_map/ppermute | solution.py:680
  102.3 8.9 %collective-permute-start.20 = (bf16[1280,128]{1,0:T(8,128)(2,1)S(1)}, bf16[1280,128]{1,0:T(8,128)(2,1)S(1)}, u32[]{:S(2)}, u32[]{:S(2)}) collective-permute-start(bf16[1280,128]{1,0:T(8,128)(2,1)S(1)} %bitcast.99), channel_id=1, source_target_pairs={{0,64},{1,5},{2,66},{3,7},{4,68},{5,1},{6,70},{7,3},{8,72},{9,13},... | collective-permute-start | bytes 983048 | tf_op jit(solution)/shard_map/ppermute | solution.py:680
  103.4 16.0 %copy-start.3 = (f32[3,3,512]{2,1,0:T(4,128)S(1)}, f32[3,3,512]{2,1,0:T(4,128)}, u32[]{:S(2)}) copy-start(f32[3,3,512]{2,1,0:T(4,128)} %refs_3_.1) | copy-start | bytes 55300
  103.4 16.0 %copy-start.4 = (f32[3,3,256]{2,1,0:T(4,128)S(1)}, f32[3,3,256]{2,1,0:T(4,128)}, u32[]{:S(2)}) copy-start(f32[3,3,256]{2,1,0:T(4,128)} %refs_0_.1) | copy-start | bytes 27652
  103.4 16.0 %copy-start.5 = (f32[5]{0:T(128)S(1)}, f32[5]{0:T(128)}, u32[]{:S(2)}) copy-start(f32[5]{0:T(128)} %get-tuple-element.34.sums) | copy-start | bytes 64
  111.3 8.0 %collective-permute-start.22 = (bf16[5120,128]{1,0:T(8,128)(2,1)S(1)}, bf16[5120,128]{1,0:T(8,128)(2,1)S(1)}, u32[]{:S(2)}, u32[]{:S(2)}) collective-permute-start(bf16[5120,128]{1,0:T(8,128)(2,1)S(1)} %bitcast.81), channel_id=1, source_target_pairs={{0,1},{1,0},{2,3},{3,2},{4,5},{5,4},{6,7},{7,6},{8,9},{9,8},{10,11... | collective-permute-start | bytes 3932168 | tf_op jit(solution)/shard_map/ppermute | solution.py:729
  (2 other events, 1.4 us)

commit v5 on v4

--- a/solution.py
+++ b/solution.py
@@ -316,7 +316,7 @@
             block = cout[c, pl.ds(n * 4 + 1, 4), :, :]
             up[c, :, pl.ds(0, hc, stride=2), :] = block
             up[c, :, pl.ds(1, hc, stride=2), :] = block
-            wide = up[c, :, :, :]
+            wide = up[c, :, 0:cols, :]
             wide = jnp.stack([wide, wide], axis=1).reshape(8, cols, LANES)
             fine = xf[c, pl.ds(n * 8 + ROWS, 8), 8 : 8 + cols, :]
             pred_ref[pl.ds(n * 8, 8), :, lanes(c)] = (wide + fine).astype(BF16)
@@ -449,7 +449,7 @@
             pltpu.VMEM((cb2, hr + 4, slots + 16, LANES), F32),
             pltpu.VMEM((cb2, hr + 2, slots + 16, LANES), F32),
             pltpu.VMEM((cb1, hr + 2, hc, LANES), F32),
-            pltpu.VMEM((cb1, 4, cols, LANES), F32),
+            pltpu.VMEM((cb1, 4, cols + 8, LANES), F32),
             pltpu.VMEM(((hr + 2) * hc, hid), BF16),
             pltpu.VMEM(((hr + 2) * hc, chan), BF16),
             pltpu.VMEM((hr * hc, hid), BF16),
@@ -519,7 +519,7 @@
         st_ref,
         sems,
     ) = refs
-    chan, hid = p1_ref.shape
+    chan, hid = p2_ref.shape[1], p1_ref.shape[1]
     cb1, cb2 = chan // LANES, hid // LANES
     parts, block = 4, st_ref.shape[1]
     step = pl.program_id(0)
@@ -586,18 +586,19 @@
                     normed = small[at : at + 3, :] * scale[j : j + 1, :]
                     out[r, :, cut] = normed
                     new[r, :, cut] = w[r, :, cut] - scale[5 + j : 6 + j, :] * normed
-        for c in range(cb2):
+
+    for j, at, height, blocks, w, new, out in (
+        (1, p1_at, chan, cb2, p1_ref, np1_ref, sp1_ref),
+        (4, p2_at, hid, cb1, p2_ref, np2_ref, sp2_ref),
+    ):
+        count = w.shape[0]
+        for c in range(blocks):
             cut = slice(c * LANES, (c + 1) * LANES)
-            at = p1_at + (c % (cb2 // 2)) * chan
-            normed = g[2 * c // cb2, at : at + chan, :].astype(F32) * scale[1:2, :]
-            sp1_ref[:, cut] = normed
-            np1_ref[:, cut] = p1_ref[:, cut] - scale[6:7, :] * normed
-        for c in range(cb1):
-            cut = slice(c * LANES, (c + 1) * LANES)
-            at = p2_at + (c % (cb1 // 2)) * hid
-            normed = g[2 * c // cb1, at : at + hid, :].astype(F32) * scale[4:5, :]
-            sp2_ref[:, cut] = normed
-            np2_ref[:, cut] = p2_ref[:, cut] - scale[9:10, :] * normed
+            first = at + (c % (blocks // 2)) * height + step * count
+            rows = pl.ds(pl.multiple_of(first, count), count)
+            normed = g[2 * c // blocks, rows, :].astype(F32) * scale[j : j + 1, :]
+            out[:, cut] = normed
+            new[:, cut] = w[:, cut] - scale[5 + j : 6 + j, :] * normed
 
     fetch(step).wait()
     ph = step // per
@@ -618,7 +619,11 @@
         return pl.BlockSpec(w.shape, lambda n: (0,) * w.ndim)
 
     st = pl.BlockSpec((1, block, hid), lambda n: (n // per, n % per, 0))
-    specs = [whole(k1), whole(p1), st, whole(k2), whole(p2)]
+    steps = 4 * per
+    p1_spec, p2_spec = [
+        pl.BlockSpec((p.shape[0] // steps, p.shape[1]), lambda n: (n, 0)) for p in (p1, p2)
+    ]
+    specs = [whole(k1), p1_spec, st, whole(k2), p2_spec]
     shapes = [jax.ShapeDtypeStruct(w.shape, F32) for w in (k1, p1, taps, k2, p2)]
     return pl.pallas_call(
         update_kernel,
@@ -636,7 +641,7 @@
             pltpu.VMEM((4 * per, block, hid), F32),
             pltpu.SemaphoreType.DMA((4 * per,)),
         ],
-        compiler_params=pltpu.CompilerParams(vmem_limit_bytes=40 * 1024 * 1024),
+        compiler_params=pltpu.CompilerParams(vmem_limit_bytes=50 * 1024 * 1024),
     )(where, sums, small, own, other, k1, p1, taps, k2, p2)
 
 
@@ -658,7 +663,6 @@
         self.names, self.sizes = names, sizes
         self.count = sizes[names[0]]
         assert sizes[names[1]] == self.count
-        self.steps = range(1, self.count)
         self.me = jnp.where(lax.axis_index("tx") % 2 == 0, place[names[0]], place[names[1]])
 
     def send(self, block, step):
@@ -685,7 +689,7 @@
         share = lax.dynamic_index_in_dim(shares, self.me, 0, False)
         cut = share.shape[0]
         got = {}
-        for d in self.steps:
+        for d in range(1, n):
             out = lax.dynamic_index_in_dim(shares, (self.me + d) % n, 0, False)
             got[d] = self.send(jnp.concatenate([out, extra], axis=0), d)
         total = sum([g[:cut].astype(F32) for g in got.values()], share.astype(F32))
@@ -701,14 +705,14 @@
         return total.astype(BF16)
 
     def reduce(self, block):
-        got = {d: self.send(block, d) for d in self.steps}
+        got = {d: self.send(block, d) for d in range(1, self.count)}
         return self.added([block] + [got[d] for d in range(1, self.count)])
 
     def gather(self, share):
         n = self.count
         out = jnp.zeros((n,) + share.shape, share.dtype)
         out = lax.dynamic_update_index_in_dim(out, share, self.me, 0)
-        for d in self.steps:
+        for d in range(1, n):
             got = self.send(share, d)
             out = lax.dynamic_update_index_in_dim(out, got, (self.me + n - d) % n, 0)
         return out.reshape(-1, LANES)

time: 128 us -> 127 us (level)
  no operation moved by 1% of the time
where the time goes in v5:
time: 127 us
  starting transfers between devices  44.2 us (35%)
  Pallas kernels  42.7 us (34%)
  waiting for transfers between devices  34.2 us (27%)
  other arithmetic  2.21 us (2%)
  local copies, waits for them, and re-layouts  2.17 us (2%)
  between operations  1.33 us (1%)
    pallas_call x1, Pallas kernels, tile_step(): pl.pallas_call(tile_kernel, out_shape=(jax.ShapeDtypeStruct(x.shape, BF16...  32.2 us
    ppermute x15, waiting for transfers between devices, send(): return lax.ppermute(block, ('rep', 'ty', 'tx'), pairs)  25.4 us
    ppermute x15, starting transfers between devices, send(): return lax.ppermute(block, ('rep', 'ty', 'tx'), pairs)  21.4 us
    ppermute x6, starting transfers between devices, shift(): return lax.ppermute(block, ('ty', 'tx'), pairs)  17.4 us
    pallas_call x1, Pallas kernels, update(): pl.pallas_call(update_kernel, grid=(4 * per,), out_shape=shapes + shapes,...  7.29 us
    ppermute x1, starting transfers between devices, reduced(): return (small, share, lax.ppermute(share, 'tx', cores))  5.38 us
    pallas_call x1, Pallas kernels, edges(): pl.pallas_call(edges_kernel, grid=(1,), out_shape=[jax.ShapeDtypeStruct(s...  3.17 us
    ppermute x1, waiting for transfers between devices, reduced(): got = lax.ppermute(send, 'tx', cores)  3.17 us
  transfers between devices with their start and end apart: 23, of which 11 were waited for; matrix products, arithmetic and copies ran while one was open for 1% of the time, Pallas kernels for 0%

profile of v5, /device:TPU:1, one launch (start us, length us, event | category | flops | bytes accessed | tf_op | source)
XLA Modules:
  0.0 126.8 jit_solution(16105343416742485143)
XLA Ops:
  0.6 3.2 %shard_map.158 = (bf16[8,32,256]{2,1,0:T(8,128)(2,1)}, bf16[8,32,256]{2,1,0:T(8,128)(2,1)}, bf16[96,8,256]{2,1,0:T(8,128)(2,1)}, bf16[96,8,256]{2,1,0:T(8,128)(2,1)}) custom-call(bf16[96,32,256]{2,1,0:T(8,128)(2,1)} %bitcast.83, bf16[96,32,256]{2,1,0:T(8,128)(2,1)} %bitcast.88, bf16[96,32,256]{2,1,0:T(8,128)(2,1)} %bitcast.84, ...), custom_call_target="tpu_custom_call" | custom-call | tf_op jit(solution)/shard_map/pallas_call | solution.py:483
  3.8 4.4 %collective-permute-start = (bf16[8,32,256]{2,1,0:T(8,128)(2,1)}, bf16[8,32,256]{2,1,0:T(8,128)(2,1)S(1)}, u32[]{:S(2)}, u32[]{:S(2)}) collective-permute-start(bf16[8,32,256]{2,1,0:T(8,128)(2,1)} %get-tuple-element.29), channel_id=1, source_target_pairs={{0,8},{1,9},{2,10},{3,11},{4,12},{5,13},{6,14},{7,15},{8,16},{9,17... | collective-permute-start | bytes 393224 | tf_op jit(solution)/shard_map/ppermute | solution.py:656
  8.2 1.3 %collective-permute-start.1 = (bf16[8,32,256]{2,1,0:T(8,128)(2,1)}, bf16[8,32,256]{2,1,0:T(8,128)(2,1)S(1)}, u32[]{:S(2)}, u32[]{:S(2)}) collective-permute-start(bf16[8,32,256]{2,1,0:T(8,128)(2,1)} %get-tuple-element.30), channel_id=1, source_target_pairs={{8,0},{9,1},{10,2},{11,3},{12,4},{13,5},{14,6},{15,7},{16,8},{17,9... | collective-permute-start | bytes 393224 | tf_op jit(solution)/shard_map/ppermute | solution.py:656
  9.5 2.9 %collective-permute-start.2 = (bf16[96,8,256]{2,1,0:T(8,128)(2,1)}, bf16[96,8,256]{2,1,0:T(8,128)(2,1)S(1)}, u32[]{:S(2)}, u32[]{:S(2)}) collective-permute-start(bf16[96,8,256]{2,1,0:T(8,128)(2,1)} %get-tuple-element.31), channel_id=1, source_target_pairs={{1,0},{2,1},{3,2},{4,3},{5,4},{6,5},{7,6},{9,8},{10,9},{11,10},{12... | collective-permute-start | bytes 1179656 | tf_op jit(solution)/shard_map/ppermute | solution.py:656
  12.4 3.0 %collective-permute-start.3 = (bf16[96,8,256]{2,1,0:T(8,128)(2,1)}, bf16[96,8,256]{2,1,0:T(8,128)(2,1)}, u32[]{:S(2)}, u32[]{:S(2)}) collective-permute-start(bf16[96,8,256]{2,1,0:T(8,128)(2,1)} %get-tuple-element.32), channel_id=1, source_target_pairs={{0,1},{1,2},{2,3},{3,4},{4,5},{5,6},{6,7},{8,9},{9,10},{10,11},{11... | collective-permute-start | bytes 1179656 | tf_op jit(solution)/shard_map/ppermute | solution.py:656
  15.5 3.9 %collective-permute-start.5 = (bf16[16,8,256]{2,1,0:T(8,128)(2,1)S(1)}, bf16[16,8,256]{2,1,0:T(8,128)(2,1)S(1)}, u32[]{:S(2)}, u32[]{:S(2)}) collective-permute-start(bf16[16,8,256]{2,1,0:T(8,128)(2,1)S(1)} %get-tuple-element.55), channel_id=1, source_target_pairs={{0,1},{1,2},{2,3},{3,4},{4,5},{5,6},{6,7},{8,9},{9,10},{10,11},{11... | collective-permute-start | bytes 196616 | tf_op jit(solution)/shard_map/ppermute | solution.py:656
  19.4 1.9 %collective-permute-start.4 = (bf16[16,8,256]{2,1,0:T(8,128)(2,1)S(1)}, bf16[16,8,256]{2,1,0:T(8,128)(2,1)S(1)}, u32[]{:S(2)}, u32[]{:S(2)}) collective-permute-start(bf16[16,8,256]{2,1,0:T(8,128)(2,1)S(1)} %get-tuple-element.56), channel_id=1, source_target_pairs={{1,0},{2,1},{3,2},{4,3},{5,4},{6,5},{7,6},{9,8},{10,9},{11,10},{12... | collective-permute-start | bytes 196616 | tf_op jit(solution)/shard_map/ppermute | solution.py:656
  22.1 2.9 %collective-permute-done.4.right_ends = bf16[16,8,256]{2,1,0:T(8,128)(2,1)S(1)} collective-permute-done((bf16[16,8,256]{2,1,0:T(8,128)(2,1)S(1)}, bf16[16,8,256]{2,1,0:T(8,128)(2,1)S(1)}, u32[]{:S(2)}, u32[]{:S(2)}) %collective-permute-start.4) | collective-permute-done | bytes 65568 | tf_op jit(solution)/shard_map/ppermute | solution.py:656
  25.8 32.2 %shard_map.159 = (bf16[96,32,256]{2,1,0:T(8,128)(2,1)}, bf16[5184,128]{1,0:T(8,128)(2,1)}, bf16[5184,128]{1,0:T(8,128)(2,1)}, f32[5]{0:T(128)}) custom-call(s32[5]{0:T(128)} %stack.66.limits, bf16[96,32,256]{2,1,0:T(8,128)(2,1)} %bitcast.87, bf16[96,32,256]{2,1,0:T(8,128)(2,1)} %bitcast.92, bf16[8,32,256]{2,1,0:T(8,128)(2,1)} %copy-done.5, ...), custom_call_target="tpu_custom_call" | custom-call | flops 8999999488 | bytes 20000000 | tf_op jit(solution)/shard_map/pallas_call | solution.py:419
  58.2 3.2 %collective-permute-done.6 = bf16[5184,128]{1,0:T(8,128)(2,1)S(1)} collective-permute-done((bf16[5184,128]{1,0:T(8,128)(2,1)}, bf16[5184,128]{1,0:T(8,128)(2,1)S(1)}, u32[]{:S(2)}, u32[]{:S(2)}) %collective-permute-start.6) | collective-permute-done | bytes 1327136 | tf_op jit(solution)/shard_map/ppermute | solution.py:724
  61.3 1.7 %add_convert_fusion = bf16[5184,128]{1,0:T(8,128)(2,1)S(1)} fusion(bf16[5184,128]{1,0:T(8,128)(2,1)S(1)} %collective-permute-done.6, bf16[5184,128]{1,0:T(8,128)(2,1)} %get-tuple-element.35), kind=kLoop, calls=%fused_computation | loop fusion | flops 2654208 | bytes 3981312 | tf_op jit(solution)/shard_map/convert_element_type | solution.py:725
  63.3 1.3 %collective-permute-start.7 = (bf16[1344,128]{1,0:T(8,128)(2,1)S(1)}, bf16[1344,128]{1,0:T(8,128)(2,1)S(1)}, u32[]{:S(2)}, u32[]{:S(2)}) collective-permute-start(bf16[1344,128]{1,0:T(8,128)(2,1)S(1)} %get-tuple-element.64), channel_id=1, source_target_pairs={{0,32},{1,3},{2,34},{3,5},{4,36},{5,7},{6,38},{7,1},{8,40},{9,11},... | collective-permute-start | bytes 1032200 | tf_op jit(solution)/shard_map/ppermute | solution.py:684
  64.6 1.5 %collective-permute-start.9 = (bf16[1344,128]{1,0:T(8,128)(2,1)S(1)}, bf16[1344,128]{1,0:T(8,128)(2,1)S(1)}, u32[]{:S(2)}, u32[]{:S(2)}) collective-permute-start(bf16[1344,128]{1,0:T(8,128)(2,1)S(1)} %get-tuple-element.65), channel_id=1, source_target_pairs={{0,96},{1,7},{2,98},{3,1},{4,100},{5,3},{6,102},{7,5},{8,104},{9,1... | collective-permute-start | bytes 1032200 | tf_op jit(solution)/shard_map/ppermute | solution.py:684
  66.0 1.2 collective-permute-start.8
  67.3 7.4 %collective-permute-done.7 = bf16[1344,128]{1,0:T(8,128)(2,1)S(1)} collective-permute-done((bf16[1344,128]{1,0:T(8,128)(2,1)S(1)}, bf16[1344,128]{1,0:T(8,128)(2,1)S(1)}, u32[]{:S(2)}, u32[]{:S(2)}) %collective-permute-start.7) | collective-permute-done | bytes 344096 | tf_op jit(solution)/shard_map/ppermute | solution.py:684
  75.0 1.2 collective-permute-start.10
  76.2 2.8 %collective-permute-start.11 = (bf16[384,128]{1,0:T(8,128)(2,1)S(1)}, bf16[384,128]{1,0:T(8,128)(2,1)S(1)}, u32[]{:S(2)}, u32[]{:S(2)}) collective-permute-start(bf16[384,128]{1,0:T(8,128)(2,1)S(1)} %get-tuple-element.62), channel_id=1, source_target_pairs={{0,4},{1,65},{2,6},{3,67},{4,0},{5,69},{6,2},{7,71},{8,12},{9,73},... | collective-permute-start | bytes 294920 | tf_op jit(solution)/shard_map/ppermute | solution.py:684
  79.0 0.8 collective-permute-start.12
  79.8 2.2 %collective-permute-done.11 = bf16[384,128]{1,0:T(8,128)(2,1)S(1)} collective-permute-done((bf16[384,128]{1,0:T(8,128)(2,1)S(1)}, bf16[384,128]{1,0:T(8,128)(2,1)S(1)}, u32[]{:S(2)}, u32[]{:S(2)}) %collective-permute-start.11) | collective-permute-done | bytes 98336 | tf_op jit(solution)/shard_map/ppermute | solution.py:684
  82.8 3.2 %collective-permute-start.14 = (bf16[384,128]{1,0:T(8,128)(2,1)S(1)}, bf16[384,128]{1,0:T(8,128)(2,1)S(1)}, u32[]{:S(2)}, u32[]{:S(2)}) collective-permute-start(bf16[384,128]{1,0:T(8,128)(2,1)S(1)} %get-tuple-element.60), channel_id=1, source_target_pairs={{0,16},{1,17},{2,18},{3,19},{4,20},{5,21},{6,22},{7,23},{8,24},{9,... | collective-permute-start | bytes 294920 | tf_op jit(solution)/shard_map/ppermute | solution.py:684
  86.4 2.3 %collective-permute-start.15 = (bf16[384,128]{1,0:T(8,128)(2,1)S(1)}, bf16[384,128]{1,0:T(8,128)(2,1)S(1)}, u32[]{:S(2)}, u32[]{:S(2)}) collective-permute-start(bf16[384,128]{1,0:T(8,128)(2,1)S(1)} %get-tuple-element.60), channel_id=1, source_target_pairs={{0,24},{1,25},{2,26},{3,27},{4,28},{5,29},{6,30},{7,31},{8,0},{9,1... | collective-permute-start | bytes 294920 | tf_op jit(solution)/shard_map/ppermute | solution.py:684
  88.7 3.0 %collective-permute-done.13 = bf16[384,128]{1,0:T(8,128)(2,1)S(1)} collective-permute-done((bf16[384,128]{1,0:T(8,128)(2,1)S(1)}, bf16[384,128]{1,0:T(8,128)(2,1)S(1)}, u32[]{:S(2)}, u32[]{:S(2)}) %collective-permute-start.13) | collective-permute-done | bytes 98336 | tf_op jit(solution)/shard_map/ppermute | solution.py:684
  92.6 2.0 %collective-permute-start.18 = (bf16[320,128]{1,0:T(8,128)(2,1)S(1)}, bf16[320,128]{1,0:T(8,128)(2,1)S(1)}, u32[]{:S(2)}, u32[]{:S(2)}) collective-permute-start(bf16[320,128]{1,0:T(8,128)(2,1)S(1)} %get-tuple-element.57), channel_id=1, source_target_pairs={{0,6},{1,97},{2,0},{3,99},{4,2},{5,101},{6,4},{7,103},{8,14},{9,10... | collective-permute-start | bytes 245768 | tf_op jit(solution)/shard_map/ppermute | solution.py:684
  94.9 1.5 %collective-permute-done.16 = bf16[320,128]{1,0:T(8,128)(2,1)S(1)} collective-permute-done((bf16[320,128]{1,0:T(8,128)(2,1)S(1)}, bf16[320,128]{1,0:T(8,128)(2,1)S(1)}, u32[]{:S(2)}, u32[]{:S(2)}) %collective-permute-start.16) | collective-permute-done | bytes 81952 | tf_op jit(solution)/shard_map/ppermute | solution.py:684
  96.5 3.0 %collective-permute-done.17 = bf16[320,128]{1,0:T(8,128)(2,1)S(1)} collective-permute-done((bf16[320,128]{1,0:T(8,128)(2,1)S(1)}, bf16[320,128]{1,0:T(8,128)(2,1)S(1)}, u32[]{:S(2)}, u32[]{:S(2)}) %collective-permute-start.17) | collective-permute-done | bytes 81952 | tf_op jit(solution)/shard_map/ppermute | solution.py:684
  99.8 2.5 %collective-permute-start.21 = (bf16[1280,128]{1,0:T(8,128)(2,1)S(1)}, bf16[1280,128]{1,0:T(8,128)(2,1)S(1)}, u32[]{:S(2)}, u32[]{:S(2)}) collective-permute-start(bf16[1280,128]{1,0:T(8,128)(2,1)S(1)} %bitcast.98), channel_id=1, source_target_pairs={{0,96},{1,7},{2,98},{3,1},{4,100},{5,3},{6,102},{7,5},{8,104},{9,1... | collective-permute-start | bytes 983048 | tf_op jit(solution)/shard_map/ppermute | solution.py:684
  102.2 1.0 collective-permute-start.20
  103.5 3.5 %collective-permute-done.19 = bf16[1280,128]{1,0:T(8,128)(2,1)S(1)} collective-permute-done((bf16[1280,128]{1,0:T(8,128)(2,1)S(1)}, bf16[1280,128]{1,0:T(8,128)(2,1)S(1)}, u32[]{:S(2)}, u32[]{:S(2)}) %collective-permute-start.19) | collective-permute-done | bytes 327712 | tf_op jit(solution)/shard_map/ppermute | solution.py:684
  107.1 4.1 %collective-permute-done.20 = bf16[1280,128]{1,0:T(8,128)(2,1)S(1)} collective-permute-done((bf16[1280,128]{1,0:T(8,128)(2,1)S(1)}, bf16[1280,128]{1,0:T(8,128)(2,1)S(1)}, u32[]{:S(2)}, u32[]{:S(2)}) %collective-permute-start.20) | collective-permute-done | bytes 327712 | tf_op jit(solution)/shard_map/ppermute | solution.py:684
  111.3 5.4 %collective-permute-start.22 = (bf16[5120,128]{1,0:T(8,128)(2,1)S(1)}, bf16[5120,128]{1,0:T(8,128)(2,1)S(1)}, u32[]{:S(2)}, u32[]{:S(2)}) collective-permute-start(bf16[5120,128]{1,0:T(8,128)(2,1)S(1)} %bitcast.81), channel_id=1, source_target_pairs={{0,1},{1,0},{2,3},{3,2},{4,5},{5,4},{6,7},{7,6},{8,9},{9,8},{10,11... | collective-permute-start | bytes 3932168 | tf_op jit(solution)/shard_map/ppermute | solution.py:733
  116.7 2.7 %collective-permute-done.22.other_ref = bf16[5120,128]{1,0:T(8,128)(2,1)S(1)} collective-permute-done((bf16[5120,128]{1,0:T(8,128)(2,1)S(1)}, bf16[5120,128]{1,0:T(8,128)(2,1)S(1)}, u32[]{:S(2)}, u32[]{:S(2)}) %collective-permute-start.22) | collective-permute-done | bytes 1310752 | tf_op jit(solution)/shard_map/ppermute | solution.py:733
  119.4 7.3 %shard_map.160 = (f32[3,3,256]{2,1,0:T(4,128)}, f32[256,512]{1,0:T(8,128)}, f32[4,512,512]{2,1,0:T(8,128)}, f32[3,3,512]{2,1,0:T(4,128)}, f32[512,256]{1,0:T(8,1...) custom-call(s32[1]{0:T(128)} %bitcast.4.where, ...), custom_call_target="tpu_custom_call" | custom-call | tf_op jit(solution)/shard_map/pallas_call | solution.py:628
  (75 shorter events, 5.2 us)
Async XLA Ops:
  3.8 11.6 %collective-permute-start = (bf16[8,32,256]{2,1,0:T(8,128)(2,1)}, bf16[8,32,256]{2,1,0:T(8,128)(2,1)S(1)}, u32[]{:S(2)}, u32[]{:S(2)}) collective-permute-start(bf16[8,32,256]{2,1,0:T(8,128)(2,1)} %get-tuple-element.29), channel_id=1, source_target_pairs={{0,8},{1,9},{2,10},{3,11},{4,12},{5,13},{6,14},{7,15},{8,16},{9,17... | collective-permute-start | bytes 393224 | tf_op jit(solution)/shard_map/ppermute | solution.py:656
  8.2 7.2 %collective-permute-start.1 = (bf16[8,32,256]{2,1,0:T(8,128)(2,1)}, bf16[8,32,256]{2,1,0:T(8,128)(2,1)S(1)}, u32[]{:S(2)}, u32[]{:S(2)}) collective-permute-start(bf16[8,32,256]{2,1,0:T(8,128)(2,1)} %get-tuple-element.30), channel_id=1, source_target_pairs={{8,0},{9,1},{10,2},{11,3},{12,4},{13,5},{14,6},{15,7},{16,8},{17,9... | collective-permute-start | bytes 393224 | tf_op jit(solution)/shard_map/ppermute | solution.py:656
  9.5 15.5 %collective-permute-start.2 = (bf16[96,8,256]{2,1,0:T(8,128)(2,1)}, bf16[96,8,256]{2,1,0:T(8,128)(2,1)S(1)}, u32[]{:S(2)}, u32[]{:S(2)}) collective-permute-start(bf16[96,8,256]{2,1,0:T(8,128)(2,1)} %get-tuple-element.31), channel_id=1, source_target_pairs={{1,0},{2,1},{3,2},{4,3},{5,4},{6,5},{7,6},{9,8},{10,9},{11,10},{12... | collective-permute-start | bytes 1179656 | tf_op jit(solution)/shard_map/ppermute | solution.py:656
  12.4 12.7 %collective-permute-start.3 = (bf16[96,8,256]{2,1,0:T(8,128)(2,1)}, bf16[96,8,256]{2,1,0:T(8,128)(2,1)}, u32[]{:S(2)}, u32[]{:S(2)}) collective-permute-start(bf16[96,8,256]{2,1,0:T(8,128)(2,1)} %get-tuple-element.32), channel_id=1, source_target_pairs={{0,1},{1,2},{2,3},{3,4},{4,5},{5,6},{6,7},{8,9},{9,10},{10,11},{11... | collective-permute-start | bytes 1179656 | tf_op jit(solution)/shard_map/ppermute | solution.py:656
  15.4 9.6 %copy-start.5 = (bf16[8,32,256]{2,1,0:T(8,128)(2,1)}, bf16[8,32,256]{2,1,0:T(8,128)(2,1)S(1)}, u32[]{:S(2)}) copy-start(bf16[8,32,256]{2,1,0:T(8,128)(2,1)S(1)} %collective-permute-done.top_ref) | copy-start | bytes 393220
  15.4 9.6 %copy-start.6 = (bf16[8,32,256]{2,1,0:T(8,128)(2,1)}, bf16[8,32,256]{2,1,0:T(8,128)(2,1)S(1)}, u32[]{:S(2)}) copy-start(bf16[8,32,256]{2,1,0:T(8,128)(2,1)S(1)} %collective-permute-done.1.bot_ref) | copy-start | bytes 393220
  15.5 6.6 %collective-permute-start.5 = (bf16[16,8,256]{2,1,0:T(8,128)(2,1)S(1)}, bf16[16,8,256]{2,1,0:T(8,128)(2,1)S(1)}, u32[]{:S(2)}, u32[]{:S(2)}) collective-permute-start(bf16[16,8,256]{2,1,0:T(8,128)(2,1)S(1)} %get-tuple-element.55), channel_id=1, source_target_pairs={{0,1},{1,2},{2,3},{3,4},{4,5},{5,6},{6,7},{8,9},{9,10},{10,11},{11... | collective-permute-start | bytes 196616 | tf_op jit(solution)/shard_map/ppermute | solution.py:656
  19.4 5.6 %collective-permute-start.4 = (bf16[16,8,256]{2,1,0:T(8,128)(2,1)S(1)}, bf16[16,8,256]{2,1,0:T(8,128)(2,1)S(1)}, u32[]{:S(2)}, u32[]{:S(2)}) collective-permute-start(bf16[16,8,256]{2,1,0:T(8,128)(2,1)S(1)} %get-tuple-element.56), channel_id=1, source_target_pairs={{1,0},{2,1},{3,2},{4,3},{5,4},{6,5},{7,6},{9,8},{10,9},{11,10},{12... | collective-permute-start | bytes 196616 | tf_op jit(solution)/shard_map/ppermute | solution.py:656
  22.1 3.0 %copy-start.8 = (bf16[16,8,256]{2,1,0:T(8,128)(2,1)}, bf16[16,8,256]{2,1,0:T(8,128)(2,1)S(1)}, u32[]{:S(2)}) copy-start(bf16[16,8,256]{2,1,0:T(8,128)(2,1)S(1)} %collective-permute-done.5.left_ends) | copy-start | bytes 196612
  25.0 0.8 copy-start.7
  58.0 3.3 %collective-permute-start.6 = (bf16[5184,128]{1,0:T(8,128)(2,1)}, bf16[5184,128]{1,0:T(8,128)(2,1)S(1)}, u32[]{:S(2)}, u32[]{:S(2)}) collective-permute-start(bf16[5184,128]{1,0:T(8,128)(2,1)} %get-tuple-element.36), channel_id=1, source_target_pairs={{0,1},{1,0},{2,3},{3,2},{4,5},{5,4},{6,7},{7,6},{8,9},{9,8},{10,11... | collective-permute-start | bytes 3981320 | tf_op jit(solution)/shard_map/ppermute | solution.py:724
  63.3 11.4 %collective-permute-start.7 = (bf16[1344,128]{1,0:T(8,128)(2,1)S(1)}, bf16[1344,128]{1,0:T(8,128)(2,1)S(1)}, u32[]{:S(2)}, u32[]{:S(2)}) collective-permute-start(bf16[1344,128]{1,0:T(8,128)(2,1)S(1)} %get-tuple-element.64), channel_id=1, source_target_pairs={{0,32},{1,3},{2,34},{3,5},{4,36},{5,7},{6,38},{7,1},{8,40},{9,11},... | collective-permute-start | bytes 1032200 | tf_op jit(solution)/shard_map/ppermute | solution.py:684
  64.6 10.1 %collective-permute-start.9 = (bf16[1344,128]{1,0:T(8,128)(2,1)S(1)}, bf16[1344,128]{1,0:T(8,128)(2,1)S(1)}, u32[]{:S(2)}, u32[]{:S(2)}) collective-permute-start(bf16[1344,128]{1,0:T(8,128)(2,1)S(1)} %get-tuple-element.65), channel_id=1, source_target_pairs={{0,96},{1,7},{2,98},{3,1},{4,100},{5,3},{6,102},{7,5},{8,104},{9,1... | collective-permute-start | bytes 1032200 | tf_op jit(solution)/shard_map/ppermute | solution.py:684
  66.0 8.6 %collective-permute-start.8 = (bf16[1344,128]{1,0:T(8,128)(2,1)S(1)}, bf16[1344,128]{1,0:T(8,128)(2,1)S(1)}, u32[]{:S(2)}, u32[]{:S(2)}) collective-permute-start(bf16[1344,128]{1,0:T(8,128)(2,1)S(1)} %get-tuple-element.66), channel_id=1, source_target_pairs={{0,64},{1,5},{2,66},{3,7},{4,68},{5,1},{6,70},{7,3},{8,72},{9,13},... | collective-permute-start | bytes 1032200 | tf_op jit(solution)/shard_map/ppermute | solution.py:684
  75.0 4.8 %collective-permute-start.10 = (bf16[384,128]{1,0:T(8,128)(2,1)S(1)}, bf16[384,128]{1,0:T(8,128)(2,1)S(1)}, u32[]{:S(2)}, u32[]{:S(2)}) collective-permute-start(bf16[384,128]{1,0:T(8,128)(2,1)S(1)} %get-tuple-element.61), channel_id=1, source_target_pairs={{0,2},{1,33},{2,4},{3,35},{4,6},{5,37},{6,0},{7,39},{8,10},{9,41},... | collective-permute-start | bytes 294920 | tf_op jit(solution)/shard_map/ppermute | solution.py:684
  76.2 5.8 %collective-permute-start.11 = (bf16[384,128]{1,0:T(8,128)(2,1)S(1)}, bf16[384,128]{1,0:T(8,128)(2,1)S(1)}, u32[]{:S(2)}, u32[]{:S(2)}) collective-permute-start(bf16[384,128]{1,0:T(8,128)(2,1)S(1)} %get-tuple-element.62), channel_id=1, source_target_pairs={{0,4},{1,65},{2,6},{3,67},{4,0},{5,69},{6,2},{7,71},{8,12},{9,73},... | collective-permute-start | bytes 294920 | tf_op jit(solution)/shard_map/ppermute | solution.py:684
  79.0 3.7 %collective-permute-start.12 = (bf16[384,128]{1,0:T(8,128)(2,1)S(1)}, bf16[384,128]{1,0:T(8,128)(2,1)S(1)}, u32[]{:S(2)}, u32[]{:S(2)}) collective-permute-start(bf16[384,128]{1,0:T(8,128)(2,1)S(1)} %get-tuple-element.63), channel_id=1, source_target_pairs={{0,6},{1,97},{2,0},{3,99},{4,2},{5,101},{6,4},{7,103},{8,14},{9,10... | collective-permute-start | bytes 294920 | tf_op jit(solution)/shard_map/ppermute | solution.py:684
  82.8 5.9 %collective-permute-start.14 = (bf16[384,128]{1,0:T(8,128)(2,1)S(1)}, bf16[384,128]{1,0:T(8,128)(2,1)S(1)}, u32[]{:S(2)}, u32[]{:S(2)}) collective-permute-start(bf16[384,128]{1,0:T(8,128)(2,1)S(1)} %get-tuple-element.60), channel_id=1, source_target_pairs={{0,16},{1,17},{2,18},{3,19},{4,20},{5,21},{6,22},{7,23},{8,24},{9,... | collective-permute-start | bytes 294920 | tf_op jit(solution)/shard_map/ppermute | solution.py:684
  86.0 5.7 %collective-permute-start.13 = (bf16[384,128]{1,0:T(8,128)(2,1)S(1)}, bf16[384,128]{1,0:T(8,128)(2,1)S(1)}, u32[]{:S(2)}, u32[]{:S(2)}) collective-permute-start(bf16[384,128]{1,0:T(8,128)(2,1)S(1)} %get-tuple-element.60), channel_id=1, source_target_pairs={{0,8},{1,9},{2,10},{3,11},{4,12},{5,13},{6,14},{7,15},{8,16},{9,17... | collective-permute-start | bytes 294920 | tf_op jit(solution)/shard_map/ppermute | solution.py:684
  86.4 5.3 %collective-permute-start.15 = (bf16[384,128]{1,0:T(8,128)(2,1)S(1)}, bf16[384,128]{1,0:T(8,128)(2,1)S(1)}, u32[]{:S(2)}, u32[]{:S(2)}) collective-permute-start(bf16[384,128]{1,0:T(8,128)(2,1)S(1)} %get-tuple-element.60), channel_id=1, source_target_pairs={{0,24},{1,25},{2,26},{3,27},{4,28},{5,29},{6,30},{7,31},{8,0},{9,1... | collective-permute-start | bytes 294920 | tf_op jit(solution)/shard_map/ppermute | solution.py:684
  91.9 4.6 %collective-permute-start.16 = (bf16[320,128]{1,0:T(8,128)(2,1)S(1)}, bf16[320,128]{1,0:T(8,128)(2,1)S(1)}, u32[]{:S(2)}, u32[]{:S(2)}) collective-permute-start(bf16[320,128]{1,0:T(8,128)(2,1)S(1)} %get-tuple-element.57), channel_id=1, source_target_pairs={{0,2},{1,33},{2,4},{3,35},{4,6},{5,37},{6,0},{7,39},{8,10},{9,41},... | collective-permute-start | bytes 245768 | tf_op jit(solution)/shard_map/ppermute | solution.py:684
  92.6 6.8 %collective-permute-start.18 = (bf16[320,128]{1,0:T(8,128)(2,1)S(1)}, bf16[320,128]{1,0:T(8,128)(2,1)S(1)}, u32[]{:S(2)}, u32[]{:S(2)}) collective-permute-start(bf16[320,128]{1,0:T(8,128)(2,1)S(1)} %get-tuple-element.57), channel_id=1, source_target_pairs={{0,6},{1,97},{2,0},{3,99},{4,2},{5,101},{6,4},{7,103},{8,14},{9,10... | collective-permute-start | bytes 245768 | tf_op jit(solution)/shard_map/ppermute | solution.py:684
  94.7 4.8 %collective-permute-start.17 = (bf16[320,128]{1,0:T(8,128)(2,1)S(1)}, bf16[320,128]{1,0:T(8,128)(2,1)S(1)}, u32[]{:S(2)}, u32[]{:S(2)}) collective-permute-start(bf16[320,128]{1,0:T(8,128)(2,1)S(1)} %get-tuple-element.57), channel_id=1, source_target_pairs={{0,4},{1,65},{2,6},{3,67},{4,0},{5,69},{6,2},{7,71},{8,12},{9,73},... | collective-permute-start | bytes 245768 | tf_op jit(solution)/shard_map/ppermute | solution.py:684
  99.5 7.5 %collective-permute-start.19 = (bf16[1280,128]{1,0:T(8,128)(2,1)S(1)}, bf16[1280,128]{1,0:T(8,128)(2,1)S(1)}, u32[]{:S(2)}, u32[]{:S(2)}) collective-permute-start(bf16[1280,128]{1,0:T(8,128)(2,1)S(1)} %bitcast.97), channel_id=1, source_target_pairs={{0,32},{1,3},{2,34},{3,5},{4,36},{5,7},{6,38},{7,1},{8,40},{9,11},... | collective-permute-start | bytes 983048 | tf_op jit(solution)/shard_map/ppermute | solution.py:684
  99.8 11.5 %collective-permute-start.21 = (bf16[1280,128]{1,0:T(8,128)(2,1)S(1)}, bf16[1280,128]{1,0:T(8,128)(2,1)S(1)}, u32[]{:S(2)}, u32[]{:S(2)}) collective-permute-start(bf16[1280,128]{1,0:T(8,128)(2,1)S(1)} %bitcast.98), channel_id=1, source_target_pairs={{0,96},{1,7},{2,98},{3,1},{4,100},{5,3},{6,102},{7,5},{8,104},{9,1... | collective-permute-start | bytes 983048 | tf_op jit(solution)/shard_map/ppermute | solution.py:684
  102.2 8.9 %collective-permute-start.20 = (bf16[1280,128]{1,0:T(8,128)(2,1)S(1)}, bf16[1280,128]{1,0:T(8,128)(2,1)S(1)}, u32[]{:S(2)}, u32[]{:S(2)}) collective-permute-start(bf16[1280,128]{1,0:T(8,128)(2,1)S(1)} %bitcast.99), channel_id=1, source_target_pairs={{0,64},{1,5},{2,66},{3,7},{4,68},{5,1},{6,70},{7,3},{8,72},{9,13},... | collective-permute-start | bytes 983048 | tf_op jit(solution)/shard_map/ppermute | solution.py:684
  103.4 16.0 %copy-start = (f32[256,512]{1,0:T(8,128)S(1)}, f32[256,512]{1,0:T(8,128)}, u32[]{:S(2)}) copy-start(f32[256,512]{1,0:T(8,128)} %refs_1_.1) | copy-start | bytes 1572868
  103.4 15.9 %copy-start.1 = (f32[512,256]{1,0:T(8,128)S(1)}, f32[512,256]{1,0:T(8,128)}, u32[]{:S(2)}) copy-start(f32[512,256]{1,0:T(8,128)} %refs_4_.1) | copy-start | bytes 1572868
  103.4 15.9 %copy-start.2 = (f32[3,3,512]{2,1,0:T(4,128)S(1)}, f32[3,3,512]{2,1,0:T(4,128)}, u32[]{:S(2)}) copy-start(f32[3,3,512]{2,1,0:T(4,128)} %refs_3_.1) | copy-start | bytes 55300
  103.4 15.9 %copy-start.3 = (f32[3,3,256]{2,1,0:T(4,128)S(1)}, f32[3,3,256]{2,1,0:T(4,128)}, u32[]{:S(2)}) copy-start(f32[3,3,256]{2,1,0:T(4,128)} %refs_0_.1) | copy-start | bytes 27652
  103.4 15.9 %copy-start.4 = (f32[5]{0:T(128)S(1)}, f32[5]{0:T(128)}, u32[]{:S(2)}) copy-start(f32[5]{0:T(128)} %get-tuple-element.34.sums) | copy-start | bytes 64
  111.3 8.0 %collective-permute-start.22 = (bf16[5120,128]{1,0:T(8,128)(2,1)S(1)}, bf16[5120,128]{1,0:T(8,128)(2,1)S(1)}, u32[]{:S(2)}, u32[]{:S(2)}) collective-permute-start(bf16[5120,128]{1,0:T(8,128)(2,1)S(1)} %bitcast.81), channel_id=1, source_target_pairs={{0,1},{1,0},{2,3},{3,2},{4,5},{5,4},{6,7},{7,6},{8,9},{9,8},{10,11... | collective-permute-start | bytes 3932168 | tf_op jit(solution)/shard_map/ppermute | solution.py:733
  (1 other events, 0.6 us)

commit v6 on v5

--- a/solution.py
+++ b/solution.py
@@ -461,9 +461,12 @@
     )(limits, x, t, *halos, k1, p1, taps, k2, p2)
 
 
-def edges_kernel(xt, tt, xb, tb, xl, tl, xr, tr, up, down, ahead, back):
+def rows_kernel(xt, tt, xb, tb, up, down):
     up[...] = jnp.concatenate([xt[0:ROWS], tt[0:2]], axis=0)
     down[...] = jnp.concatenate([xb[8 - ROWS : 8], tb[6:8]], axis=0)
+
+
+def columns_kernel(xl, tl, xr, tr, ahead, back):
     col = lax.broadcasted_iota(jnp.int32, ahead.shape, 1)
     x, t = xl[:, 0:8, :].astype(F32), tl[:, 0:8, :].astype(F32)
     ahead[...] = jnp.where((col >= 5) & (col < 7), pltpu.roll(t, 5, 1), x).astype(BF16)
@@ -479,14 +482,19 @@
         pl.BlockSpec((rows, 16, chan), lambda n: (0, 0, 0)),
         pl.BlockSpec((rows, 16, chan), lambda n: (0, cols // 16 - 1, 0)),
     ]
-    shapes = [(ROWS + 2, cols, chan)] * 2 + [(rows, 8, chan)] * 2
-    return pl.pallas_call(
-        edges_kernel,
-        grid=(1,),
-        out_shape=[jax.ShapeDtypeStruct(s, BF16) for s in shapes],
-        in_specs=[s for s in specs for _ in range(2)],
-        out_specs=[pl.BlockSpec(s, lambda n: (0, 0, 0)) for s in shapes],
-    )(*[x, t] * 4)
+    outs = []
+    for kernel, pair, shape in (
+        (rows_kernel, specs[:2], (ROWS + 2, cols, chan)),
+        (columns_kernel, specs[2:], (rows, 8, chan)),
+    ):
+        outs += pl.pallas_call(
+            kernel,
+            grid=(1,),
+            out_shape=[jax.ShapeDtypeStruct(shape, BF16)] * 2,
+            in_specs=[s for s in pair for _ in range(2)],
+            out_specs=[pl.BlockSpec(shape, lambda n: (0, 0, 0))] * 2,
+        )(x, t, x, t)
+    return outs
 
 
 def update_kernel(

time: 127 us -> 128 us (level)
  Pallas kernels: 42.7 us -> 44.2 us
    ppermute x6, starting transfers between devices: 17.4 us -> 15.9 us  [shift(): return lax.ppermute(block, ('ty', 'tx'), pairs)]
    pallas_call x1 -> x2, Pallas kernels: 3.17 us -> 4.69 us  [edges(): pl.pallas_call(kernel, grid=(1,), out_shape=[jax.ShapeDtypeStruct(shape,...]
    ppermute x15, starting transfers between devices: 21.4 us -> 22.8 us  [send(): return lax.ppermute(block, ('rep', 'ty', 'tx'), pairs)]
  transfers between devices with their start and end apart: 23 -> 23, of which waited for: 11 -> 12; matrix products, arithmetic and copies ran while one was open for 1% -> 1% of each run, Pallas kernels for 0% -> 2%
where the time goes in v6:
time: 128 us
  Pallas kernels  44.2 us (35%)
  starting transfers between devices  44.1 us (34%)
  waiting for transfers between devices  34.3 us (27%)
  other arithmetic  2.21 us (2%)
  local copies, waits for them, and re-layouts  2.09 us (2%)
  between operations  1.33 us (1%)
    pallas_call x1, Pallas kernels, tile_step(): pl.pallas_call(tile_kernel, out_shape=(jax.ShapeDtypeStruct(x.shape, BF16...  32.2 us
    ppermute x15, waiting for transfers between devices, send(): return lax.ppermute(block, ('rep', 'ty', 'tx'), pairs)  25.4 us
    ppermute x15, starting transfers between devices, send(): return lax.ppermute(block, ('rep', 'ty', 'tx'), pairs)  22.8 us
    ppermute x6, starting transfers between devices, shift(): return lax.ppermute(block, ('ty', 'tx'), pairs)  15.9 us
    pallas_call x1, Pallas kernels, update(): pl.pallas_call(update_kernel, grid=(4 * per,), out_shape=shapes + shapes,...  7.29 us
    ppermute x1, starting transfers between devices, reduced(): return (small, share, lax.ppermute(share, 'tx', cores))  5.36 us
    pallas_call x2, Pallas kernels, edges(): pl.pallas_call(kernel, grid=(1,), out_shape=[jax.ShapeDtypeStruct(shape,...  4.69 us
    ppermute x1, waiting for transfers between devices, reduced(): got = lax.ppermute(send, 'tx', cores)  3.17 us
  transfers between devices with their start and end apart: 23, of which 12 were waited for; matrix products, arithmetic and copies ran while one was open for 1% of the time, Pallas kernels for 2%

profile of v6, /device:TPU:1, one launch (start us, length us, event | category | flops | bytes accessed | tf_op | source)
XLA Modules:
  0.0 128.2 jit_solution(4260727252905700510)
XLA Ops:
  0.6 1.8 %shard_map.158 = (bf16[8,32,256]{2,1,0:T(8,128)(2,1)}, bf16[8,32,256]{2,1,0:T(8,128)(2,1)}) custom-call(bf16[96,32,256]{2,1,0:T(8,128)(2,1)} %bitcast.83, bf16[96,32,256]{2,1,0:T(8,128)(2,1)} %bitcast.88, bf16[96,32,256]{2,1,0:T(8,128)(2,1)} %bitcast.84, bf16[96,32,256]{2,1,0:T(8,128)(2,1)} %bitcast.89), custom_call_target="tpu_custom_call" | custom-call | tf_op jit(solution)/shard_map/pallas_call | solution.py:490
  2.5 4.4 %collective-permute-start = (bf16[8,32,256]{2,1,0:T(8,128)(2,1)}, bf16[8,32,256]{2,1,0:T(8,128)(2,1)S(1)}, u32[]{:S(2)}, u32[]{:S(2)}) collective-permute-start(bf16[8,32,256]{2,1,0:T(8,128)(2,1)} %get-tuple-element.29), channel_id=1, source_target_pairs={{0,8},{1,9},{2,10},{3,11},{4,12},{5,13},{6,14},{7,15},{8,16},{9,17... | collective-permute-start | bytes 393224 | tf_op jit(solution)/shard_map/ppermute | solution.py:664
  6.8 1.3 %collective-permute-start.1 = (bf16[8,32,256]{2,1,0:T(8,128)(2,1)}, bf16[8,32,256]{2,1,0:T(8,128)(2,1)S(1)}, u32[]{:S(2)}, u32[]{:S(2)}) collective-permute-start(bf16[8,32,256]{2,1,0:T(8,128)(2,1)} %get-tuple-element.30), channel_id=1, source_target_pairs={{8,0},{9,1},{10,2},{11,3},{12,4},{13,5},{14,6},{15,7},{16,8},{17,9... | collective-permute-start | bytes 393224 | tf_op jit(solution)/shard_map/ppermute | solution.py:664
  8.1 2.9 %shard_map.159 = (bf16[96,8,256]{2,1,0:T(8,128)(2,1)}, bf16[96,8,256]{2,1,0:T(8,128)(2,1)}) custom-call(bf16[96,32,256]{2,1,0:T(8,128)(2,1)} %bitcast.85, bf16[96,32,256]{2,1,0:T(8,128)(2,1)} %bitcast.90, bf16[96,32,256]{2,1,0:T(8,128)(2,1)} %bitcast.86, bf16[96,32,256]{2,1,0:T(8,128)(2,1)} %bitcast.91), custom_call_target="tpu_custom_call" | custom-call | tf_op jit(solution)/shard_map/pallas_call | solution.py:490
  11.0 2.9 %collective-permute-start.2 = (bf16[96,8,256]{2,1,0:T(8,128)(2,1)}, bf16[96,8,256]{2,1,0:T(8,128)(2,1)S(1)}, u32[]{:S(2)}, u32[]{:S(2)}) collective-permute-start(bf16[96,8,256]{2,1,0:T(8,128)(2,1)} %get-tuple-element.31), channel_id=1, source_target_pairs={{1,0},{2,1},{3,2},{4,3},{5,4},{6,5},{7,6},{9,8},{10,9},{11,10},{12... | collective-permute-start | bytes 1179656 | tf_op jit(solution)/shard_map/ppermute | solution.py:664
  13.9 3.0 %collective-permute-start.3 = (bf16[96,8,256]{2,1,0:T(8,128)(2,1)}, bf16[96,8,256]{2,1,0:T(8,128)(2,1)}, u32[]{:S(2)}, u32[]{:S(2)}) collective-permute-start(bf16[96,8,256]{2,1,0:T(8,128)(2,1)} %get-tuple-element.32), channel_id=1, source_target_pairs={{0,1},{1,2},{2,3},{3,4},{4,5},{5,6},{6,7},{8,9},{9,10},{10,11},{11... | collective-permute-start | bytes 1179656 | tf_op jit(solution)/shard_map/ppermute | solution.py:664
  17.0 2.4 %collective-permute-start.5 = (bf16[16,8,256]{2,1,0:T(8,128)(2,1)S(1)}, bf16[16,8,256]{2,1,0:T(8,128)(2,1)S(1)}, u32[]{:S(2)}, u32[]{:S(2)}) collective-permute-start(bf16[16,8,256]{2,1,0:T(8,128)(2,1)S(1)} %get-tuple-element.55), channel_id=1, source_target_pairs={{0,1},{1,2},{2,3},{3,4},{4,5},{5,6},{6,7},{8,9},{9,10},{10,11},{11... | collective-permute-start | bytes 196616 | tf_op jit(solution)/shard_map/ppermute | solution.py:664
  19.4 1.9 %collective-permute-start.4 = (bf16[16,8,256]{2,1,0:T(8,128)(2,1)S(1)}, bf16[16,8,256]{2,1,0:T(8,128)(2,1)S(1)}, u32[]{:S(2)}, u32[]{:S(2)}) collective-permute-start(bf16[16,8,256]{2,1,0:T(8,128)(2,1)S(1)} %get-tuple-element.56), channel_id=1, source_target_pairs={{1,0},{2,1},{3,2},{4,3},{5,4},{6,5},{7,6},{9,8},{10,9},{11,10},{12... | collective-permute-start | bytes 196616 | tf_op jit(solution)/shard_map/ppermute | solution.py:664
  22.5 2.5 %collective-permute-done.4.right_ends = bf16[16,8,256]{2,1,0:T(8,128)(2,1)S(1)} collective-permute-done((bf16[16,8,256]{2,1,0:T(8,128)(2,1)S(1)}, bf16[16,8,256]{2,1,0:T(8,128)(2,1)S(1)}, u32[]{:S(2)}, u32[]{:S(2)}) %collective-permute-start.4) | collective-permute-done | bytes 65568 | tf_op jit(solution)/shard_map/ppermute | solution.py:664
  25.8 32.2 %shard_map.160 = (bf16[96,32,256]{2,1,0:T(8,128)(2,1)}, bf16[5184,128]{1,0:T(8,128)(2,1)}, bf16[5184,128]{1,0:T(8,128)(2,1)}, f32[5]{0:T(128)}) custom-call(s32[5]{0:T(128)} %stack.66.limits, bf16[96,32,256]{2,1,0:T(8,128)(2,1)} %bitcast.87, bf16[96,32,256]{2,1,0:T(8,128)(2,1)} %bitcast.92, bf16[8,32,256]{2,1,0:T(8,128)(2,1)} %copy-done.5, ...), custom_call_target="tpu_custom_call" | custom-call | flops 8999999488 | bytes 20000000 | tf_op jit(solution)/shard_map/pallas_call | solution.py:419
  58.2 3.2 %collective-permute-done.6 = bf16[5184,128]{1,0:T(8,128)(2,1)S(1)} collective-permute-done((bf16[5184,128]{1,0:T(8,128)(2,1)}, bf16[5184,128]{1,0:T(8,128)(2,1)S(1)}, u32[]{:S(2)}, u32[]{:S(2)}) %collective-permute-start.6) | collective-permute-done | bytes 1327136 | tf_op jit(solution)/shard_map/ppermute | solution.py:732
  61.3 1.7 %add_convert_fusion = bf16[5184,128]{1,0:T(8,128)(2,1)S(1)} fusion(bf16[5184,128]{1,0:T(8,128)(2,1)S(1)} %collective-permute-done.6, bf16[5184,128]{1,0:T(8,128)(2,1)} %get-tuple-element.35), kind=kLoop, calls=%fused_computation | loop fusion | flops 2654208 | bytes 3981312 | tf_op jit(solution)/shard_map/convert_element_type | solution.py:733
  63.3 1.5 %collective-permute-start.7 = (bf16[1344,128]{1,0:T(8,128)(2,1)S(1)}, bf16[1344,128]{1,0:T(8,128)(2,1)S(1)}, u32[]{:S(2)}, u32[]{:S(2)}) collective-permute-start(bf16[1344,128]{1,0:T(8,128)(2,1)S(1)} %get-tuple-element.64), channel_id=1, source_target_pairs={{0,32},{1,3},{2,34},{3,5},{4,36},{5,7},{6,38},{7,1},{8,40},{9,11},... | collective-permute-start | bytes 1032200 | tf_op jit(solution)/shard_map/ppermute | solution.py:692
  64.7 1.5 %collective-permute-start.9 = (bf16[1344,128]{1,0:T(8,128)(2,1)S(1)}, bf16[1344,128]{1,0:T(8,128)(2,1)S(1)}, u32[]{:S(2)}, u32[]{:S(2)}) collective-permute-start(bf16[1344,128]{1,0:T(8,128)(2,1)S(1)} %get-tuple-element.65), channel_id=1, source_target_pairs={{0,96},{1,7},{2,98},{3,1},{4,100},{5,3},{6,102},{7,5},{8,104},{9,1... | collective-permute-start | bytes 1032200 | tf_op jit(solution)/shard_map/ppermute | solution.py:692
  66.2 1.3 collective-permute-start.8
  67.4 7.4 %collective-permute-done.7 = bf16[1344,128]{1,0:T(8,128)(2,1)S(1)} collective-permute-done((bf16[1344,128]{1,0:T(8,128)(2,1)S(1)}, bf16[1344,128]{1,0:T(8,128)(2,1)S(1)}, u32[]{:S(2)}, u32[]{:S(2)}) %collective-permute-start.7) | collective-permute-done | bytes 344096 | tf_op jit(solution)/shard_map/ppermute | solution.py:692
  75.1 1.2 collective-permute-start.10
  76.3 2.8 %collective-permute-start.11 = (bf16[384,128]{1,0:T(8,128)(2,1)S(1)}, bf16[384,128]{1,0:T(8,128)(2,1)S(1)}, u32[]{:S(2)}, u32[]{:S(2)}) collective-permute-start(bf16[384,128]{1,0:T(8,128)(2,1)S(1)} %get-tuple-element.62), channel_id=1, source_target_pairs={{0,4},{1,65},{2,6},{3,67},{4,0},{5,69},{6,2},{7,71},{8,12},{9,73},... | collective-permute-start | bytes 294920 | tf_op jit(solution)/shard_map/ppermute | solution.py:692
  80.0 2.2 %collective-permute-done.11 = bf16[384,128]{1,0:T(8,128)(2,1)S(1)} collective-permute-done((bf16[384,128]{1,0:T(8,128)(2,1)S(1)}, bf16[384,128]{1,0:T(8,128)(2,1)S(1)}, u32[]{:S(2)}, u32[]{:S(2)}) %collective-permute-start.11) | collective-permute-done | bytes 98336 | tf_op jit(solution)/shard_map/ppermute | solution.py:692
  83.0 4.4 %collective-permute-start.14 = (bf16[384,128]{1,0:T(8,128)(2,1)S(1)}, bf16[384,128]{1,0:T(8,128)(2,1)S(1)}, u32[]{:S(2)}, u32[]{:S(2)}) collective-permute-start(bf16[384,128]{1,0:T(8,128)(2,1)S(1)} %get-tuple-element.60), channel_id=1, source_target_pairs={{0,16},{1,17},{2,18},{3,19},{4,20},{5,21},{6,22},{7,23},{8,24},{9,... | collective-permute-start | bytes 294920 | tf_op jit(solution)/shard_map/ppermute | solution.py:692
  88.1 1.9 %collective-permute-start.15 = (bf16[384,128]{1,0:T(8,128)(2,1)S(1)}, bf16[384,128]{1,0:T(8,128)(2,1)S(1)}, u32[]{:S(2)}, u32[]{:S(2)}) collective-permute-start(bf16[384,128]{1,0:T(8,128)(2,1)S(1)} %get-tuple-element.60), channel_id=1, source_target_pairs={{0,24},{1,25},{2,26},{3,27},{4,28},{5,29},{6,30},{7,31},{8,0},{9,1... | collective-permute-start | bytes 294920 | tf_op jit(solution)/shard_map/ppermute | solution.py:692
  90.0 2.9 %collective-permute-done.13 = bf16[384,128]{1,0:T(8,128)(2,1)S(1)} collective-permute-done((bf16[384,128]{1,0:T(8,128)(2,1)S(1)}, bf16[384,128]{1,0:T(8,128)(2,1)S(1)}, u32[]{:S(2)}, u32[]{:S(2)}) %collective-permute-start.13) | collective-permute-done | bytes 98336 | tf_op jit(solution)/shard_map/ppermute | solution.py:692
  94.0 2.0 %collective-permute-start.18 = (bf16[320,128]{1,0:T(8,128)(2,1)S(1)}, bf16[320,128]{1,0:T(8,128)(2,1)S(1)}, u32[]{:S(2)}, u32[]{:S(2)}) collective-permute-start(bf16[320,128]{1,0:T(8,128)(2,1)S(1)} %get-tuple-element.57), channel_id=1, source_target_pairs={{0,6},{1,97},{2,0},{3,99},{4,2},{5,101},{6,4},{7,103},{8,14},{9,10... | collective-permute-start | bytes 245768 | tf_op jit(solution)/shard_map/ppermute | solution.py:692
  96.2 1.6 %collective-permute-done.16 = bf16[320,128]{1,0:T(8,128)(2,1)S(1)} collective-permute-done((bf16[320,128]{1,0:T(8,128)(2,1)S(1)}, bf16[320,128]{1,0:T(8,128)(2,1)S(1)}, u32[]{:S(2)}, u32[]{:S(2)}) %collective-permute-start.16) | collective-permute-done | bytes 81952 | tf_op jit(solution)/shard_map/ppermute | solution.py:692
  97.8 3.0 %collective-permute-done.17 = bf16[320,128]{1,0:T(8,128)(2,1)S(1)} collective-permute-done((bf16[320,128]{1,0:T(8,128)(2,1)S(1)}, bf16[320,128]{1,0:T(8,128)(2,1)S(1)}, u32[]{:S(2)}, u32[]{:S(2)}) %collective-permute-start.17) | collective-permute-done | bytes 81952 | tf_op jit(solution)/shard_map/ppermute | solution.py:692
  101.8 1.7 %collective-permute-start.21 = (bf16[1280,128]{1,0:T(8,128)(2,1)S(1)}, bf16[1280,128]{1,0:T(8,128)(2,1)S(1)}, u32[]{:S(2)}, u32[]{:S(2)}) collective-permute-start(bf16[1280,128]{1,0:T(8,128)(2,1)S(1)} %bitcast.98), channel_id=1, source_target_pairs={{0,96},{1,7},{2,98},{3,1},{4,100},{5,3},{6,102},{7,5},{8,104},{9,1... | collective-permute-start | bytes 983048 | tf_op jit(solution)/shard_map/ppermute | solution.py:692
  103.5 1.0 collective-permute-start.20
  104.9 3.5 %collective-permute-done.19 = bf16[1280,128]{1,0:T(8,128)(2,1)S(1)} collective-permute-done((bf16[1280,128]{1,0:T(8,128)(2,1)S(1)}, bf16[1280,128]{1,0:T(8,128)(2,1)S(1)}, u32[]{:S(2)}, u32[]{:S(2)}) %collective-permute-start.19) | collective-permute-done | bytes 327712 | tf_op jit(solution)/shard_map/ppermute | solution.py:692
  108.4 4.1 %collective-permute-done.20 = bf16[1280,128]{1,0:T(8,128)(2,1)S(1)} collective-permute-done((bf16[1280,128]{1,0:T(8,128)(2,1)S(1)}, bf16[1280,128]{1,0:T(8,128)(2,1)S(1)}, u32[]{:S(2)}, u32[]{:S(2)}) %collective-permute-start.20) | collective-permute-done | bytes 327712 | tf_op jit(solution)/shard_map/ppermute | solution.py:692
  112.7 5.4 %collective-permute-start.22 = (bf16[5120,128]{1,0:T(8,128)(2,1)S(1)}, bf16[5120,128]{1,0:T(8,128)(2,1)S(1)}, u32[]{:S(2)}, u32[]{:S(2)}) collective-permute-start(bf16[5120,128]{1,0:T(8,128)(2,1)S(1)} %bitcast.81), channel_id=1, source_target_pairs={{0,1},{1,0},{2,3},{3,2},{4,5},{5,4},{6,7},{7,6},{8,9},{9,8},{10,11... | collective-permute-start | bytes 3932168 | tf_op jit(solution)/shard_map/ppermute | solution.py:741
  118.0 2.7 %collective-permute-done.22.other_ref = bf16[5120,128]{1,0:T(8,128)(2,1)S(1)} collective-permute-done((bf16[5120,128]{1,0:T(8,128)(2,1)S(1)}, bf16[5120,128]{1,0:T(8,128)(2,1)S(1)}, u32[]{:S(2)}, u32[]{:S(2)}) %collective-permute-start.22) | collective-permute-done | bytes 1310752 | tf_op jit(solution)/shard_map/ppermute | solution.py:741
  120.7 7.3 %shard_map.161 = (f32[3,3,256]{2,1,0:T(4,128)}, f32[256,512]{1,0:T(8,128)}, f32[4,512,512]{2,1,0:T(8,128)}, f32[3,3,512]{2,1,0:T(4,128)}, f32[512,256]{1,0:T(8,1...) custom-call(s32[1]{0:T(128)} %bitcast.4.where, ...), custom_call_target="tpu_custom_call" | custom-call | tf_op jit(solution)/shard_map/pallas_call | solution.py:636
  (76 shorter events, 7.5 us)
Async XLA Ops:
  2.5 14.4 %collective-permute-start = (bf16[8,32,256]{2,1,0:T(8,128)(2,1)}, bf16[8,32,256]{2,1,0:T(8,128)(2,1)S(1)}, u32[]{:S(2)}, u32[]{:S(2)}) collective-permute-start(bf16[8,32,256]{2,1,0:T(8,128)(2,1)} %get-tuple-element.29), channel_id=1, source_target_pairs={{0,8},{1,9},{2,10},{3,11},{4,12},{5,13},{6,14},{7,15},{8,16},{9,17... | collective-permute-start | bytes 393224 | tf_op jit(solution)/shard_map/ppermute | solution.py:664
  6.8 10.1 %collective-permute-start.1 = (bf16[8,32,256]{2,1,0:T(8,128)(2,1)}, bf16[8,32,256]{2,1,0:T(8,128)(2,1)S(1)}, u32[]{:S(2)}, u32[]{:S(2)}) collective-permute-start(bf16[8,32,256]{2,1,0:T(8,128)(2,1)} %get-tuple-element.30), channel_id=1, source_target_pairs={{8,0},{9,1},{10,2},{11,3},{12,4},{13,5},{14,6},{15,7},{16,8},{17,9... | collective-permute-start | bytes 393224 | tf_op jit(solution)/shard_map/ppermute | solution.py:664
  11.0 14.0 %collective-permute-start.2 = (bf16[96,8,256]{2,1,0:T(8,128)(2,1)}, bf16[96,8,256]{2,1,0:T(8,128)(2,1)S(1)}, u32[]{:S(2)}, u32[]{:S(2)}) collective-permute-start(bf16[96,8,256]{2,1,0:T(8,128)(2,1)} %get-tuple-element.31), channel_id=1, source_target_pairs={{1,0},{2,1},{3,2},{4,3},{5,4},{6,5},{7,6},{9,8},{10,9},{11,10},{12... | collective-permute-start | bytes 1179656 | tf_op jit(solution)/shard_map/ppermute | solution.py:664
  13.9 11.1 %collective-permute-start.3 = (bf16[96,8,256]{2,1,0:T(8,128)(2,1)}, bf16[96,8,256]{2,1,0:T(8,128)(2,1)}, u32[]{:S(2)}, u32[]{:S(2)}) collective-permute-start(bf16[96,8,256]{2,1,0:T(8,128)(2,1)} %get-tuple-element.32), channel_id=1, source_target_pairs={{0,1},{1,2},{2,3},{3,4},{4,5},{5,6},{6,7},{8,9},{9,10},{10,11},{11... | collective-permute-start | bytes 1179656 | tf_op jit(solution)/shard_map/ppermute | solution.py:664
  16.9 8.1 %copy-start.5 = (bf16[8,32,256]{2,1,0:T(8,128)(2,1)}, bf16[8,32,256]{2,1,0:T(8,128)(2,1)S(1)}, u32[]{:S(2)}) copy-start(bf16[8,32,256]{2,1,0:T(8,128)(2,1)S(1)} %collective-permute-done.top_ref) | copy-start | bytes 393220
  16.9 8.1 %copy-start.6 = (bf16[8,32,256]{2,1,0:T(8,128)(2,1)}, bf16[8,32,256]{2,1,0:T(8,128)(2,1)S(1)}, u32[]{:S(2)}) copy-start(bf16[8,32,256]{2,1,0:T(8,128)(2,1)S(1)} %collective-permute-done.1.bot_ref) | copy-start | bytes 393220
  17.0 5.5 %collective-permute-start.5 = (bf16[16,8,256]{2,1,0:T(8,128)(2,1)S(1)}, bf16[16,8,256]{2,1,0:T(8,128)(2,1)S(1)}, u32[]{:S(2)}, u32[]{:S(2)}) collective-permute-start(bf16[16,8,256]{2,1,0:T(8,128)(2,1)S(1)} %get-tuple-element.55), channel_id=1, source_target_pairs={{0,1},{1,2},{2,3},{3,4},{4,5},{5,6},{6,7},{8,9},{9,10},{10,11},{11... | collective-permute-start | bytes 196616 | tf_op jit(solution)/shard_map/ppermute | solution.py:664
  19.4 5.6 %collective-permute-start.4 = (bf16[16,8,256]{2,1,0:T(8,128)(2,1)S(1)}, bf16[16,8,256]{2,1,0:T(8,128)(2,1)S(1)}, u32[]{:S(2)}, u32[]{:S(2)}) collective-permute-start(bf16[16,8,256]{2,1,0:T(8,128)(2,1)S(1)} %get-tuple-element.56), channel_id=1, source_target_pairs={{1,0},{2,1},{3,2},{4,3},{5,4},{6,5},{7,6},{9,8},{10,9},{11,10},{12... | collective-permute-start | bytes 196616 | tf_op jit(solution)/shard_map/ppermute | solution.py:664
  22.5 2.5 %copy-start.8 = (bf16[16,8,256]{2,1,0:T(8,128)(2,1)}, bf16[16,8,256]{2,1,0:T(8,128)(2,1)S(1)}, u32[]{:S(2)}) copy-start(bf16[16,8,256]{2,1,0:T(8,128)(2,1)S(1)} %collective-permute-done.5.left_ends) | copy-start | bytes 196612
  25.0 0.8 copy-start.7
  58.0 3.3 %collective-permute-start.6 = (bf16[5184,128]{1,0:T(8,128)(2,1)}, bf16[5184,128]{1,0:T(8,128)(2,1)S(1)}, u32[]{:S(2)}, u32[]{:S(2)}) collective-permute-start(bf16[5184,128]{1,0:T(8,128)(2,1)} %get-tuple-element.36), channel_id=1, source_target_pairs={{0,1},{1,0},{2,3},{3,2},{4,5},{5,4},{6,7},{7,6},{8,9},{9,8},{10,11... | collective-permute-start | bytes 3981320 | tf_op jit(solution)/shard_map/ppermute | solution.py:732
  63.3 11.5 %collective-permute-start.7 = (bf16[1344,128]{1,0:T(8,128)(2,1)S(1)}, bf16[1344,128]{1,0:T(8,128)(2,1)S(1)}, u32[]{:S(2)}, u32[]{:S(2)}) collective-permute-start(bf16[1344,128]{1,0:T(8,128)(2,1)S(1)} %get-tuple-element.64), channel_id=1, source_target_pairs={{0,32},{1,3},{2,34},{3,5},{4,36},{5,7},{6,38},{7,1},{8,40},{9,11},... | collective-permute-start | bytes 1032200 | tf_op jit(solution)/shard_map/ppermute | solution.py:692
  64.7 10.1 %collective-permute-start.9 = (bf16[1344,128]{1,0:T(8,128)(2,1)S(1)}, bf16[1344,128]{1,0:T(8,128)(2,1)S(1)}, u32[]{:S(2)}, u32[]{:S(2)}) collective-permute-start(bf16[1344,128]{1,0:T(8,128)(2,1)S(1)} %get-tuple-element.65), channel_id=1, source_target_pairs={{0,96},{1,7},{2,98},{3,1},{4,100},{5,3},{6,102},{7,5},{8,104},{9,1... | collective-permute-start | bytes 1032200 | tf_op jit(solution)/shard_map/ppermute | solution.py:692
  66.2 8.6 %collective-permute-start.8 = (bf16[1344,128]{1,0:T(8,128)(2,1)S(1)}, bf16[1344,128]{1,0:T(8,128)(2,1)S(1)}, u32[]{:S(2)}, u32[]{:S(2)}) collective-permute-start(bf16[1344,128]{1,0:T(8,128)(2,1)S(1)} %get-tuple-element.66), channel_id=1, source_target_pairs={{0,64},{1,5},{2,66},{3,7},{4,68},{5,1},{6,70},{7,3},{8,72},{9,13},... | collective-permute-start | bytes 1032200 | tf_op jit(solution)/shard_map/ppermute | solution.py:692
  75.1 4.8 %collective-permute-start.10 = (bf16[384,128]{1,0:T(8,128)(2,1)S(1)}, bf16[384,128]{1,0:T(8,128)(2,1)S(1)}, u32[]{:S(2)}, u32[]{:S(2)}) collective-permute-start(bf16[384,128]{1,0:T(8,128)(2,1)S(1)} %get-tuple-element.61), channel_id=1, source_target_pairs={{0,2},{1,33},{2,4},{3,35},{4,6},{5,37},{6,0},{7,39},{8,10},{9,41},... | collective-permute-start | bytes 294920 | tf_op jit(solution)/shard_map/ppermute | solution.py:692
  76.3 5.8 %collective-permute-start.11 = (bf16[384,128]{1,0:T(8,128)(2,1)S(1)}, bf16[384,128]{1,0:T(8,128)(2,1)S(1)}, u32[]{:S(2)}, u32[]{:S(2)}) collective-permute-start(bf16[384,128]{1,0:T(8,128)(2,1)S(1)} %get-tuple-element.62), channel_id=1, source_target_pairs={{0,4},{1,65},{2,6},{3,67},{4,0},{5,69},{6,2},{7,71},{8,12},{9,73},... | collective-permute-start | bytes 294920 | tf_op jit(solution)/shard_map/ppermute | solution.py:692
  79.1 3.7 %collective-permute-start.12 = (bf16[384,128]{1,0:T(8,128)(2,1)S(1)}, bf16[384,128]{1,0:T(8,128)(2,1)S(1)}, u32[]{:S(2)}, u32[]{:S(2)}) collective-permute-start(bf16[384,128]{1,0:T(8,128)(2,1)S(1)} %get-tuple-element.63), channel_id=1, source_target_pairs={{0,6},{1,97},{2,0},{3,99},{4,2},{5,101},{6,4},{7,103},{8,14},{9,10... | collective-permute-start | bytes 294920 | tf_op jit(solution)/shard_map/ppermute | solution.py:692
  83.0 7.1 %collective-permute-start.14 = (bf16[384,128]{1,0:T(8,128)(2,1)S(1)}, bf16[384,128]{1,0:T(8,128)(2,1)S(1)}, u32[]{:S(2)}, u32[]{:S(2)}) collective-permute-start(bf16[384,128]{1,0:T(8,128)(2,1)S(1)} %get-tuple-element.60), channel_id=1, source_target_pairs={{0,16},{1,17},{2,18},{3,19},{4,20},{5,21},{6,22},{7,23},{8,24},{9,... | collective-permute-start | bytes 294920 | tf_op jit(solution)/shard_map/ppermute | solution.py:692
  87.4 5.6 %collective-permute-start.13 = (bf16[384,128]{1,0:T(8,128)(2,1)S(1)}, bf16[384,128]{1,0:T(8,128)(2,1)S(1)}, u32[]{:S(2)}, u32[]{:S(2)}) collective-permute-start(bf16[384,128]{1,0:T(8,128)(2,1)S(1)} %get-tuple-element.60), channel_id=1, source_target_pairs={{0,8},{1,9},{2,10},{3,11},{4,12},{5,13},{6,14},{7,15},{8,16},{9,17... | collective-permute-start | bytes 294920 | tf_op jit(solution)/shard_map/ppermute | solution.py:692
  88.1 4.9 %collective-permute-start.15 = (bf16[384,128]{1,0:T(8,128)(2,1)S(1)}, bf16[384,128]{1,0:T(8,128)(2,1)S(1)}, u32[]{:S(2)}, u32[]{:S(2)}) collective-permute-start(bf16[384,128]{1,0:T(8,128)(2,1)S(1)} %get-tuple-element.60), channel_id=1, source_target_pairs={{0,24},{1,25},{2,26},{3,27},{4,28},{5,29},{6,30},{7,31},{8,0},{9,1... | collective-permute-start | bytes 294920 | tf_op jit(solution)/shard_map/ppermute | solution.py:692
  93.2 4.6 %collective-permute-start.16 = (bf16[320,128]{1,0:T(8,128)(2,1)S(1)}, bf16[320,128]{1,0:T(8,128)(2,1)S(1)}, u32[]{:S(2)}, u32[]{:S(2)}) collective-permute-start(bf16[320,128]{1,0:T(8,128)(2,1)S(1)} %get-tuple-element.57), channel_id=1, source_target_pairs={{0,2},{1,33},{2,4},{3,35},{4,6},{5,37},{6,0},{7,39},{8,10},{9,41},... | collective-permute-start | bytes 245768 | tf_op jit(solution)/shard_map/ppermute | solution.py:692
  94.0 6.8 %collective-permute-start.18 = (bf16[320,128]{1,0:T(8,128)(2,1)S(1)}, bf16[320,128]{1,0:T(8,128)(2,1)S(1)}, u32[]{:S(2)}, u32[]{:S(2)}) collective-permute-start(bf16[320,128]{1,0:T(8,128)(2,1)S(1)} %get-tuple-element.57), channel_id=1, source_target_pairs={{0,6},{1,97},{2,0},{3,99},{4,2},{5,101},{6,4},{7,103},{8,14},{9,10... | collective-permute-start | bytes 245768 | tf_op jit(solution)/shard_map/ppermute | solution.py:692
  96.0 4.8 %collective-permute-start.17 = (bf16[320,128]{1,0:T(8,128)(2,1)S(1)}, bf16[320,128]{1,0:T(8,128)(2,1)S(1)}, u32[]{:S(2)}, u32[]{:S(2)}) collective-permute-start(bf16[320,128]{1,0:T(8,128)(2,1)S(1)} %get-tuple-element.57), channel_id=1, source_target_pairs={{0,4},{1,65},{2,6},{3,67},{4,0},{5,69},{6,2},{7,71},{8,12},{9,73},... | collective-permute-start | bytes 245768 | tf_op jit(solution)/shard_map/ppermute | solution.py:692
  100.8 7.6 %collective-permute-start.19 = (bf16[1280,128]{1,0:T(8,128)(2,1)S(1)}, bf16[1280,128]{1,0:T(8,128)(2,1)S(1)}, u32[]{:S(2)}, u32[]{:S(2)}) collective-permute-start(bf16[1280,128]{1,0:T(8,128)(2,1)S(1)} %bitcast.97), channel_id=1, source_target_pairs={{0,32},{1,3},{2,34},{3,5},{4,36},{5,7},{6,38},{7,1},{8,40},{9,11},... | collective-permute-start | bytes 983048 | tf_op jit(solution)/shard_map/ppermute | solution.py:692
  101.8 10.8 %collective-permute-start.21 = (bf16[1280,128]{1,0:T(8,128)(2,1)S(1)}, bf16[1280,128]{1,0:T(8,128)(2,1)S(1)}, u32[]{:S(2)}, u32[]{:S(2)}) collective-permute-start(bf16[1280,128]{1,0:T(8,128)(2,1)S(1)} %bitcast.98), channel_id=1, source_target_pairs={{0,96},{1,7},{2,98},{3,1},{4,100},{5,3},{6,102},{7,5},{8,104},{9,1... | collective-permute-start | bytes 983048 | tf_op jit(solution)/shard_map/ppermute | solution.py:692
  103.5 9.0 %collective-permute-start.20 = (bf16[1280,128]{1,0:T(8,128)(2,1)S(1)}, bf16[1280,128]{1,0:T(8,128)(2,1)S(1)}, u32[]{:S(2)}, u32[]{:S(2)}) collective-permute-start(bf16[1280,128]{1,0:T(8,128)(2,1)S(1)} %bitcast.99), channel_id=1, source_target_pairs={{0,64},{1,5},{2,66},{3,7},{4,68},{5,1},{6,70},{7,3},{8,72},{9,13},... | collective-permute-start | bytes 983048 | tf_op jit(solution)/shard_map/ppermute | solution.py:692
  104.7 15.9 %copy-start = (f32[256,512]{1,0:T(8,128)S(1)}, f32[256,512]{1,0:T(8,128)}, u32[]{:S(2)}) copy-start(f32[256,512]{1,0:T(8,128)} %refs_1_.1) | copy-start | bytes 1572868
  104.8 15.9 %copy-start.1 = (f32[512,256]{1,0:T(8,128)S(1)}, f32[512,256]{1,0:T(8,128)}, u32[]{:S(2)}) copy-start(f32[512,256]{1,0:T(8,128)} %refs_4_.1) | copy-start | bytes 1572868
  104.8 15.9 %copy-start.2 = (f32[3,3,512]{2,1,0:T(4,128)S(1)}, f32[3,3,512]{2,1,0:T(4,128)}, u32[]{:S(2)}) copy-start(f32[3,3,512]{2,1,0:T(4,128)} %refs_3_.1) | copy-start | bytes 55300
  104.8 15.9 %copy-start.3 = (f32[3,3,256]{2,1,0:T(4,128)S(1)}, f32[3,3,256]{2,1,0:T(4,128)}, u32[]{:S(2)}) copy-start(f32[3,3,256]{2,1,0:T(4,128)} %refs_0_.1) | copy-start | bytes 27652
  104.8 15.9 %copy-start.4 = (f32[5]{0:T(128)S(1)}, f32[5]{0:T(128)}, u32[]{:S(2)}) copy-start(f32[5]{0:T(128)} %get-tuple-element.34.sums) | copy-start | bytes 64
  112.7 8.0 %collective-permute-start.22 = (bf16[5120,128]{1,0:T(8,128)(2,1)S(1)}, bf16[5120,128]{1,0:T(8,128)(2,1)S(1)}, u32[]{:S(2)}, u32[]{:S(2)}) collective-permute-start(bf16[5120,128]{1,0:T(8,128)(2,1)S(1)} %bitcast.81), channel_id=1, source_target_pairs={{0,1},{1,0},{2,3},{3,2},{4,5},{5,4},{6,7},{7,6},{8,9},{9,8},{10,11... | collective-permute-start | bytes 3932168 | tf_op jit(solution)/shard_map/ppermute | solution.py:741
  (1 other events, 0.6 us)
